TPU v7x, 32 devices: a whole 2x2x4 slice. The times are simulated.
32 devices in a mesh: section: 2 (over x), tensor: 4 (over y, core), dp: 4 (over z).
Axes of the slice: x: 2, y: 2, z: 4, core: 2. Of those that a mesh axis runs over, the one named last changes fastest.
Arguments:
- tokens: bfloat16 [8, 256, 1152], P('dp')
- cotangent: bfloat16 [8, 256, 1152], P('dp'), may hold values from -6 to 6
- kept_index: int32 [8, 256], P('dp'), may hold values from 0 to 255, as said below
- full_flag: int32 [8], P('dp'), may hold values 0 or 1
- labels: int32 [8], P('dp'), may hold values from 0 to 999
- timesteps: int32 [8], P('dp'), may hold values from 0 to 999
- class_table: bfloat16 [1000, 1152], replicated, may hold values from -6 to 6
- heads_weight: float32 [2, 3, 1152, 1152], P('section', None, 'dp', 'tensor')
- heads_first: float32 [2, 3, 1152, 1152], P('section', None, 'dp', 'tensor'), may hold values from -0.00024414062 to 0.00024414062
- heads_second: float32 [2, 3, 1152, 1152], P('section', None, 'dp', 'tensor'), may hold values from 2.1139925e-10 to 8.45597e-10
- output_weight: float32 [2, 1152, 1152], P('section', 'tensor', 'dp'), may hold values from -0.75 to 0.75
- output_first: float32 [2, 1152, 1152], P('section', 'tensor', 'dp'), may hold values from -0.00024414062 to 0.00024414062
- output_second: float32 [2, 1152, 1152], P('section', 'tensor', 'dp'), may hold values from 2.1139925e-10 to 8.45597e-10
- up_weight: float32 [2, 1152, 4608], P('section', 'dp', 'tensor')
- up_first: float32 [2, 1152, 4608], P('section', 'dp', 'tensor'), may hold values from -4.5776367e-05 to 4.5776367e-05
- up_second: float32 [2, 1152, 4608], P('section', 'dp', 'tensor'), may hold values from 8.45597e-12 to 3.382388e-11
- down_weight: float32 [2, 4608, 1152], P('section', 'tensor', 'dp'), may hold values from -0.09375 to 0.09375
- down_first: float32 [2, 4608, 1152], P('section', 'tensor', 'dp'), may hold values from -0.00024414062 to 0.00024414062
- down_second: float32 [2, 4608, 1152], P('section', 'tensor', 'dp'), may hold values from 2.1139925e-10 to 8.45597e-10
- adaln_weight: float32 [2, 1152, 6912], P('section', 'dp', 'tensor'), may hold values from -0.1875 to 0.1875
- adaln_first: float32 [2, 1152, 6912], P('section', 'dp', 'tensor'), may hold values from -0.00024414062 to 0.00024414062
- adaln_second: float32 [2, 1152, 6912], P('section', 'dp', 'tensor'), may hold values from 2.1139925e-10 to 8.45597e-10
- mask_token: float32 [1152], replicated, may hold values from -1.25 to 1.25
- mask_first: float32 [1152], replicated, may hold values from -0.0014648438 to 0.0014648438
- mask_second: float32 [1152], replicated, may hold values from 7.618746e-09 to 3.043312e-08
Outputs:
- block_outputs: bfloat16 [2, 8, 256, 1152], P('section', 'dp')
- input_grads: bfloat16 [2, 8, 256, 1152], P('section', 'dp')
- heads_weight_next: float32 [2, 3, 1152, 1152], P('section', None, 'dp', 'tensor')
- heads_first_next: float32 [2, 3, 1152, 1152], P('section', None, 'dp', 'tensor')
- heads_second_next: float32 [2, 3, 1152, 1152], P('section', None, 'dp', 'tensor')
- output_weight_next: float32 [2, 1152, 1152], P('section', 'tensor', 'dp')
- output_first_next: float32 [2, 1152, 1152], P('section', 'tensor', 'dp')
- output_second_next: float32 [2, 1152, 1152], P('section', 'tensor', 'dp')
- up_weight_next: float32 [2, 1152, 4608], P('section', 'dp', 'tensor')
- up_first_next: float32 [2, 1152, 4608], P('section', 'dp', 'tensor')
- up_second_next: float32 [2, 1152, 4608], P('section', 'dp', 'tensor')
- down_weight_next: float32 [2, 4608, 1152], P('section', 'tensor', 'dp')
- down_first_next: float32 [2, 4608, 1152], P('section', 'tensor', 'dp')
- down_second_next: float32 [2, 4608, 1152], P('section', 'tensor', 'dp')
- adaln_weight_next: float32 [2, 1152, 6912], P('section', 'dp', 'tensor')
- adaln_first_next: float32 [2, 1152, 6912], P('section', 'dp', 'tensor')
- adaln_second_next: float32 [2, 1152, 6912], P('section', 'dp', 'tensor')
- mask_token_next: float32 [1152], replicated
- mask_first_next: float32 [1152], replicated
- mask_second_next: float32 [1152], replicated
- grad_norm: float32 [], replicated
Inputs may be any that keep to these rules, and one draw needn't show every extreme that they name: `kept_index`: each row is a permutation of 0 to 255; an image keeps the tokens named by its first 128 entries, or all of them where its flag is 1.
All inputs are finite; a program needn't handle non-finite values. No bound on the sum of `full_flag` on one device may be relied on, other than what follows from the above.
Results may differ from a plain program's by a relative error of at most 0.025.
Values may be sent and summed in bfloat16 or wider, within the bound.
No kernel may reach another device: no remote copies, remote signals or barrier semaphores. Data moves between devices by JAX's collectives and lax.ppermute only.
A program may use at most 192 MiB of HBM per device.

v0:
```python
import math

import jax
import jax.numpy as jnp
from jax import lax
from jax.sharding import PartitionSpec as P

HEAD_DIM = 72
MICRO = 2
STEP = 10


PRECISE = lax.Precision.HIGHEST
NORM_EPS = 1e-06
BETA_ONE = 0.9
BETA_TWO = 0.99
LEARN_RATE = 0.05
WEIGHT_DECAY = 0.01
ADAM_EPS = 1e-08
CLIP_NORM = 1.0
MASK_SCORE = -1000000000.0


def passed_along(block, axis, distance):
    devices = range(lax.axis_size(axis))
    route = [(i - distance, i) for i in devices if i - distance in devices]
    return lax.ppermute(block, axis, route)


def layer_norm(values):
    center = values - jnp.mean(values, axis=-1, keepdims=True)
    spread = jnp.mean(center * center, axis=-1, keepdims=True)
    return center * lax.rsqrt(spread + NORM_EPS)


def modulate(values, shift_in, scale_in):
    return layer_norm(values) * (1.0 + scale_in) + shift_in


def gelu_tanh(values):
    return jax.nn.gelu(values, approximate=True)


def time_embed(steps_in, model_width):
    half_width = model_width // 2
    frequency = jnp.exp(-math.log(10000.0) * jnp.arange(half_width, dtype=jnp.float32) / half_width)
    angles = steps_in.astype(jnp.float32)[:, None] * frequency[None, :]
    return jnp.concatenate([jnp.cos(angles), jnp.sin(angles)], axis=-1)


def split_modulation(modulation):
    return [modulation[:, position][:, None, :] for position in range(6)]


def attention_scores(queries, keys_in, keys_live):
    scores = jnp.einsum(
        "bqhe,bkhe->bhqk", queries, keys_in, preferred_element_type=jnp.float32
    ) * HEAD_DIM ** (-0.5)
    return jnp.where(keys_live[:, None, None, :] > 0, scores, MASK_SCORE)


def block_forward(inputs, modulation, keys_live, w_heads, w_output, w_up, w_down):
    batch_size, seq_length, model_width = inputs.shape
    head_count = w_heads.shape[-1] // HEAD_DIM
    shift_a, scale_a, gate_a, shift_b, scale_b, gate_b = split_modulation(modulation)
    normed = modulate(inputs, shift_a, scale_a).astype(jnp.bfloat16)
    stacked = jnp.einsum(
        "bsd,nde->nbse", normed, w_heads, preferred_element_type=jnp.float32
    ).astype(jnp.bfloat16)
    by_head = stacked.reshape(3, batch_size, seq_length, head_count, HEAD_DIM)
    scores = attention_scores(by_head[0], by_head[1], keys_live)
    row_peak = jnp.max(scores, axis=-1, keepdims=True)
    exponent = jnp.exp(scores - row_peak)
    row_total = jnp.sum(exponent, axis=-1, keepdims=True)
    log_total = row_peak + jnp.log(row_total)
    probability = (exponent / row_total).astype(jnp.bfloat16)
    attended = jnp.einsum(
        "bhqk,bkhe->bqhe", probability, by_head[2], preferred_element_type=jnp.float32
    )
    attended = attended.astype(jnp.bfloat16).reshape(batch_size, seq_length, head_count * HEAD_DIM)
    attn_share = lax.psum_scatter(
        jnp.einsum("bse,ed->bsd", attended, w_output, preferred_element_type=jnp.float32),
        "tensor",
        scatter_dimension=1,
        tiled=True,
    )
    branch_a = lax.all_gather(attn_share, "tensor", axis=1, tiled=True)
    hidden = inputs + gate_a * branch_a
    normed_b = modulate(hidden, shift_b, scale_b).astype(jnp.bfloat16)
    up_value = jnp.einsum("bsd,df->bsf", normed_b, w_up, preferred_element_type=jnp.float32)
    activated = gelu_tanh(up_value).astype(jnp.bfloat16)
    feed_share = lax.psum_scatter(
        jnp.einsum("bsf,fd->bsd", activated, w_down, preferred_element_type=jnp.float32),
        "tensor",
        scatter_dimension=1,
        tiled=True,
    )
    branch_b = lax.all_gather(feed_share, "tensor", axis=1, tiled=True)
    outputs = hidden + gate_b * branch_b
    saved_state = (
        inputs,
        normed,
        stacked,
        log_total,
        attended,
        branch_a,
        hidden,
        normed_b,
        up_value,
        activated,
        branch_b,
    )
    return (outputs, saved_state)


def block_backward(grad_out, saved_state, modulation, keys_live, w_heads, w_output, w_up, w_down):
    (
        inputs,
        normed,
        stacked,
        log_total,
        attended,
        branch_a,
        hidden,
        normed_b,
        up_value,
        activated,
        branch_b,
    ) = saved_state
    batch_size, seq_length, model_width = inputs.shape
    head_count = w_heads.shape[-1] // HEAD_DIM
    shift_a, scale_a, gate_a, shift_b, scale_b, gate_b = split_modulation(modulation)
    gate_b_grad = jnp.sum(grad_out * branch_b, axis=1)
    down_in = (gate_b * grad_out).astype(jnp.bfloat16)
    grad_down = jnp.einsum("bsf,bsd->fd", activated, down_in, preferred_element_type=jnp.float32)
    act_grad = jnp.einsum("bsd,fd->bsf", down_in, w_down, preferred_element_type=jnp.float32)
    gelu_pull = jax.vjp(gelu_tanh, up_value)[1]
    up_grad = gelu_pull(act_grad)[0].astype(jnp.bfloat16)
    grad_up = jnp.einsum("bsd,bsf->df", normed_b, up_grad, preferred_element_type=jnp.float32)
    normed_b_grad = lax.psum(
        jnp.einsum("bsf,df->bsd", up_grad, w_up, preferred_element_type=jnp.float32).astype(
            jnp.bfloat16
        ),
        "tensor",
    ).astype(jnp.float32)
    pull_b = jax.vjp(modulate, hidden, shift_b, scale_b)[1]
    hidden_grad, shift_b_grad, scale_b_grad = pull_b(normed_b_grad)
    hidden_grad = hidden_grad + grad_out
    gate_a_grad = jnp.sum(hidden_grad * branch_a, axis=1)
    output_in = (gate_a * hidden_grad).astype(jnp.bfloat16)
    grad_output = jnp.einsum("bse,bsd->ed", attended, output_in, preferred_element_type=jnp.float32)
    attended_grad = jnp.einsum(
        "bsd,ed->bse", output_in, w_output, preferred_element_type=jnp.float32
    )
    attended_grad = attended_grad.astype(jnp.bfloat16).reshape(
        batch_size, seq_length, head_count, HEAD_DIM
    )
    by_head = stacked.reshape(3, batch_size, seq_length, head_count, HEAD_DIM)
    scores = attention_scores(by_head[0], by_head[1], keys_live)
    soft_weights = jnp.exp(scores - log_total)
    value_grad = jnp.einsum(
        "bhqk,bqhe->bkhe",
        soft_weights.astype(jnp.bfloat16),
        attended_grad,
        preferred_element_type=jnp.float32,
    )
    prob_grad = jnp.einsum(
        "bqhe,bkhe->bhqk", attended_grad, by_head[2], preferred_element_type=jnp.float32
    )
    score_grad = soft_weights * (
        prob_grad - jnp.sum(soft_weights * prob_grad, axis=-1, keepdims=True)
    )
    score_grad = score_grad.astype(jnp.bfloat16)
    query_grad = jnp.einsum(
        "bhqk,bkhe->bqhe", score_grad, by_head[1], preferred_element_type=jnp.float32
    ) * HEAD_DIM ** (-0.5)
    key_grad = jnp.einsum(
        "bhqk,bqhe->bkhe", score_grad, by_head[0], preferred_element_type=jnp.float32
    ) * HEAD_DIM ** (-0.5)
    stacked_grad = jnp.stack([query_grad, key_grad, value_grad]).astype(jnp.bfloat16)
    stacked_grad = stacked_grad.reshape(3, batch_size, seq_length, head_count * HEAD_DIM)
    grad_heads = jnp.einsum(
        "bsd,nbse->nde", normed, stacked_grad, preferred_element_type=jnp.float32
    )
    normed_grad = lax.psum(
        jnp.einsum("nbse,nde->bsd", stacked_grad, w_heads, preferred_element_type=jnp.float32),
        "tensor",
    )
    pull_a = jax.vjp(modulate, inputs, shift_a, scale_a)[1]
    input_grad, shift_a_grad, scale_a_grad = pull_a(normed_grad)
    input_grad = input_grad + hidden_grad
    modulation_grad = jnp.stack(
        [
            shift_a_grad[:, 0],
            scale_a_grad[:, 0],
            gate_a_grad,
            shift_b_grad[:, 0],
            scale_b_grad[:, 0],
            gate_b_grad,
        ],
        axis=1,
    )
    return (input_grad, (grad_heads, grad_output, grad_up, grad_down), modulation_grad)


def adam_update(weight_in, first_in, second_in, gradient, factor):
    clipped = gradient * factor
    first_out = BETA_ONE * first_in + (1.0 - BETA_ONE) * clipped
    second_out = BETA_TWO * second_in + (1.0 - BETA_TWO) * clipped * clipped
    ratio = (
        first_out
        / (1.0 - BETA_ONE**STEP)
        / (jnp.sqrt(second_out / (1.0 - BETA_TWO**STEP)) + ADAM_EPS)
    )
    weight_out = weight_in - LEARN_RATE * (ratio + WEIGHT_DECAY * weight_in)
    return (weight_out, first_out, second_out)


def per_device(
    tokens,
    cotangent,
    kept_index,
    full_flag,
    labels,
    timesteps,
    class_table,
    heads_weight,
    heads_first,
    heads_second,
    output_weight,
    output_first,
    output_second,
    up_weight,
    up_first,
    up_second,
    down_weight,
    down_first,
    down_second,
    adaln_weight,
    adaln_first,
    adaln_second,
    mask_token,
    mask_first,
    mask_second,
):
    image_count, seq_length, model_width = tokens.shape
    batch_size = image_count // MICRO
    tensor_count = lax.axis_size("tensor")
    section_index = lax.axis_index("section")
    tensor_index = lax.axis_index("tensor")
    is_first = section_index == 0
    gathered = (
        lax.all_gather(heads_weight.astype(jnp.bfloat16), "dp", axis=2, tiled=True),
        lax.all_gather(output_weight.astype(jnp.bfloat16), "dp", axis=2, tiled=True),
        lax.all_gather(up_weight.astype(jnp.bfloat16), "dp", axis=1, tiled=True),
        lax.all_gather(down_weight.astype(jnp.bfloat16), "dp", axis=2, tiled=True),
        lax.all_gather(adaln_weight.astype(jnp.bfloat16), "dp", axis=1, tiled=True),
    )
    w_heads = gathered[0][0]
    w_output = gathered[1][0]
    w_up = gathered[2][0]
    w_down = gathered[3][0]
    w_adaln = gathered[4][0]
    class_count = class_table.shape[0]
    label_hot = (labels[:, None] == jnp.arange(class_count, dtype=jnp.int32)[None, :]).astype(
        jnp.bfloat16
    )
    condition = jnp.dot(label_hot, class_table, preferred_element_type=jnp.float32) + time_embed(
        timesteps, model_width
    )
    cond_act = jax.nn.silu(condition).astype(jnp.bfloat16)
    adaln_part = jnp.dot(cond_act, w_adaln, preferred_element_type=jnp.float32)
    column_count = adaln_part.shape[1]
    modulation_all = lax.all_gather(adaln_part, "tensor", axis=1, tiled=True).reshape(
        image_count, 6, model_width
    )
    slot_ids = jnp.arange(seq_length, dtype=jnp.int32)
    counts = jnp.where(full_flag > 0, seq_length, seq_length // 2)
    slot_live = (slot_ids[None, :] < counts[:, None]).astype(jnp.float32)
    placement = (
        (kept_index[:, :, None] == slot_ids[None, None, :]).astype(jnp.float32)
        * slot_live[:, :, None]
    ).astype(jnp.bfloat16)
    covered = jnp.sum(placement.astype(jnp.float32), axis=1)

    def take_batch(values, row_start):
        return lax.dynamic_slice_in_dim(values, row_start, batch_size, 0)

    def arrangement(row_start):
        place_batch = take_batch(placement, row_start)
        live_batch = take_batch(slot_live, row_start)
        cover_batch = take_batch(covered, row_start)
        arrange = jnp.where(is_first, place_batch, jnp.swapaxes(place_batch, 1, 2))
        keys_live = jnp.where(is_first, live_batch, jnp.ones_like(live_batch))
        fill_rows = jnp.where(is_first, jnp.zeros_like(cover_batch), 1.0 - cover_batch)
        return (arrange, keys_live, fill_rows)

    batch_shape = (batch_size, seq_length, model_width)
    received = jnp.zeros(batch_shape, jnp.bfloat16)
    layer_out = jnp.zeros((image_count, seq_length, model_width), jnp.bfloat16)
    states = []
    for tick_index in range(MICRO + 1):
        batch_index = tick_index - section_index
        active = (batch_index >= 0) & (batch_index < MICRO)
        row_start = jnp.clip(batch_index, 0, MICRO - 1) * batch_size
        arrange, keys_live, fill_rows = arrangement(row_start)
        source = jnp.where(is_first, take_batch(tokens, row_start), received)
        inputs = jnp.einsum("bij,bjd->bid", arrange, source, preferred_element_type=jnp.float32)
        inputs = inputs + fill_rows[:, :, None] * mask_token[None, None, :]
        outputs, saved_state = block_forward(
            inputs,
            take_batch(modulation_all, row_start),
            keys_live,
            w_heads,
            w_output,
            w_up,
            w_down,
        )
        sent_rows = (outputs * keys_live[:, :, None]).astype(jnp.bfloat16)
        old_rows = take_batch(layer_out, row_start)
        layer_out = lax.dynamic_update_slice_in_dim(
            layer_out, jnp.where(active, sent_rows, old_rows), row_start, 0
        )
        received = passed_along(sent_rows, "section", 1)
        states.append(saved_state)
    grad_total = None
    returned = jnp.zeros(batch_shape, jnp.bfloat16)
    in_grads = jnp.zeros((image_count, seq_length, model_width), jnp.bfloat16)
    mask_grad = jnp.zeros((model_width,), jnp.float32)
    for tick_index in range(MICRO + 1):
        batch_index = MICRO - tick_index - section_index
        active = (batch_index >= 0) & (batch_index < MICRO)
        row_start = jnp.clip(batch_index, 0, MICRO - 1) * batch_size
        arrange, keys_live, fill_rows = arrangement(row_start)
        grad_out = jnp.where(
            is_first,
            returned.astype(jnp.float32),
            take_batch(cotangent, row_start).astype(jnp.float32),
        )
        grad_out = jnp.where(active, grad_out, jnp.zeros_like(grad_out))
        input_grad, weight_grads, modulation_grad = block_backward(
            grad_out,
            states[MICRO - tick_index],
            take_batch(modulation_all, row_start),
            keys_live,
            w_heads,
            w_output,
            w_up,
            w_down,
        )
        adaln_cols = lax.dynamic_slice_in_dim(
            modulation_grad.reshape(batch_size, 6 * model_width),
            tensor_index * column_count,
            column_count,
            1,
        )
        grad_adaln = jnp.dot(
            take_batch(cond_act, row_start).astype(jnp.float32).T, adaln_cols, precision=PRECISE
        )
        tick_grads = weight_grads + (grad_adaln,)
        if grad_total is None:
            grad_total = tick_grads
        else:
            grad_total = tuple(
                (old_part + new_part for old_part, new_part in zip(grad_total, tick_grads))
            )
        grad_low = input_grad.astype(jnp.bfloat16)
        back_rows = jnp.einsum(
            "bij,bid->bjd", arrange, grad_low, preferred_element_type=jnp.float32
        )
        back_rows = back_rows.astype(jnp.bfloat16)
        written = jnp.where(is_first, back_rows, grad_low)
        old_rows = take_batch(in_grads, row_start)
        in_grads = lax.dynamic_update_slice_in_dim(
            in_grads, jnp.where(active, written, old_rows), row_start, 0
        )
        mask_grad = mask_grad + jnp.sum(fill_rows[:, :, None] * input_grad, axis=(0, 1))
        returned = passed_along(back_rows, "section", -1)
    reduced = (
        lax.psum_scatter(
            grad_total[0][None].astype(jnp.bfloat16), "dp", scatter_dimension=2, tiled=True
        ).astype(jnp.float32),
        lax.psum_scatter(
            grad_total[1][None].astype(jnp.bfloat16), "dp", scatter_dimension=2, tiled=True
        ).astype(jnp.float32),
        lax.psum_scatter(
            grad_total[2][None].astype(jnp.bfloat16), "dp", scatter_dimension=1, tiled=True
        ).astype(jnp.float32),
        lax.psum_scatter(
            grad_total[3][None].astype(jnp.bfloat16), "dp", scatter_dimension=2, tiled=True
        ).astype(jnp.float32),
        lax.psum_scatter(
            grad_total[4][None].astype(jnp.bfloat16), "dp", scatter_dimension=1, tiled=True
        ).astype(jnp.float32),
    )
    local_square = sum((jnp.sum(member * member) for member in reduced))
    own_cols = (
        jnp.arange(model_width, dtype=jnp.int32) // (model_width // tensor_count) == tensor_index
    )
    square_total, mask_total = lax.psum(
        (local_square, mask_grad * own_cols.astype(jnp.float32)), ("section", "tensor", "dp")
    )
    grad_norm = jnp.sqrt(square_total + jnp.sum(mask_total * mask_total))
    factor = jnp.minimum(1.0, CLIP_NORM / (grad_norm + NORM_EPS))
    masters = (heads_weight, output_weight, up_weight, down_weight, adaln_weight)
    firsts = (heads_first, output_first, up_first, down_first, adaln_first)
    seconds = (heads_second, output_second, up_second, down_second, adaln_second)
    updated = [
        adam_update(
            masters[position], firsts[position], seconds[position], reduced[position], factor
        )
        for position in range(5)
    ]
    mask_next = adam_update(mask_token, mask_first, mask_second, mask_total, factor)
    return (
        layer_out[None],
        in_grads[None],
        updated[0][0],
        updated[0][1],
        updated[0][2],
        updated[1][0],
        updated[1][1],
        updated[1][2],
        updated[2][0],
        updated[2][1],
        updated[2][2],
        updated[3][0],
        updated[3][1],
        updated[3][2],
        updated[4][0],
        updated[4][1],
        updated[4][2],
        mask_next[0],
        mask_next[1],
        mask_next[2],
        grad_norm,
    )


def solution(mesh):
    return jax.shard_map(
        per_device,
        mesh=mesh,
        in_specs=(
            P("dp", None, None),
            P("dp", None, None),
            P("dp", None),
            P("dp"),
            P("dp"),
            P("dp"),
            P(),
            P("section", None, "dp", "tensor"),
            P("section", None, "dp", "tensor"),
            P("section", None, "dp", "tensor"),
            P("section", "tensor", "dp"),
            P("section", "tensor", "dp"),
            P("section", "tensor", "dp"),
            P("section", "dp", "tensor"),
            P("section", "dp", "tensor"),
            P("section", "dp", "tensor"),
            P("section", "tensor", "dp"),
            P("section", "tensor", "dp"),
            P("section", "tensor", "dp"),
            P("section", "dp", "tensor"),
            P("section", "dp", "tensor"),
            P("section", "dp", "tensor"),
            P(),
            P(),
            P(),
        ),
        out_specs=(
            P("section", "dp", None, None),
            P("section", "dp", None, None),
            P("section", None, "dp", "tensor"),
            P("section", None, "dp", "tensor"),
            P("section", None, "dp", "tensor"),
            P("section", "tensor", "dp"),
            P("section", "tensor", "dp"),
            P("section", "tensor", "dp"),
            P("section", "dp", "tensor"),
            P("section", "dp", "tensor"),
            P("section", "dp", "tensor"),
            P("section", "tensor", "dp"),
            P("section", "tensor", "dp"),
            P("section", "tensor", "dp"),
            P("section", "dp", "tensor"),
            P("section", "dp", "tensor"),
            P("section", "dp", "tensor"),
            P(),
            P(),
            P(),
            P(),
        ),
        check_vma=False,
    )
```

profile of v0, /device:TPU:0, one launch (start us, length us, event | category | flops | bytes accessed | tf_op | source)
XLA Modules:
  0.0 1313.1 jit_solution(1205950206725213273)
XLA Ops:
  15.5 66.2 %all_gather.39 = bf16[1,288,1152]{1,0,2:T(2,128)(2,1)} all-gather(bf16[1,288,288]{1,0,2:T(2,128)(2,1)} %copy.257), channel_id=1, replica_groups=mesh['section'=2,'tensor'=4,'dp'=4] {'dp'}, dimensions={2}, use_global_device_ids=true | all-gather | bytes 829440 | tf_op jit(solution)/shard_map/all_gather | solution.py:254
  92.1 19.1 %all-gather.14.cloned.1.call-done = bf16[1,3,1152,288]{3,1,0,2:T(4,128)(2,1)} async-done(((bf16[1,3,288,288]{3,1,0,2:T(4,128)(2,1)}), bf16[1,3,1152,288]{3,1,0,2:T(4,128)(2,1)}) %all-gather.14.cloned.1.call-update) | async-done | bytes 1990672 | tf_op jit(solution)/shard_map/all_gather | solution.py:253
  117.3 74.4 %all-gather.12.cloned.1.call-done = bf16[1,1152,1728]{2,1,0:T(8,128)(2,1)} async-done(((bf16[1,288,1728]{2,1,0:T(8,128)(2,1)}), bf16[1,1152,1728]{2,1,0:T(8,128)(2,1)}) %all-gather.12.cloned.1.call-update) | async-done | bytes 3981328 | tf_op jit(solution)/shard_map/all_gather | solution.py:257
  207.2 24.4 %reduce-scatter.18.cloned.1.call-done = f32[1,64,1152]{2,1,0:T(8,128)} async-done(((f32[1,256,1152]{2,1,0:T(8,128)}), f32[1,64,1152]{2,1,0:T(8,128)}) %reduce-scatter.18.cloned.1.call-update) | async-done | bytes 294928 | tf_op jit(solution)/shard_map/reduce_scatter | solution.py:81
  235.0 15.6 %all-gather.16.cloned.1.call-done = f32[1,256,1152]{2,1,0:T(8,128)} async-done(((f32[1,64,1152]{2,1,0:T(8,128)}), f32[1,256,1152]{2,1,0:T(8,128)}) %all-gather.16.cloned.1.call-update) | async-done | bytes 1179664 | tf_op jit(solution)/shard_map/all_gather | solution.py:87
  252.7 55.3 %all-gather.18.cloned.1.call-done = bf16[1,1152,1152]{2,1,0:T(8,128)(2,1)} async-done(((bf16[1,288,1152]{2,1,0:T(8,128)(2,1)}), bf16[1,1152,1152]{2,1,0:T(8,128)(2,1)}) %all-gather.18.cloned.1.call-update) | async-done | bytes 2654224 | tf_op jit(solution)/shard_map/all_gather | solution.py:255
  311.9 52.4 %all-gather.20.cloned.1.call-done = bf16[1,1152,1152]{1,2,0:T(8,128)(2,1)} async-done(((bf16[1,1152,288]{1,2,0:T(8,128)(2,1)}), bf16[1,1152,1152]{1,2,0:T(8,128)(2,1)}) %all-gather.20.cloned.1.call-update) | async-done | bytes 2654224 | tf_op jit(solution)/shard_map/all_gather | solution.py:256
  368.6 24.6 %reduce-scatter.20.cloned.1.call-done = f32[1,64,1152]{2,1,0:T(8,128)} async-done(((f32[1,256,1152]{2,1,0:T(8,128)}), f32[1,64,1152]{2,1,0:T(8,128)}) %reduce-scatter.20.cloned.1.call-update) | async-done | bytes 294928 | tf_op jit(solution)/shard_map/reduce_scatter | solution.py:92
  393.2 19.0 %all-gather.22.cloned.1.call-done = f32[1,256,1152]{2,1,0:T(8,128)} async-done(((f32[1,64,1152]{2,1,0:T(8,128)}), f32[1,256,1152]{2,1,0:T(8,128)}) %all-gather.22.cloned.1.call-update) | async-done | bytes 1179664 | tf_op jit(solution)/shard_map/all_gather | solution.py:98
  419.7 12.2 collective-permute-done
  438.9 27.0 %reduce-scatter.22.cloned.1.call-done = f32[1,64,1152]{2,1,0:T(8,128)} async-done(((f32[1,256,1152]{2,1,0:T(8,128)}), f32[1,64,1152]{2,1,0:T(8,128)}) %reduce-scatter.22.cloned.1.call-update) | async-done | bytes 294928 | tf_op jit(solution)/shard_map/reduce_scatter | solution.py:81
  466.0 18.9 %all-gather.24.cloned.1.call-done = f32[1,256,1152]{2,1,0:T(8,128)} async-done(((f32[1,64,1152]{2,1,0:T(8,128)}), f32[1,256,1152]{2,1,0:T(8,128)}) %all-gather.24.cloned.1.call-update) | async-done | bytes 1179664 | tf_op jit(solution)/shard_map/all_gather | solution.py:87
  491.8 25.8 %reduce-scatter.24.cloned.1.call-done = f32[1,64,1152]{2,1,0:T(8,128)} async-done(((f32[1,256,1152]{2,1,0:T(8,128)}), f32[1,64,1152]{2,1,0:T(8,128)}) %reduce-scatter.24.cloned.1.call-update) | async-done | bytes 294928 | tf_op jit(solution)/shard_map/reduce_scatter | solution.py:92
  517.7 18.8 %all-gather.26.cloned.1.call-done = f32[1,256,1152]{2,1,0:T(8,128)} async-done(((f32[1,64,1152]{2,1,0:T(8,128)}), f32[1,256,1152]{2,1,0:T(8,128)}) %all-gather.26.cloned.1.call-update) | async-done | bytes 1179664 | tf_op jit(solution)/shard_map/all_gather | solution.py:98
  543.6 12.0 collective-permute-done.1
  562.7 27.1 %reduce-scatter.26.cloned.1.call-done = f32[1,64,1152]{2,1,0:T(8,128)} async-done(((f32[1,256,1152]{2,1,0:T(8,128)}), f32[1,64,1152]{2,1,0:T(8,128)}) %reduce-scatter.26.cloned.1.call-update) | async-done | bytes 294928 | tf_op jit(solution)/shard_map/reduce_scatter | solution.py:81
  589.9 18.9 %all-gather.28.cloned.1.call-done = f32[1,256,1152]{2,1,0:T(8,128)} async-done(((f32[1,64,1152]{2,1,0:T(8,128)}), f32[1,256,1152]{2,1,0:T(8,128)}) %all-gather.28.cloned.1.call-update) | async-done | bytes 1179664 | tf_op jit(solution)/shard_map/all_gather | solution.py:87
  619.5 32.1 %all-reduce.8.cloned.1.call-done = bf16[1,256,1152]{2,1,0:T(8,128)(2,1)} async-done(((bf16[1,256,1152]{2,1,0:T(8,128)(2,1)}), bf16[1,256,1152]{2,1,0:T(8,128)(2,1)}) %all-reduce.8.cloned.1.call-update) | async-done | bytes 589840 | tf_op jit(solution)/shard_map/psum | solution.py:140
  663.1 37.4 %all-reduce.10.cloned.1.call-done = f32[1,256,1152]{2,1,0:T(8,128)} async-done(((f32[1,256,1152]{2,1,0:T(8,128)}), f32[1,256,1152]{2,1,0:T(8,128)}) %all-reduce.10.cloned.1.call-update) | async-done | bytes 1179664 | tf_op jit(solution)/shard_map/psum | solution.py:185
  709.3 15.6 %collective-permute-done.2 = bf16[1,256,1152]{2,1,0:T(8,128)(2,1)S(1)} collective-permute-done((bf16[1,256,1152]{2,1,0:T(8,128)(2,1)S(1)}, bf16[1,256,1152]{2,1,0:T(8,128)(2,1)S(1)}, u32[]{:S(2)}, u32[]{:S(2)}) %collective-permute-start.2) | collective-permute-done | bytes 589856 | tf_op jit(solution)/shard_map/ppermute | solution.py:27
  731.2 31.7 %all-reduce.12.cloned.1.call-done = bf16[1,256,1152]{2,1,0:T(8,128)(2,1)} async-done(((bf16[1,256,1152]{2,1,0:T(8,128)(2,1)}), bf16[1,256,1152]{2,1,0:T(8,128)(2,1)}) %all-reduce.12.cloned.1.call-update) | async-done | bytes 589840 | tf_op jit(solution)/shard_map/psum | solution.py:140
  774.3 37.0 %all-reduce.14.cloned.1.call-done = f32[1,256,1152]{2,1,0:T(8,128)} async-done(((f32[1,256,1152]{2,1,0:T(8,128)}), f32[1,256,1152]{2,1,0:T(8,128)}) %all-reduce.14.cloned.1.call-update) | async-done | bytes 1179664 | tf_op jit(solution)/shard_map/psum | solution.py:185
  820.8 15.0 %collective-permute-done.3 = bf16[1,256,1152]{2,1,0:T(8,128)(2,1)S(1)} collective-permute-done((bf16[1,256,1152]{2,1,0:T(8,128)(2,1)S(1)}, bf16[1,256,1152]{2,1,0:T(8,128)(2,1)S(1)}, u32[]{:S(2)}, u32[]{:S(2)}) %collective-permute-start.3) | collective-permute-done | bytes 589856 | tf_op jit(solution)/shard_map/ppermute | solution.py:27
  845.1 28.6 %all-reduce.16.cloned.1.call-done = bf16[1,256,1152]{2,1,0:T(8,128)(2,1)} async-done(((bf16[1,256,1152]{2,1,0:T(8,128)(2,1)}), bf16[1,256,1152]{2,1,0:T(8,128)(2,1)}) %all-reduce.16.cloned.1.call-update) | async-done | bytes 589840 | tf_op jit(solution)/shard_map/psum | solution.py:140
  884.7 18.0 %reduce-scatter.28.cloned.1.call-done = f32[1,64,1152]{2,1,0:T(8,128)} async-done(((f32[1,256,1152]{2,1,0:T(8,128)}), f32[1,64,1152]{2,1,0:T(8,128)}) %reduce-scatter.28.cloned.1.call-update) | async-done | bytes 294928 | tf_op jit(solution)/shard_map/reduce_scatter | solution.py:92
  928.9 7.5 reshape.1317
  943.7 12.6 copy.303
  1022.6 12.1 reduce-scatter.34.cloned.1.call-done
  1040.4 48.7 %reduce-scatter.38.cloned.1.call-done = bf16[288,1152]{1,0:T(8,128)(2,1)} async-done(((bf16[1152,1152]{1,0:T(8,128)(2,1)}), bf16[288,1152]{1,0:T(8,128)(2,1)}) %reduce-scatter.38.cloned.1.call-update) | async-done | bytes 663568
  1093.0 50.7 %reduce-scatter.30.cloned.1.call-done = bf16[1,288,1152]{2,1,0:T(8,128)(2,1)} async-done(((bf16[1,1152,1152]{2,1,0:T(8,128)(2,1)}), bf16[1,288,1152]{2,1,0:T(8,128)(2,1)}) %reduce-scatter.30.cloned.1.call-update) | async-done | bytes 663568 | tf_op jit(solution)/shard_map/reduce_scatter | solution.py:386
  1148.1 73.3 %reduce-scatter.32.cloned.1.call-done = bf16[1,288,1728]{2,1,0:T(8,128)(2,1)} async-done(((bf16[1,1152,1728]{2,1,0:T(8,128)(2,1)}), bf16[1,288,1728]{2,1,0:T(8,128)(2,1)}) %reduce-scatter.32.cloned.1.call-update) | async-done | bytes 995344 | tf_op jit(solution)/shard_map/reduce_scatter | solution.py:392
  1226.6 41.1 %all-reduce = (f32[]{:T(128)}, f32[1152]{0:T(1024)S(1)}) all-reduce(f32[]{:T(128)S(6)} %add.583, f32[1152]{0:T(1024)S(1)} %add_select_fusion.1), channel_id=1, replica_groups=mesh['section'=2,'tensor'=4,'dp'=4] {'section','tensor','dp'}, use_global_device_ids=true, to_apply=%region_74.75 | all-reduce | flops 1153 | bytes 9224 | tf_op jit(solution)/shard_map/psum | solution.py:400
  (836 shorter events, 316.5 us)
Async XLA Ops:
  7.2 104.0 %all-gather.14.cloned.1.call-start = ((), (), s32[]{:S(2)}) async-start(), calls=%async_computation.12 | async-start | bytes 4423680 | tf_op jit(solution)/shard_map/all_gather | solution.py:253
  10.2 181.4 %all-gather.12.cloned.1.call-start = ((), (), s32[]{:S(2)}) async-start(), calls=%async_computation.11 | async-start | bytes 5160960 | tf_op jit(solution)/shard_map/all_gather | solution.py:257
  12.9 218.6 %reduce-scatter.18.cloned.1.call-start = ((), (), s32[]{:S(2)}) async-start(), calls=%async_computation.13 | async-start | bytes 1474560 | tf_op jit(solution)/shard_map/reduce_scatter | solution.py:81
  117.3 316.5 %copy-start.2 = (bf16[1,3,1152,288]{2,3,1,0:T(8,128)(2,1)}, bf16[1,3,1152,288]{2,3,1,0:T(8,128)(2,1)S(1)}, u32[]{:S(2)}) copy-start(bf16[1,3,1152,288]{2,3,1,0:T(8,128)(2,1)S(1)} %copy.255) | copy-start | bytes 5971972
  207.2 43.4 %all-gather.16.cloned.1.call-start = ((), (), s32[]{:S(2)}) async-start(), calls=%async_computation.14 | async-start | bytes 1474560 | tf_op jit(solution)/shard_map/all_gather | solution.py:87
  231.6 76.4 %all-gather.18.cloned.1.call-start = ((), (), s32[]{:S(2)}) async-start(), calls=%async_computation.15 | async-start | bytes 3317760 | tf_op jit(solution)/shard_map/all_gather | solution.py:255
  232.6 131.6 %all-gather.20.cloned.1.call-start = ((), (), s32[]{:S(2)}) async-start(), calls=%async_computation.16 | async-start | bytes 3317760 | tf_op jit(solution)/shard_map/all_gather | solution.py:256
  234.9 158.3 %reduce-scatter.20.cloned.1.call-start = ((), (), s32[]{:S(2)}) async-start(), calls=%async_computation.17 | async-start | bytes 1474560 | tf_op jit(solution)/shard_map/reduce_scatter | solution.py:92
  368.5 43.7 %all-gather.22.cloned.1.call-start = ((), (), s32[]{:S(2)}) async-start(), calls=%async_computation.18 | async-start | bytes 1474560 | tf_op jit(solution)/shard_map/all_gather | solution.py:98
  393.2 72.8 %reduce-scatter.22.cloned.1.call-start = ((), (), s32[]{:S(2)}) async-start(), calls=%async_computation.19 | async-start | bytes 1474560 | tf_op jit(solution)/shard_map/reduce_scatter | solution.py:81
  415.2 16.7 %collective-permute-start = (bf16[1,256,1152]{2,1,0:T(8,128)(2,1)}, bf16[1,256,1152]{2,1,0:T(8,128)(2,1)}, u32[]{:S(2)}, u32[]{:S(2)}) collective-permute-start(bf16[1,256,1152]{2,1,0:T(8,128)(2,1)} %get-tuple-element.253), channel_id=1, source_target_pairs={{0,16},{1,17},{2,18},{3,19},{4,20},{5,21},{6,22},{7,23},{8,24},{9,... | collective-permute-start | bytes 1769480 | tf_op jit(solution)/shard_map/ppermute | solution.py:27
  438.9 46.0 %all-gather.24.cloned.1.call-start = ((), (), s32[]{:S(2)}) async-start(), calls=%async_computation.20 | async-start | bytes 1474560 | tf_op jit(solution)/shard_map/all_gather | solution.py:87
  466.0 51.7 %reduce-scatter.24.cloned.1.call-start = ((), (), s32[]{:S(2)}) async-start(), calls=%async_computation.21 | async-start | bytes 1474560 | tf_op jit(solution)/shard_map/reduce_scatter | solution.py:92
  491.8 44.8 %all-gather.26.cloned.1.call-start = ((), (), s32[]{:S(2)}) async-start(), calls=%async_computation.22 | async-start | bytes 1474560 | tf_op jit(solution)/shard_map/all_gather | solution.py:98
  517.7 72.1 %reduce-scatter.26.cloned.1.call-start = ((), (), s32[]{:S(2)}) async-start(), calls=%async_computation.23 | async-start | bytes 1474560 | tf_op jit(solution)/shard_map/reduce_scatter | solution.py:81
  539.2 16.3 %collective-permute-start.1 = (bf16[1,256,1152]{2,1,0:T(8,128)(2,1)S(1)}, bf16[1,256,1152]{2,1,0:T(8,128)(2,1)}, u32[]{:S(2)}, u32[]{:S(2)}) collective-permute-start(bf16[1,256,1152]{2,1,0:T(8,128)(2,1)S(1)} %get-tuple-element.249), channel_id=1, source_target_pairs={{0,16},{1,17},{2,18},{3,19},{4,20},{5,21},{6,22},{7,23},{8,24},{9,... | collective-permute-start | bytes 1769480 | tf_op jit(solution)/shard_map/ppermute | solution.py:27
  562.6 46.2 %all-gather.28.cloned.1.call-start = ((), (), s32[]{:S(2)}) async-start(), calls=%async_computation.24 | async-start | bytes 1474560 | tf_op jit(solution)/shard_map/all_gather | solution.py:87
  589.8 61.7 %all-reduce.8.cloned.1.call-start = ((), (), s32[]{:S(2)}) async-start(), calls=%async_computation.27 | async-start | bytes 1179648 | tf_op jit(solution)/shard_map/psum | solution.py:140
  617.9 82.5 %all-reduce.10.cloned.1.call-start = ((), (), s32[]{:S(2)}) async-start(), calls=%async_computation.28 | async-start | bytes 2359296 | tf_op jit(solution)/shard_map/psum | solution.py:185
  663.0 99.8 %all-reduce.12.cloned.1.call-start = ((), (), s32[]{:S(2)}) async-start(), calls=%async_computation.29 | async-start | bytes 1179648 | tf_op jit(solution)/shard_map/psum | solution.py:140
  707.7 17.2 %collective-permute-start.2 = (bf16[1,256,1152]{2,1,0:T(8,128)(2,1)S(1)}, bf16[1,256,1152]{2,1,0:T(8,128)(2,1)S(1)}, u32[]{:S(2)}, u32[]{:S(2)}) collective-permute-start(bf16[1,256,1152]{2,1,0:T(8,128)(2,1)S(1)} %get-tuple-element.291), channel_id=1, source_target_pairs={{16,0},{17,1},{18,2},{19,3},{20,4},{21,5},{22,6},{23,7},{24,8},{25... | collective-permute-start | bytes 1769480 | tf_op jit(solution)/shard_map/ppermute | solution.py:27
  729.8 81.5 %all-reduce.14.cloned.1.call-start = ((), (), s32[]{:S(2)}) async-start(), calls=%async_computation.30 | async-start | bytes 2359296 | tf_op jit(solution)/shard_map/psum | solution.py:185
  773.8 99.9 %all-reduce.16.cloned.1.call-start = ((), (), s32[]{:S(2)}) async-start(), calls=%async_computation.31 | async-start | bytes 1179648 | tf_op jit(solution)/shard_map/psum | solution.py:140
  818.9 16.9 %collective-permute-start.3 = (bf16[1,256,1152]{2,1,0:T(8,128)(2,1)S(1)}, bf16[1,256,1152]{2,1,0:T(8,128)(2,1)S(1)}, u32[]{:S(2)}, u32[]{:S(2)}) collective-permute-start(bf16[1,256,1152]{2,1,0:T(8,128)(2,1)S(1)} %get-tuple-element.295), channel_id=1, source_target_pairs={{16,0},{17,1},{18,2},{19,3},{20,4},{21,5},{22,6},{23,7},{24,8},{25... | collective-permute-start | bytes 1769480 | tf_op jit(solution)/shard_map/ppermute | solution.py:27
  840.8 61.9 %reduce-scatter.28.cloned.1.call-start = ((), (), s32[]{:S(2)}) async-start(), calls=%async_computation.25 | async-start | bytes 1474560 | tf_op jit(solution)/shard_map/reduce_scatter | solution.py:92
  845.1 130.5 %all-reduce.18.cloned.1.call-start = ((), (), s32[]{:S(2)}) async-start(), calls=%async_computation.32 | async-start | bytes 2359296 | tf_op jit(solution)/shard_map/psum | solution.py:185
  884.7 97.8 %all-gather.30.cloned.1.call-start = ((), (), s32[]{:S(2)}) async-start(), calls=%async_computation.26 | async-start | bytes 1474560 | tf_op jit(solution)/shard_map/all_gather | solution.py:98
  902.7 117.1 %reduce-scatter.36.cloned.1.call-start = ((), (), s32[]{:S(2)}) async-start(), calls=%async_computation.36 | async-start | bytes 1105920
  914.3 120.4 %reduce-scatter.34.cloned.1.call-start = ((), (), s32[]{:S(2)}) async-start(), calls=%async_computation.35 | async-start | bytes 2580480
  936.4 152.7 %reduce-scatter.38.cloned.1.call-start = ((), (), s32[]{:S(2)}) async-start(), calls=%async_computation.37 | async-start | bytes 3317760
  960.8 182.9 %reduce-scatter.30.cloned.1.call-start = ((), (), s32[]{:S(2)}) async-start(), calls=%async_computation.33 | async-start | bytes 3317760 | tf_op jit(solution)/shard_map/reduce_scatter | solution.py:386
  967.2 254.2 %reduce-scatter.32.cloned.1.call-start = ((), (), s32[]{:S(2)}) async-start(), calls=%async_computation.34 | async-start | bytes 5160960 | tf_op jit(solution)/shard_map/reduce_scatter | solution.py:392
  (274 other events, 2415.4 us)
Sparse Core Ops, SparseCore 0:
  10.3 100.8 all-gather.13
  113.3 78.2 all-gather.11
  207.3 24.2 reduce-scatter.17
  233.1 17.4 all-gather.15
  252.6 55.3 all-gather.17
  310.1 54.1 all-gather.19
  368.6 24.4 reduce-scatter.19
  394.7 17.4 all-gather.21
  439.0 26.9 reduce-scatter.21
  467.4 17.4 all-gather.23
  491.9 25.7 reduce-scatter.23
  519.0 17.4 all-gather.25
  562.7 26.9 reduce-scatter.25
  591.3 17.4 all-gather.27
  618.0 33.4 all-reduce.7
  663.1 37.2 all-reduce.9
  729.9 32.8 all-reduce.11
  774.0 37.2 all-reduce.13
  840.9 32.8 all-reduce.15
  876.9 25.7 reduce-scatter.27
  905.7 37.2 all-reduce.17
  944.5 17.5 all-gather.29
  965.1 24.5 reduce-scatter.35
  992.5 42.1 reduce-scatter.33
  1037.1 51.9 reduce-scatter.37
  1091.3 52.3 reduce-scatter.29
  1146.0 75.4 reduce-scatter.31
where the time goes:
time: 1320 us; the launch traced here: 1310 us
  waiting for transfers between devices  846 us (64%)
  local copies, waits for them, and re-layouts  141 us (11%)
  blocking collectives  113 us (9%)
  other arithmetic  90.8 us (7%)
  matrix products  85.6 us (6%)
  between operations  23.6 us (2%)
  starting transfers between devices  13.5 us (1%)
    unnamed x583, local copies, waits for them, and re-layouts  113 us
    psum x3, waiting for transfers between devices, block_backward(): lax.psum(jnp.einsum('bsf,df->bsd', up_grad, w_up, preferred_element_type=...  92.4 us
    reduce_scatter x3, waiting for transfers between devices, block_forward(): lax.psum_scatter(jnp.einsum('bse,ed->bsd', attended, w_output, preferred_...  78.5 us
    psum x3, waiting for transfers between devices, block_backward(): lax.psum(jnp.einsum('nbse,nde->bsd', stacked_grad, w_heads, preferred_ele...  74.4 us
    all_gather x1, waiting for transfers between devices, per_device(): lax.all_gather(adaln_weight.astype(jnp.bfloat16), 'dp', axis=1, tiled=True)  74.4 us
    reduce_scatter x1, waiting for transfers between devices, per_device(): lax.psum_scatter(grad_total[4][None].astype(jnp.bfloat16), 'dp', scatter_...  73.3 us
    reduce_scatter x3, waiting for transfers between devices, block_forward(): lax.psum_scatter(jnp.einsum('bsf,fd->bsd', activated, w_down, preferred_e...  68.4 us
    all_gather x1, blocking collectives, per_device(): lax.all_gather(output_weight.astype(jnp.bfloat16), 'dp', axis=2, tiled=True)  66.2 us
  transfers between devices with their start and end apart: 31, of which 28 were waited for; matrix products, arithmetic and copies ran while one was open for 13% of the time, Pallas kernels for 0%

commit v1 on v0

v1 whole, which is shorter than its diff:
```python
import math

import jax
import jax.numpy as jnp
from jax import lax
from jax.sharding import Mesh
from jax.sharding import PartitionSpec as P

HEAD_DIM = 72
STEP = 10

PRECISE = lax.Precision.HIGHEST
NORM_EPS = 1e-06
BETA_ONE = 0.9
BETA_TWO = 0.99
LEARN_RATE = 0.05
WEIGHT_DECAY = 0.01
ADAM_EPS = 1e-08
CLIP_NORM = 1.0
MASK_SCORE = -1000000000.0

BF = jnp.bfloat16
F32 = jnp.float32
PLANE = ("section", "row", "core")
CHIPS = ("section", "row")
ROWS_BY = ("dp", "core")


def dot(left, right, dims, out=F32):
    return lax.dot_general(left, right, (dims, ((), ())), preferred_element_type=F32).astype(out)


def mm(left, right, out=F32):
    return dot(left, right, ((1,), (0,)), out)


def mm_nt(left, right, out=F32):
    return dot(left, right, ((1,), (1,)), out)


def mm_tn(left, right, out=F32):
    return dot(left, right, ((0,), (0,)), out)


def chip_route(offset):
    return [
        (s * 2 + r, (s ^ (offset & 1)) * 2 + (r ^ (offset >> 1)))
        for s in range(2)
        for r in range(2)
    ]


def swap_chips(block, offset):
    return lax.ppermute(block, CHIPS, chip_route(offset))


def swap_cores(block):
    return lax.ppermute(block, "core", [(0, 1), (1, 0)])


def gather_rows(own):
    return jnp.concatenate([own] + [swap_chips(own, offset) for offset in (1, 2, 3)], axis=0)


def sum_rows(partial):
    count = partial.shape[0] // 4
    low = partial.astype(BF)
    total = partial[:count]
    for offset in (1, 2, 3):
        total = total + swap_chips(low[offset * count : (offset + 1) * count], offset).astype(F32)
    return total


def xor_route(size, offset):
    return [(i, i ^ offset) for i in range(size)]


def planes_gather(block):
    size = lax.axis_size("dp")
    parts = [block] + [
        lax.ppermute(block, "dp", xor_route(size, offset)) for offset in range(1, size)
    ]
    return jnp.concatenate(parts, axis=0)


def planes_sum(blocks):
    size = lax.axis_size("dp")
    count = blocks.shape[0] // size
    total = blocks[:count]
    for offset in range(1, size):
        part = blocks[offset * count : (offset + 1) * count]
        total = total + lax.ppermute(part, "dp", xor_route(size, offset))
    return total


def sum_everywhere(values):
    for axis in ("core", "section", "row", "dp"):
        size = lax.axis_size(axis)
        step = 1
        while step < size:
            values = values + lax.ppermute(values, axis, xor_route(size, step))
            step *= 2
    return values


def plane_index(section, core):
    return section * 2 + core


def send_shares(pack, section):
    half = pack.shape[0] // 2
    cases = [(s, c) for s in range(2) for c in range(2)]
    same = lax.dynamic_slice_in_dim(pack, section * half, half, 0)
    other = lax.dynamic_slice_in_dim(pack, (1 - section) * half, half, 0)
    axes = ("section", "core")
    same = lax.ppermute(same, axes, [(s * 2 + c, c * 2 + s) for s, c in cases])
    other = lax.ppermute(other, axes, [(s * 2 + c, c * 2 + 1 - s) for s, c in cases])
    return (same, other)


def return_shares(first, second, section, core):
    cases = [(s, c) for s in range(2) for c in range(2)]
    axes = ("section", "core")
    same = jnp.where(core == 0, first, second)
    other = jnp.where(core == 0, second, first)
    same = lax.ppermute(same, axes, [(s * 2 + h, h * 2 + s) for s, h in cases])
    other = lax.ppermute(other, axes, [(s * 2 + h, (1 - h) * 2 + s) for s, h in cases])
    top = jnp.where(section == 0, same, other)
    bottom = jnp.where(section == 0, other, same)
    return jnp.concatenate([top, bottom], axis=0)


def normalize(values):
    center = values - jnp.mean(values, axis=-1, keepdims=True)
    spread = jnp.mean(center * center, axis=-1, keepdims=True)
    scale = lax.rsqrt(spread + NORM_EPS)
    return (center * scale, scale)


def modulate(values, shift, scale):
    return normalize(values)[0] * (1.0 + scale) + shift


def modulate_back(grad, values, scale):
    unit, inverse = normalize(values)
    shift_grad = jnp.sum(grad, axis=0)
    scale_grad = jnp.sum(grad * unit, axis=0)
    inner = grad * (1.0 + scale)
    mean_one = jnp.mean(inner, axis=-1, keepdims=True)
    mean_two = jnp.mean(inner * unit, axis=-1, keepdims=True)
    return ((inner - mean_one - unit * mean_two) * inverse, shift_grad, scale_grad)


def gelu_tanh(values):
    return jax.nn.gelu(values, approximate=True)


def time_embed(steps_in, model_width):
    half_width = model_width // 2
    frequency = jnp.exp(-math.log(10000.0) * jnp.arange(half_width, dtype=F32) / half_width)
    angles = steps_in.astype(F32)[:, None] * frequency[None, :]
    return jnp.concatenate([jnp.cos(angles), jnp.sin(angles)], axis=-1)


def split_heads(stacked):
    rows, width = stacked.shape
    parts = stacked.reshape(rows, 3, width // 3 // HEAD_DIM, HEAD_DIM)
    return parts[:, 0], parts[:, 1], parts[:, 2]


def scores_of(queries, keys_in, live):
    scores = jnp.einsum("qhe,khe->hqk", queries, keys_in, preferred_element_type=F32)
    return jnp.where(live[None, None, :] > 0, scores * HEAD_DIM ** (-0.5), MASK_SCORE)


def attend(stacked, live):
    queries, keys_in, values = split_heads(stacked)
    scores = scores_of(queries, keys_in, live)
    row_peak = jnp.max(scores, axis=-1, keepdims=True)
    exponent = jnp.exp(scores - row_peak)
    row_total = jnp.sum(exponent, axis=-1, keepdims=True)
    probability = (exponent / row_total).astype(BF)
    attended = jnp.einsum("hqk,khe->qhe", probability, values, preferred_element_type=F32)
    return attended.astype(BF).reshape(stacked.shape[0], -1), row_peak + jnp.log(row_total)


def attend_back(attended_grad, stacked, live, log_total):
    rows = stacked.shape[0]
    queries, keys_in, values = split_heads(stacked)
    grad = attended_grad.reshape(values.shape)
    soft = jnp.exp(scores_of(queries, keys_in, live) - log_total)
    value_grad = jnp.einsum("hqk,qhe->khe", soft.astype(BF), grad, preferred_element_type=F32)
    prob_grad = jnp.einsum("qhe,khe->hqk", grad, values, preferred_element_type=F32)
    score_grad = soft * (prob_grad - jnp.sum(soft * prob_grad, axis=-1, keepdims=True))
    score_grad = score_grad.astype(BF)
    scale = HEAD_DIM ** (-0.5)
    query_grad = jnp.einsum("hqk,khe->qhe", score_grad, keys_in, preferred_element_type=F32) * scale
    key_grad = jnp.einsum("hqk,qhe->khe", score_grad, queries, preferred_element_type=F32) * scale
    stacked_grad = jnp.stack([query_grad, key_grad, value_grad], axis=1).astype(BF)
    return stacked_grad.reshape(rows, -1)


def block_attention(inputs, mod, live, w_attn, own_count):
    columns = w_attn.shape[1] // 4
    shift_a, scale_a, gate_a, shift_b, scale_b = (mod[i][None] for i in range(5))
    normed = modulate(inputs, shift_a, scale_a).astype(BF)
    stacked = mm(normed, w_attn[:, : 3 * columns], BF)
    attended, log_total = attend(stacked, live)
    branch_a = sum_rows(mm_nt(attended, w_attn[:, 3 * columns :]))
    hidden = inputs[:own_count] + gate_a * branch_a
    normed_b = gather_rows(modulate(hidden, shift_b, scale_b).astype(BF))
    return (normed, stacked, attended, log_total, branch_a, hidden, normed_b)


def block_back_feed(grad_all, mod, saved, w_up, w_down, up_value, activated):
    hidden, normed_b, branch_b, branch_a = saved
    own_count = hidden.shape[0]
    gate_a, scale_b, gate_b = (mod[i][None] for i in (2, 4, 5))
    grad_own = grad_all[:own_count]
    gate_b_grad = jnp.sum(grad_own * branch_b, axis=0)
    down_in = (gate_b * grad_all).astype(BF)
    grad_down = mm_tn(down_in, activated, BF)
    act_grad = mm(down_in, w_down)
    up_grad = jax.vjp(gelu_tanh, up_value)[1](act_grad)[0].astype(BF)
    grad_up = mm_tn(normed_b, up_grad, BF)
    normed_grad = sum_rows(mm_nt(up_grad, w_up))
    hidden_grad, shift_b_grad, scale_b_grad = modulate_back(normed_grad, hidden, scale_b)
    hidden_grad = hidden_grad + grad_own
    gate_a_grad = jnp.sum(hidden_grad * branch_a, axis=0)
    output_in = gather_rows((gate_a * hidden_grad).astype(BF))
    return (
        hidden_grad,
        output_in,
        grad_up,
        grad_down,
        (gate_a_grad, shift_b_grad, scale_b_grad, gate_b_grad),
    )


def block_back_attention(output_in, hidden_grad, inputs_own, mod, live, saved, w_attn):
    normed, stacked, attended, log_total = saved
    columns = w_attn.shape[1] // 4
    grad_output = mm_tn(output_in, attended, BF)
    attended_grad = mm(output_in, w_attn[:, 3 * columns :], BF)
    stacked_grad = attend_back(attended_grad, stacked, live, log_total)
    grad_heads = mm_tn(normed, stacked_grad, BF)
    normed_grad = sum_rows(mm_nt(stacked_grad, w_attn[:, : 3 * columns]))
    input_grad, shift_a_grad, scale_a_grad = modulate_back(normed_grad, inputs_own, mod[1][None])
    grad_attn = jnp.concatenate([grad_heads, grad_output], axis=1)
    return (input_grad + hidden_grad, grad_attn, shift_a_grad, scale_a_grad)


def adam_update(weight_in, first_in, second_in, gradient, factor):
    clipped = gradient * factor
    first_out = BETA_ONE * first_in + (1.0 - BETA_ONE) * clipped
    second_out = BETA_TWO * second_in + (1.0 - BETA_TWO) * clipped * clipped
    ratio = (
        first_out
        / (1.0 - BETA_ONE**STEP)
        / (jnp.sqrt(second_out / (1.0 - BETA_TWO**STEP)) + ADAM_EPS)
    )
    weight_out = weight_in - LEARN_RATE * (ratio + WEIGHT_DECAY * weight_in)
    return (weight_out, first_out, second_out)


def per_device(
    tokens,
    cotangent,
    kept_index,
    full_flag,
    labels,
    timesteps,
    class_table,
    heads_weight,
    heads_first,
    heads_second,
    output_weight,
    output_first,
    output_second,
    up_weight,
    up_first,
    up_second,
    down_weight,
    down_first,
    down_second,
    adaln_weight,
    adaln_first,
    adaln_second,
    mask_token,
    mask_first,
    mask_second,
):
    image_count, seq_length, model_width = tokens.shape
    section = lax.axis_index("section")
    core = lax.axis_index("core")
    plane = lax.axis_index("dp")
    chip = lax.axis_index("row") * 2 + section
    quarter = seq_length // 4
    shard = model_width // lax.axis_size("dp")
    columns = heads_weight.shape[-1]

    with jax.named_scope("weights_in"):
        attn_pack = jnp.concatenate(
            [heads_weight[0, 0], heads_weight[0, 1], heads_weight[0, 2], output_weight[0].T], axis=1
        ).astype(BF)
        packs = (attn_pack, up_weight[0].astype(BF), down_weight[0].T.astype(BF))
        shares = [send_shares(pack, section) for pack in packs]
        enc_half = [jnp.where(core == 0, same, other) for same, other in shares]
        dec_half = [jnp.where(core == 0, other, same) for same, other in shares]

        def gather_weight(half):
            return lax.all_gather(half, ROWS_BY, axis=0, tiled=True)

        enc_w = [gather_weight(half) for half in enc_half]
        dec_w = [gather_weight(half) for half in dec_half]

    with jax.named_scope("modulation"):
        codes = planes_gather(jnp.stack([labels, timesteps], axis=1))
        class_count = class_table.shape[0]
        label_hot = (codes[:, :1] == jnp.arange(class_count, dtype=jnp.int32)[None, :]).astype(BF)
        condition = mm(label_hot, class_table) + time_embed(codes[:, 1], model_width)
        cond_act = jax.nn.silu(condition).astype(BF)
        cond_rows = lax.dynamic_slice_in_dim(cond_act, plane * shard, shard, 1)
        adaln_part = planes_sum(mm(cond_rows, adaln_weight[0].astype(BF)))
        adaln_all = lax.all_gather(adaln_part, PLANE, axis=0, tiled=False)
        mod_all = lax.dynamic_index_in_dim(adaln_all, core, 1, keepdims=False)
        mod_all = mod_all.reshape(2, 6, model_width)
        enc_mod, dec_mod = mod_all[0], mod_all[1]

    def relative(values):
        parts = [
            lax.dynamic_slice_in_dim(values, (chip ^ offset) * quarter, quarter, 0)
            for offset in range(4)
        ]
        return jnp.concatenate(parts, axis=0)

    with jax.named_scope("placement"):
        image_tokens = lax.dynamic_index_in_dim(tokens, core, 0, keepdims=False)
        image_cot = relative(lax.dynamic_index_in_dim(cotangent, core, 0, keepdims=False))
        kept = relative(lax.dynamic_index_in_dim(kept_index, core, 0, keepdims=False))
        flag = lax.dynamic_index_in_dim(full_flag, core, 0, keepdims=False)
        plain_ids = jnp.arange(seq_length, dtype=jnp.int32)
        ids = ((plain_ids // quarter) ^ chip) * quarter + plain_ids % quarter
        live = ids < jnp.where(flag > 0, seq_length, seq_length // 2)
        place_plain = ((kept[:, None] == plain_ids[None, :]) & live[:, None]).astype(BF)
        place = ((kept[:, None] == ids[None, :]) & live[:, None]).astype(BF)
        live = live.astype(F32)
        uncovered = 1.0 - jnp.sum(place.astype(F32), axis=0)
        restore = (ids[:, None] == plain_ids[None, :]).astype(BF)
        enc_in = mm(place_plain, image_tokens)

    with jax.named_scope("encoder"):
        normed, stacked, attended, log_total, branch_a, hidden, normed_b = block_attention(
            enc_in, enc_mod, live, enc_w[0], quarter
        )
        up_value = mm(normed_b, enc_w[1])
        activated = gelu_tanh(up_value).astype(BF)
        branch_b = sum_rows(mm_nt(activated, enc_w[2]))
        enc_out = (hidden + enc_mod[5][None] * branch_b) * live[:quarter, None]
        sent = gather_rows(enc_out.astype(BF))
        enc_attn_saved = (normed, stacked, attended, log_total)
        enc_feed_saved = (hidden, normed_b, branch_b, branch_a)
        enc_up, enc_act = up_value, activated

    with jax.named_scope("decoder"):
        dec_in = mm_tn(place, sent) + uncovered[:, None] * mask_token[None, :]
        all_live = jnp.ones_like(live)
        normed, stacked, attended, log_total, branch_a, hidden, normed_b = block_attention(
            dec_in, dec_mod, all_live, dec_w[0], quarter
        )
        up_value = mm(normed_b, dec_w[1])
        activated = gelu_tanh(up_value).astype(BF)
        branch_b = sum_rows(mm_nt(activated, dec_w[2]))
        dec_out = gather_rows((hidden + dec_mod[5][None] * branch_b).astype(BF))
        dec_attn_saved = (normed, stacked, attended, log_total)
        dec_feed_saved = (hidden, normed_b, branch_b, branch_a)

    def reduce_grad(grad):
        return lax.psum_scatter(grad, ROWS_BY, scatter_dimension=0, tiled=True)

    with jax.named_scope("decoder_back"):
        hidden_grad, output_in, grad_up, grad_down, mods = block_back_feed(
            image_cot.astype(F32), dec_mod, dec_feed_saved, dec_w[1], dec_w[2], up_value, activated
        )
        dec_sums = [None, reduce_grad(grad_up), reduce_grad(grad_down)]
        dec_grad, grad_attn, shift_grad, scale_grad = block_back_attention(
            output_in, hidden_grad, dec_in[:quarter], dec_mod, all_live, dec_attn_saved, dec_w[0]
        )
        dec_sums[0] = reduce_grad(grad_attn)
        dec_mods = (shift_grad, scale_grad) + mods
        mask_part = jnp.sum(uncovered[:quarter, None] * dec_grad, axis=0)
        dec_low = gather_rows(dec_grad.astype(BF))

    with jax.named_scope("encoder_back"):
        enc_cot = mm(place, dec_low)
        hidden_grad, output_in, grad_up, grad_down, mods = block_back_feed(
            enc_cot, enc_mod, enc_feed_saved, enc_w[1], enc_w[2], enc_up, enc_act
        )
        enc_sums = [None, reduce_grad(grad_up), reduce_grad(grad_down)]
        enc_grad, grad_attn, shift_grad, scale_grad = block_back_attention(
            output_in, hidden_grad, enc_in[:quarter], enc_mod, live, enc_attn_saved, enc_w[0]
        )
        enc_sums[0] = reduce_grad(grad_attn)
        enc_mods = (shift_grad, scale_grad) + mods
        enc_low = gather_rows(enc_grad.astype(BF))

    with jax.named_scope("modulation_back"):
        mod_parts = jnp.stack([jnp.concatenate(enc_mods), jnp.concatenate(dec_mods)])
        mod_parts = mod_parts.reshape(8, -1)
        mod_parts = lax.all_to_all(mod_parts, PLANE, 0, 0, tiled=True)
        mod_grad = jnp.sum(mod_parts.reshape(4, 2, -1), axis=0)
        mod_grad = planes_gather(mod_grad)
        grad_adaln = lax.dot_general(
            cond_rows.astype(F32), mod_grad, (((0,), (0,)), ((), ())), precision=PRECISE
        )

    with jax.named_scope("norm"):
        square = jnp.sum(grad_adaln * grad_adaln)
        for part in enc_sums + dec_sums:
            wide = part.astype(F32)
            square = square + jnp.sum(wide * wide)
        totals = jnp.concatenate([mask_part, jnp.full((128,), square / 128.0, F32)])
        totals = sum_everywhere(totals.reshape(1, -1))[0]
        mask_total = totals[:model_width]
        grad_norm = jnp.sqrt(jnp.sum(totals[model_width:]) + jnp.sum(mask_total * mask_total))
        factor = jnp.minimum(1.0, CLIP_NORM / (grad_norm + NORM_EPS))

    with jax.named_scope("update"):
        own = [
            return_shares(first, second, section, core).astype(F32)
            for first, second in zip(enc_sums, dec_sums)
        ]
        heads_grad = own[0][:, : 3 * columns].reshape(shard, 3, columns).transpose(1, 0, 2)
        gradients = (
            heads_grad[None],
            own[0][:, 3 * columns :].T[None],
            own[1][None],
            own[2].T[None],
            grad_adaln[None],
        )
        masters = (heads_weight, output_weight, up_weight, down_weight, adaln_weight)
        firsts = (heads_first, output_first, up_first, down_first, adaln_first)
        seconds = (heads_second, output_second, up_second, down_second, adaln_second)
        updated = []
        for position in range(5):
            updated += adam_update(
                masters[position], firsts[position], seconds[position], gradients[position], factor
            )
        mask_next = adam_update(mask_token, mask_first, mask_second, mask_total, factor)

    with jax.named_scope("outputs"):

        def both_images(mine):
            other = swap_cores(mine)
            pair = jnp.where(core == 0, jnp.stack([mine, other]), jnp.stack([other, mine]))
            return pair[None]

        is_first = section == 0
        layer_out = mm_tn(restore, jnp.where(is_first, sent, dec_out), BF)
        arrange = jnp.where(is_first, place_plain, restore)
        in_grads = mm_tn(arrange, jnp.where(is_first, enc_low, dec_low), BF)
        layer_out, in_grads = both_images(layer_out), both_images(in_grads)

    return (layer_out, in_grads, *updated, *mask_next, grad_norm)


def solution(mesh):
    sizes = dict(mesh.shape)
    parted = Mesh(
        mesh.devices.reshape(sizes["section"], sizes["tensor"] // 2, 2, sizes["dp"]),
        ("section", "row", "core", "dp"),
    )
    tensor = ("row", "core")
    heads = P("section", None, "dp", tensor)
    tensor_dp = P("section", tensor, "dp")
    dp_tensor = P("section", "dp", tensor)
    weights = [heads] * 3 + [tensor_dp] * 3 + [dp_tensor] * 3 + [tensor_dp] * 3 + [dp_tensor] * 3
    images = P("dp", None, None)
    layers = P("section", "dp", None, None)
    return jax.shard_map(
        per_device,
        mesh=parted,
        in_specs=(
            images,
            images,
            P("dp", None),
            P("dp"),
            P("dp"),
            P("dp"),
            P(),
            *weights,
            P(),
            P(),
            P(),
        ),
        out_specs=(layers, layers, *weights, P(), P(), P(), P()),
        check_vma=False,
    )
```

time: 1320 us -> 575 us (0.44)
  waiting for transfers between devices: 846 us -> 227 us
  blocking collectives: 113 us -> 9.22 us
  starting transfers between devices: 13.5 us -> 103 us
  local copies, waits for them, and re-layouts: 141 us -> 62.9 us
  other arithmetic: 90.8 us -> 66.1 us
  matrix products: 85.6 us -> 71 us
    all_gather x10 -> x6, waiting for transfers between devices: 292 us -> 69.8 us  [gather_weight(): return lax.all_gather(half, ROWS_BY, axis=0, tiled=True)]
    reduce_scatter x8 -> x6, waiting for transfers between devices: 271 us -> 50.4 us  [reduce_grad(): return lax.psum_scatter(grad, ROWS_BY, scatter_dimension=0, tiled=True)]
    psum x6 -> x0, waiting for transfers between devices: 167 us -> none  [the longest x3 92.4 us: block_backward(): lax.psum(jnp.einsum('bsf,df->bsd', up_grad, w_up, preferred_element_type=...]
    ppermute x4 -> x76, starting transfers between devices: 11.4 us -> 98.3 us  [the longest x48 57.8 us: swap_chips(): return lax.ppermute(block, CHIPS, chip_route(offset))]
    all_gather x2 -> x1, blocking collectives: 71.5 us -> 9.22 us  [per_device(): adaln_all = lax.all_gather(adaln_part, PLANE, axis=0, tiled=False)]
    unnamed x30 -> x12, waiting for transfers between devices: 61.2 us -> 0.7 us
    unnamed x583 -> x350, local copies, waits for them, and re-layouts: 113 us -> 54.6 us
    ppermute x4 -> x76, waiting for transfers between devices: 54.7 us -> 102 us  [the longest x48 67 us: swap_chips(): return lax.ppermute(block, CHIPS, chip_route(offset))]
  transfers between devices with their start and end apart: 31 -> 89, of which waited for: 28 -> 45; matrix products, arithmetic and copies ran while one was open for 13% -> 27% of each run, Pallas kernels for 0% -> 0%
where the time goes in v1:
time: 575 us; the launch traced here: 564 us
  waiting for transfers between devices  227 us (39%)
  starting transfers between devices  103 us (18%)
  matrix products  71 us (12%)
  other arithmetic  66.1 us (11%)
  local copies, waits for them, and re-layouts  62.9 us (11%)
  between operations  24.7 us (4%)
  blocking collectives  9.22 us (2%)
    all_gather x6, waiting for transfers between devices, gather_weight(): return lax.all_gather(half, ROWS_BY, axis=0, tiled=True)  69.8 us
    ppermute x48, waiting for transfers between devices, swap_chips(): return lax.ppermute(block, CHIPS, chip_route(offset))  67 us
    dot_general x31, matrix products, dot(): lax.dot_general(left, right, (dims, ((), ())), preferred_element_type=F32)  64.3 us
    ppermute x48, starting transfers between devices, swap_chips(): return lax.ppermute(block, CHIPS, chip_route(offset))  57.8 us
    unnamed x350, local copies, waits for them, and re-layouts  54.6 us
    reduce_scatter x6, waiting for transfers between devices, reduce_grad(): return lax.psum_scatter(grad, ROWS_BY, scatter_dimension=0, tiled=True)  50.4 us
    ppermute x3, waiting for transfers between devices, send_shares(): lax.ppermute(other, axes, [(s * 2 + c, c * 2 + 1 - s) for s, c in cases])  26.9 us
    sub x6, other arithmetic, adam_update(): weight_out = weight_in - LEARN_RATE * (ratio + WEIGHT_DECAY * weight_in)  18.3 us
  transfers between devices with their start and end apart: 89, of which 45 were waited for; matrix products, arithmetic and copies ran while one was open for 27% of the time, Pallas kernels for 0%

profile of v1, /device:TPU:0, one launch (start us, length us, event | category | flops | bytes accessed | tf_op | source)
XLA Modules:
  0.0 564.1 jit_solution(9196291710293602748)
XLA Ops:
  14.8 3.3 collective-permute-start.7
  18.1 8.7 %collective-permute-done.7 = bf16[144,1152]{1,0:T(8,128)(2,1)S(1)} collective-permute-done((bf16[144,1152]{1,0:T(8,128)(2,1)}, bf16[144,1152]{1,0:T(8,128)(2,1)S(1)}, u32[]{:S(2)}, u32[]{:S(2)}) %collective-permute-start.7) | collective-permute-done | bytes 331808 | tf_op jit(solution)/shard_map/weights_in/ppermute | solution.py:117
  31.0 9.6 %collective-permute-done.15 = bf16[144,1152]{1,0:T(8,128)(2,1)S(1)} collective-permute-done((bf16[144,1152]{1,0:T(8,128)(2,1)S(1)}, bf16[144,1152]{1,0:T(8,128)(2,1)S(1)}, u32[]{:S(2)}, u32[]{:S(2)}) %collective-permute-start.15) | collective-permute-done | bytes 331808 | tf_op jit(solution)/shard_map/weights_in/ppermute | solution.py:117
  44.9 8.5 %collective-permute-done.17 = bf16[144,1152]{1,0:T(8,128)(2,1)S(1)} collective-permute-done((bf16[144,1152]{1,0:T(8,128)(2,1)S(1)}, bf16[144,1152]{1,0:T(8,128)(2,1)S(1)}, u32[]{:S(2)}, u32[]{:S(2)}) %collective-permute-start.17) | collective-permute-done | bytes 331808 | tf_op jit(solution)/shard_map/weights_in/ppermute | solution.py:117
  66.9 3.4 collective-permute-start.4
  71.9 4.0 collective-permute-done.5
  76.0 9.2 %all-gather.1 = f32[8,2,1728]{2,1,0:T(2,128)S(1)} all-gather(f32[1,2,1728]{2,1,0:T(2,128)S(1)} %fusion.141), channel_id=2, replica_groups=mesh['section'=2,'row'=2,'core'=2,'dp'=4] {'section','row','core'}, dimensions={0}, use_global_device_ids=true | all-gather | bytes 124416 | tf_op jit(solution)/shard_map/modulation/all_gather | solution.py:325
  95.3 4.1 collective-permute-done.10
  112.4 3.9 fusion.129
  116.3 17.2 %all-gather.13.cloned.1.call-done = bf16[1152,1152]{1,0:T(8,128)(2,1)} async-done(((bf16[144,1152]{1,0:T(8,128)(2,1)}), bf16[1152,1152]{1,0:T(8,128)(2,1)}) %all-gather.13.cloned.1.call-update) | async-done | bytes 2654224 | tf_op jit(solution)/shard_map/weights_in/all_gather | solution.py:312
  143.6 3.7 collective-permute-done.19
  159.5 9.3 %all-gather.15.cloned.1.call-done = bf16[1152,1152]{1,0:T(8,128)(2,1)} async-done(((bf16[144,1152]{1,0:T(8,128)(2,1)}), bf16[1152,1152]{1,0:T(8,128)(2,1)}) %all-gather.15.cloned.1.call-update) | async-done | bytes 2654224 | tf_op jit(solution)/shard_map/weights_in/all_gather | solution.py:312
  181.7 3.7 collective-permute-done.25
  192.0 12.1 %all-gather.17.cloned.1.call-done = bf16[1152,1152]{1,0:T(8,128)(2,1)} async-done(((bf16[144,1152]{1,0:T(8,128)(2,1)}), bf16[1152,1152]{1,0:T(8,128)(2,1)}) %all-gather.17.cloned.1.call-update) | async-done | bytes 2654224 | tf_op jit(solution)/shard_map/weights_in/all_gather | solution.py:312
  204.1 4.1 fusion.128
  208.1 31.2 %all-gather.19.cloned.1.call-done = bf16[1152,1152]{1,0:T(8,128)(2,1)} async-done(((bf16[144,1152]{1,0:T(8,128)(2,1)}), bf16[1152,1152]{1,0:T(8,128)(2,1)}) %all-gather.19.cloned.1.call-update) | async-done | bytes 2654224 | tf_op jit(solution)/shard_map/weights_in/all_gather | solution.py:312
  239.3 3.7 fusion.35
  243.8 3.7 convolution_convert_fusion.1
  269.4 3.6 collective-permute-done.31
  293.5 5.2 copy.277
  323.8 3.4 convolution_convert_fusion.3
  340.2 3.9 convolution_convert_fusion.2
  375.7 5.2 copy.275
  397.0 3.6 all-to-all-start
  400.6 4.7 all-to-all-done
  427.0 14.4 %reduce-scatter.25.cloned.1.call-done = bf16[144,1152]{1,0:T(8,128)(2,1)} async-done(((bf16[1152,1152]{1,0:T(8,128)(2,1)}), bf16[144,1152]{1,0:T(8,128)(2,1)}) %reduce-scatter.25.cloned.1.call-update) | async-done | bytes 331792 | tf_op jit(solution)/shard_map/encoder_back/reduce_scatter | solution.py:379
  444.4 35.9 %reduce-scatter.19.cloned.1.call-done = bf16[144,1152]{1,0:T(8,128)(2,1)} async-done(((bf16[1152,1152]{1,0:T(8,128)(2,1)}), bf16[144,1152]{1,0:T(8,128)(2,1)}) %reduce-scatter.19.cloned.1.call-update) | async-done | bytes 331792 | tf_op jit(solution)/shard_map/encoder_back/reduce_scatter | solution.py:379
  496.4 4.3 collective-permute-start.74
  501.7 4.3 collective-permute-start.72
  510.6 4.5 collective-permute-start.62
  517.9 6.6 %multiply_subtract_fusion = (f32[1,288,1728]{2,1,0:T(8,128)}, f32[1,288,1728]{2,1,0:T(8,128)}, f32[1,288,1728]{2,1,0:T(8,128)}) fusion(f32[1,288,1728]{2,1,0:T(8,128)S(1)} %copy-done.8, f32[288,1728]{1,0:T(8,128)} %get-tuple-element.292, f32[]{:T(128)S(6)} %min.3, f32[1,288,1728]{2,1,0:T(8,128)} %param.45, f32[1,288,1728]{2,1,0:T(8,128)} %param.46), kind=kLoop, calls=%fused_computation.18 | loop fusion | flops 7962624 | bytes 13934596 | tf_op jit(solution)/shard_map/update/sub | solution.py:262
  543.8 4.3 multiply_subtract_fusion.3
  (692 shorter events, 292.1 us)
Async XLA Ops:
  7.2 78.4 %all-gather.9.cloned.1.call-start = ((), (), s32[]{:S(2)}) async-start(), calls=%async_computation.7 | async-start | bytes 2985984 | tf_op jit(solution)/shard_map/weights_in/all_gather | solution.py:312
  14.8 12.0 %collective-permute-start.7 = (bf16[144,1152]{1,0:T(8,128)(2,1)}, bf16[144,1152]{1,0:T(8,128)(2,1)S(1)}, u32[]{:S(2)}, u32[]{:S(2)}) collective-permute-start(bf16[144,1152]{1,0:T(8,128)(2,1)} %get-tuple-element.224), channel_id=1, source_target_pairs={{0,4},{4,20},{16,0},{20,16},{1,5},{5,21},{17,1},{21,17},{2,6},{6,2... | collective-permute-start | bytes 995336 | tf_op jit(solution)/shard_map/weights_in/ppermute | solution.py:117
  27.8 79.0 %all-gather.11.cloned.1.call-start = ((), (), s32[]{:S(2)}) async-start(), calls=%async_computation.8 | async-start | bytes 2985984 | tf_op jit(solution)/shard_map/weights_in/all_gather | solution.py:312
  30.0 10.7 %collective-permute-start.15 = (bf16[144,1152]{1,0:T(8,128)(2,1)S(1)}, bf16[144,1152]{1,0:T(8,128)(2,1)S(1)}, u32[]{:S(2)}, u32[]{:S(2)}) collective-permute-start(bf16[144,1152]{1,0:T(8,128)(2,1)S(1)} %get-tuple-element.217), channel_id=1, source_target_pairs={{0,4},{4,20},{16,0},{20,16},{1,5},{5,21},{17,1},{21,17},{2,6},{6,2... | collective-permute-start | bytes 995336 | tf_op jit(solution)/shard_map/weights_in/ppermute | solution.py:117
  41.6 92.0 %all-gather.13.cloned.1.call-start = ((), (), s32[]{:S(2)}) async-start(), calls=%async_computation.9 | async-start | bytes 2985984 | tf_op jit(solution)/shard_map/weights_in/all_gather | solution.py:312
  43.9 9.4 %collective-permute-start.17 = (bf16[144,1152]{1,0:T(8,128)(2,1)S(1)}, bf16[144,1152]{1,0:T(8,128)(2,1)S(1)}, u32[]{:S(2)}, u32[]{:S(2)}) collective-permute-start(bf16[144,1152]{1,0:T(8,128)(2,1)S(1)} %get-tuple-element.219), channel_id=1, source_target_pairs={{0,4},{4,20},{16,0},{20,16},{1,5},{5,21},{17,1},{21,17},{2,6},{6,2... | collective-permute-start | bytes 995336 | tf_op jit(solution)/shard_map/weights_in/ppermute | solution.py:117
  54.3 114.5 %all-gather.15.cloned.1.call-start = ((), (), s32[]{:S(2)}) async-start(), calls=%async_computation.10 | async-start | bytes 2985984 | tf_op jit(solution)/shard_map/weights_in/all_gather | solution.py:312
  54.9 149.2 %all-gather.17.cloned.1.call-start = ((), (), s32[]{:S(2)}) async-start(), calls=%async_computation.11 | async-start | bytes 2985984 | tf_op jit(solution)/shard_map/weights_in/all_gather | solution.py:312
  85.6 153.7 %all-gather.19.cloned.1.call-start = ((), (), s32[]{:S(2)}) async-start(), calls=%async_computation.12 | async-start | bytes 2985984 | tf_op jit(solution)/shard_map/weights_in/all_gather | solution.py:312
  138.4 8.9 %collective-permute-start.19 = (bf16[64,1152]{1,0:T(8,128)(2,1)S(1)}, bf16[64,1152]{1,0:T(8,128)(2,1)S(1)}, u32[]{:S(2)}, u32[]{:S(2)}) collective-permute-start(bf16[64,1152]{1,0:T(8,128)(2,1)S(1)} %get-tuple-element.248), channel_id=1, source_target_pairs={{0,8},{8,0},{16,24},{24,16},{1,9},{9,1},{17,25},{25,17},{2,10},{10... | collective-permute-start | bytes 442376 | tf_op jit(solution)/shard_map/encoder/ppermute | solution.py:54
  152.3 267.1 %reduce-scatter.27.cloned.1.call-start = ((), (), s32[]{:S(2)}) async-start(), calls=%async_computation.17 | async-start | bytes 2985984 | tf_op jit(solution)/shard_map/decoder_back/reduce_scatter | solution.py:379
  187.6 16.5 %collective-permute-start.27 = (bf16[64,1152]{1,0:T(8,128)(2,1)}, bf16[64,1152]{1,0:T(8,128)(2,1)}, u32[]{:S(2)}, u32[]{:S(2)}) collective-permute-start(bf16[64,1152]{1,0:T(8,128)(2,1)} %add_convert_fusion.4), channel_id=1, source_target_pairs={{0,16},{8,24},{16,0},{24,8},{1,17},{9,25},{17,1},{25,9},{2,18},{10... | collective-permute-start | bytes 442376 | tf_op jit(solution)/shard_map/decoder/ppermute | solution.py:54
  188.7 15.3 %collective-permute-start.28 = (bf16[64,1152]{1,0:T(8,128)(2,1)}, bf16[64,1152]{1,0:T(8,128)(2,1)}, u32[]{:S(2)}, u32[]{:S(2)}) collective-permute-start(bf16[64,1152]{1,0:T(8,128)(2,1)} %add_convert_fusion.4), channel_id=1, source_target_pairs={{0,8},{8,0},{16,24},{24,16},{1,9},{9,1},{17,25},{25,17},{2,10},{10... | collective-permute-start | bytes 442376 | tf_op jit(solution)/shard_map/decoder/ppermute | solution.py:54
  189.6 14.5 %collective-permute-start.29 = (bf16[64,1152]{1,0:T(8,128)(2,1)}, bf16[64,1152]{1,0:T(8,128)(2,1)}, u32[]{:S(2)}, u32[]{:S(2)}) collective-permute-start(bf16[64,1152]{1,0:T(8,128)(2,1)} %add_convert_fusion.4), channel_id=1, source_target_pairs={{0,24},{8,16},{16,8},{24,0},{1,25},{9,17},{17,9},{25,1},{2,26},{10... | collective-permute-start | bytes 442376 | tf_op jit(solution)/shard_map/decoder/ppermute | solution.py:54
  247.5 173.2 %reduce-scatter.29.cloned.1.call-start = ((), (), s32[]{:S(2)}) async-start(), calls=%async_computation.18 | async-start | bytes 2985984 | tf_op jit(solution)/shard_map/decoder_back/reduce_scatter | solution.py:379
  252.6 171.1 %reduce-scatter.21.cloned.1.call-start = ((), (), s32[]{:S(2)}) async-start(), calls=%async_computation.14 | async-start | bytes 2985984 | tf_op jit(solution)/shard_map/decoder_back/reduce_scatter | solution.py:379
  257.8 8.9 %collective-permute-start.38 = (bf16[64,1152]{1,0:T(8,128)(2,1)S(1)}, bf16[64,1152]{1,0:T(8,128)(2,1)S(1)}, u32[]{:S(2)}, u32[]{:S(2)}) collective-permute-start(bf16[64,1152]{1,0:T(8,128)(2,1)S(1)} %get-tuple-element.239), channel_id=1, source_target_pairs={{0,8},{8,0},{16,24},{24,16},{1,9},{9,1},{17,25},{25,17},{2,10},{10... | collective-permute-start | bytes 442376 | tf_op jit(solution)/shard_map/decoder_back/ppermute | solution.py:54
  262.6 10.4 %collective-permute-start.31 = (bf16[64,1152]{1,0:T(8,128)(2,1)S(1)}, bf16[64,1152]{1,0:T(8,128)(2,1)S(1)}, u32[]{:S(2)}, u32[]{:S(2)}) collective-permute-start(bf16[64,1152]{1,0:T(8,128)(2,1)S(1)} %get-tuple-element.242), channel_id=1, source_target_pairs={{0,8},{8,0},{16,24},{24,16},{1,9},{9,1},{17,25},{25,17},{2,10},{10... | collective-permute-start | bytes 442376 | tf_op jit(solution)/shard_map/decoder/ppermute | solution.py:54
  264.1 8.9 %collective-permute-start.32 = (bf16[64,1152]{1,0:T(8,128)(2,1)S(1)}, bf16[64,1152]{1,0:T(8,128)(2,1)S(1)}, u32[]{:S(2)}, u32[]{:S(2)}) collective-permute-start(bf16[64,1152]{1,0:T(8,128)(2,1)S(1)} %get-tuple-element.241), channel_id=1, source_target_pairs={{0,24},{8,16},{16,8},{24,0},{1,25},{9,17},{17,9},{25,1},{2,26},{10... | collective-permute-start | bytes 442376 | tf_op jit(solution)/shard_map/decoder/ppermute | solution.py:54
  298.7 127.1 %reduce-scatter.23.cloned.1.call-start = ((), (), s32[]{:S(2)}) async-start(), calls=%async_computation.15 | async-start | bytes 2985984 | tf_op jit(solution)/shard_map/encoder_back/reduce_scatter | solution.py:379
  327.3 114.1 %reduce-scatter.25.cloned.1.call-start = ((), (), s32[]{:S(2)}) async-start(), calls=%async_computation.16 | async-start | bytes 2985984 | tf_op jit(solution)/shard_map/encoder_back/reduce_scatter | solution.py:379
  344.2 136.2 %reduce-scatter.19.cloned.1.call-start = ((), (), s32[]{:S(2)}) async-start(), calls=%async_computation.13 | async-start | bytes 2985984 | tf_op jit(solution)/shard_map/encoder_back/reduce_scatter | solution.py:379
  362.5 18.5 %collective-permute-start.33 = (bf16[64,1152]{1,0:T(8,128)(2,1)}, bf16[64,1152]{1,0:T(8,128)(2,1)}, u32[]{:S(2)}, u32[]{:S(2)}) collective-permute-start(bf16[64,1152]{1,0:T(8,128)(2,1)} %get-tuple-element.191), channel_id=1, source_target_pairs={{0,16},{8,24},{16,0},{24,8},{1,17},{9,25},{17,1},{25,9},{2,18},{10... | collective-permute-start | bytes 442376 | tf_op jit(solution)/shard_map/decoder/ppermute | solution.py:54
  364.0 17.0 %collective-permute-start.34 = (bf16[64,1152]{1,0:T(8,128)(2,1)}, bf16[64,1152]{1,0:T(8,128)(2,1)}, u32[]{:S(2)}, u32[]{:S(2)}) collective-permute-start(bf16[64,1152]{1,0:T(8,128)(2,1)} %get-tuple-element.191), channel_id=1, source_target_pairs={{0,8},{8,0},{16,24},{24,16},{1,9},{9,1},{17,25},{25,17},{2,10},{10... | collective-permute-start | bytes 442376 | tf_op jit(solution)/shard_map/decoder/ppermute | solution.py:54
  365.3 15.7 %collective-permute-start.35 = (bf16[64,1152]{1,0:T(8,128)(2,1)}, bf16[64,1152]{1,0:T(8,128)(2,1)}, u32[]{:S(2)}, u32[]{:S(2)}) collective-permute-start(bf16[64,1152]{1,0:T(8,128)(2,1)} %get-tuple-element.191), channel_id=1, source_target_pairs={{0,24},{8,16},{16,8},{24,0},{1,25},{9,17},{17,9},{25,1},{2,26},{10... | collective-permute-start | bytes 442376 | tf_op jit(solution)/shard_map/decoder/ppermute | solution.py:54
  384.6 102.5 %collective-permute-start.36 = (bf16[256,1152]{1,0:T(8,128)(2,1)}, bf16[256,1152]{1,0:T(8,128)(2,1)}, u32[]{:S(2)}, u32[]{:S(2)}) collective-permute-start(bf16[256,1152]{1,0:T(8,128)(2,1)} %convolution_convert_fusion.9), channel_id=1, source_target_pairs={{0,4},{4,0},{1,5},{5,1},{2,6},{6,2},{3,7},{7,3},{8,12},{12,8},{9,1... | collective-permute-start | bytes 1769480 | tf_op jit(solution)/shard_map/outputs/ppermute | solution.py:58
  419.3 72.4 %collective-permute-start.61 = (bf16[256,1152]{1,0:T(8,128)(2,1)S(1)}, bf16[256,1152]{1,0:T(8,128)(2,1)S(1)}, u32[]{:S(2)}, u32[]{:S(2)}) collective-permute-start(bf16[256,1152]{1,0:T(8,128)(2,1)S(1)} %convolution_convert_fusion.8), channel_id=1, source_target_pairs={{0,4},{4,0},{1,5},{5,1},{2,6},{6,2},{3,7},{7,3},{8,12},{12,8},{9,1... | collective-permute-start | bytes 1769480 | tf_op jit(solution)/shard_map/outputs/ppermute | solution.py:58
  496.4 28.8 %collective-permute-start.74 = (bf16[144,1152]{1,0:T(8,128)(2,1)}, bf16[144,1152]{1,0:T(8,128)(2,1)}, u32[]{:S(2)}, u32[]{:S(2)}) collective-permute-start(bf16[144,1152]{1,0:T(8,128)(2,1)} %get-tuple-element.203), channel_id=1, source_target_pairs={{0,0},{4,16},{16,4},{20,20},{1,1},{5,17},{17,5},{21,21},{2,2},{6,1... | collective-permute-start | bytes 995336 | tf_op jit(solution)/shard_map/update/ppermute | solution.py:126
  500.7 24.5 %collective-permute-start.75 = (bf16[144,1152]{1,0:T(8,128)(2,1)}, bf16[144,1152]{1,0:T(8,128)(2,1)}, u32[]{:S(2)}, u32[]{:S(2)}) collective-permute-start(bf16[144,1152]{1,0:T(8,128)(2,1)} %get-tuple-element.204), channel_id=1, source_target_pairs={{0,16},{4,0},{16,20},{20,4},{1,17},{5,1},{17,21},{21,5},{2,18},{6,... | collective-permute-start | bytes 995336 | tf_op jit(solution)/shard_map/update/ppermute | solution.py:127
  501.7 27.3 %collective-permute-start.72 = (bf16[144,1152]{1,0:T(8,128)(2,1)}, bf16[144,1152]{1,0:T(8,128)(2,1)}, u32[]{:S(2)}, u32[]{:S(2)}) collective-permute-start(bf16[144,1152]{1,0:T(8,128)(2,1)} %get-tuple-element.207), channel_id=1, source_target_pairs={{0,0},{4,16},{16,4},{20,20},{1,1},{5,17},{17,5},{21,21},{2,2},{6,1... | collective-permute-start | bytes 995336 | tf_op jit(solution)/shard_map/update/ppermute | solution.py:126
  506.0 23.0 %collective-permute-start.73 = (bf16[144,1152]{1,0:T(8,128)(2,1)}, bf16[144,1152]{1,0:T(8,128)(2,1)}, u32[]{:S(2)}, u32[]{:S(2)}) collective-permute-start(bf16[144,1152]{1,0:T(8,128)(2,1)} %get-tuple-element.208), channel_id=1, source_target_pairs={{0,16},{4,0},{16,20},{20,4},{1,17},{5,1},{17,21},{21,5},{2,18},{6,... | collective-permute-start | bytes 995336 | tf_op jit(solution)/shard_map/update/ppermute | solution.py:127
  510.6 22.5 %collective-permute-start.62 = (bf16[144,1152]{1,0:T(8,128)(2,1)}, bf16[144,1152]{1,0:T(8,128)(2,1)}, u32[]{:S(2)}, u32[]{:S(2)}) collective-permute-start(bf16[144,1152]{1,0:T(8,128)(2,1)} %get-tuple-element.211), channel_id=1, source_target_pairs={{0,0},{4,16},{16,4},{20,20},{1,1},{5,17},{17,5},{21,21},{2,2},{6,1... | collective-permute-start | bytes 995336 | tf_op jit(solution)/shard_map/update/ppermute | solution.py:126
  (218 other events, 1765.7 us)
Sparse Core Ops, SparseCore 0:
  27.9 34.8 all-gather.8
  65.0 33.3 all-gather.10
  100.6 32.8 all-gather.12
  135.6 33.1 all-gather.14
  170.9 33.1 all-gather.16
  206.1 33.1 all-gather.18
  247.6 36.6 reduce-scatter.26
  286.6 36.7 reduce-scatter.28
  325.7 36.8 reduce-scatter.20
  364.8 37.0 reduce-scatter.22
  404.2 37.1 reduce-scatter.24
  443.6 36.7 reduce-scatter.18

commit v2 on v1

--- a/solution.py
+++ b/solution.py
@@ -42,6 +42,19 @@
     return dot(left, right, ((0,), (0,)), out)
 
 
+def turned(values):
+    return mm_tn(values, jnp.eye(values.shape[0], dtype=values.dtype), values.dtype)
+
+
+def paired(left_one, right_one, left_two, right_two):
+    one, two = right_one.shape[1], right_two.shape[1]
+    lefts = jnp.concatenate([left_one, left_two], axis=0)
+    rights = jnp.concatenate(
+        [jnp.pad(right_one, ((0, 0), (0, two))), jnp.pad(right_two, ((0, 0), (one, 0)))], axis=0
+    )
+    return mm_tn(lefts, rights, BF)
+
+
 def chip_route(offset):
     return [
         (s * 2 + r, (s ^ (offset & 1)) * 2 + (r ^ (offset >> 1)))
@@ -94,7 +107,7 @@
 
 
 def sum_everywhere(values):
-    for axis in ("core", "section", "row", "dp"):
+    for axis in ("dp", "row", "section", "core"):
         size = lax.axis_size(axis)
         step = 1
         while step < size:
@@ -103,31 +116,51 @@
     return values
 
 
-def plane_index(section, core):
-    return section * 2 + core
-
-
-def send_shares(pack, section):
+def send_shares(pack, section, core, later=None):
     half = pack.shape[0] // 2
-    cases = [(s, c) for s in range(2) for c in range(2)]
-    same = lax.dynamic_slice_in_dim(pack, section * half, half, 0)
-    other = lax.dynamic_slice_in_dim(pack, (1 - section) * half, half, 0)
-    axes = ("section", "core")
-    same = lax.ppermute(same, axes, [(s * 2 + c, c * 2 + s) for s, c in cases])
-    other = lax.ppermute(other, axes, [(s * 2 + c, c * 2 + 1 - s) for s, c in cases])
-    return (same, other)
+    mine = lax.dynamic_slice_in_dim(pack, core * half, half, 0)
+    other = swap_cores(lax.dynamic_slice_in_dim(pack, (1 - core) * half, half, 0))
+    keep = jnp.where(core == section, mine, other)
+    give = jnp.where(core == section, other, mine)
+    if later is not None:
+        give, later = tie(give, later)
+    given = lax.ppermute(give, "section", [(0, 1), (1, 0)])
+    return (jnp.where(section == 0, keep, given), jnp.where(section == 0, given, keep), later)
 
 
 def return_shares(first, second, section, core):
-    cases = [(s, c) for s in range(2) for c in range(2)]
-    axes = ("section", "core")
-    same = jnp.where(core == 0, first, second)
-    other = jnp.where(core == 0, second, first)
-    same = lax.ppermute(same, axes, [(s * 2 + h, h * 2 + s) for s, h in cases])
-    other = lax.ppermute(other, axes, [(s * 2 + h, (1 - h) * 2 + s) for s, h in cases])
-    top = jnp.where(section == 0, same, other)
-    bottom = jnp.where(section == 0, other, same)
+    keep = jnp.where(section == 0, first, second)
+    give = jnp.where(section == 0, second, first)
+    given = lax.ppermute(give, "section", [(0, 1), (1, 0)])
+    mine = jnp.where(core == section, keep, given)
+    other = swap_cores(jnp.where(core == section, given, keep))
+    top = jnp.where(core == 0, mine, other)
+    bottom = jnp.where(core == 0, other, mine)
     return jnp.concatenate([top, bottom], axis=0)
+
+
+def tie(*values):
+    return lax.optimization_barrier(values)
+
+
+def gather_weight(half):
+    return lax.all_gather(half, ROWS_BY, axis=0, tiled=True)
+
+
+def sum_cores(core, *grads):
+    planes = lax.axis_size("dp")
+    sums = []
+    for grad in grads:
+        halves = grad.reshape(planes, 2, grad.shape[0] // planes // 2, grad.shape[1])
+        theirs = swap_cores(lax.dynamic_index_in_dim(halves, 1 - core, 1, keepdims=False))
+        mine = lax.dynamic_index_in_dim(halves, core, 1, keepdims=False)
+        sums.append((mine.astype(F32) + theirs.astype(F32)).astype(BF))
+    return jnp.concatenate(sums, axis=2)
+
+
+def sum_planes(grad):
+    summed = lax.psum_scatter(grad, "dp", scatter_dimension=0, tiled=True)
+    return summed.reshape(summed.shape[1:])
 
 
 def normalize(values):
@@ -212,42 +245,58 @@
     return (normed, stacked, attended, log_total, branch_a, hidden, normed_b)
 
 
-def block_back_feed(grad_all, mod, saved, w_up, w_down, up_value, activated):
-    hidden, normed_b, branch_b, branch_a = saved
+def block_back_feed(grad_all, mod, saved, w_up, w_down, up_value, activated, split, core, earlier):
+    hidden, normed_b, branch_a = saved
     own_count = hidden.shape[0]
     gate_a, scale_b, gate_b = (mod[i][None] for i in (2, 4, 5))
     grad_own = grad_all[:own_count]
-    gate_b_grad = jnp.sum(grad_own * branch_b, axis=0)
     down_in = (gate_b * grad_all).astype(BF)
-    grad_down = mm_tn(down_in, activated, BF)
+    if split:
+        grad_down = mm_tn(down_in, activated, BF)
+        down_in, grad_down = tie(down_in, grad_down)
+        grad_down = sum_cores(core, grad_down)
     act_grad = mm(down_in, w_down)
     up_grad = jax.vjp(gelu_tanh, up_value)[1](act_grad)[0].astype(BF)
-    grad_up = mm_tn(normed_b, up_grad, BF)
-    normed_grad = sum_rows(mm_nt(up_grad, w_up))
+    sums = []
+    if split:
+        up_grad, grad_down = tie(up_grad, grad_down)
+        sums.append(sum_planes(grad_down))
+        earlier = sums
+    partial, up_grad, down_in = tie(mm_nt(up_grad, w_up), up_grad, down_in)
+    grads = [mm_tn(normed_b, up_grad, BF)]
+    if not split:
+        grads.append(mm_tn(down_in, activated, BF))
+    normed_grad, grad_up = tie(sum_rows(partial), sum_cores(core, *grads))
+    up_sum = sum_planes(grad_up)
+    normed_grad, *earlier = tie(normed_grad, *earlier)
     hidden_grad, shift_b_grad, scale_b_grad = modulate_back(normed_grad, hidden, scale_b)
     hidden_grad = hidden_grad + grad_own
     gate_a_grad = jnp.sum(hidden_grad * branch_a, axis=0)
     output_in = gather_rows((gate_a * hidden_grad).astype(BF))
-    return (
-        hidden_grad,
-        output_in,
-        grad_up,
-        grad_down,
-        (gate_a_grad, shift_b_grad, scale_b_grad, gate_b_grad),
-    )
-
-
-def block_back_attention(output_in, hidden_grad, inputs_own, mod, live, saved, w_attn):
+    mods = (gate_a_grad, shift_b_grad, scale_b_grad)
+    return (hidden_grad, output_in, up_sum, mods, earlier)
+
+
+def block_back_attention(output_in, hidden_grad, inputs_own, mod, live, saved, w_attn, core, earlier):
     normed, stacked, attended, log_total = saved
     columns = w_attn.shape[1] // 4
-    grad_output = mm_tn(output_in, attended, BF)
     attended_grad = mm(output_in, w_attn[:, 3 * columns :], BF)
     stacked_grad = attend_back(attended_grad, stacked, live, log_total)
-    grad_heads = mm_tn(normed, stacked_grad, BF)
-    normed_grad = sum_rows(mm_nt(stacked_grad, w_attn[:, : 3 * columns]))
+    partial = mm_nt(stacked_grad, w_attn[:, : 3 * columns])
+    partial, stacked_grad, output_in = tie(partial, stacked_grad, output_in)
+    grad_attn = paired(normed, stacked_grad, output_in, attended)
+    normed_grad, grad_attn = tie(sum_rows(partial), sum_cores(core, grad_attn))
+    attn_sum = sum_planes(grad_attn)
+    normed_grad, *earlier = tie(normed_grad, *earlier)
     input_grad, shift_a_grad, scale_a_grad = modulate_back(normed_grad, inputs_own, mod[1][None])
-    grad_attn = jnp.concatenate([grad_heads, grad_output], axis=1)
-    return (input_grad + hidden_grad, grad_attn, shift_a_grad, scale_a_grad)
+    input_grad = input_grad + hidden_grad
+    low_grad = gather_rows(input_grad.astype(BF))
+    return (input_grad, low_grad, attn_sum, shift_a_grad, scale_a_grad, earlier)
+
+
+def squared(values):
+    wide = values.astype(F32)
+    return jnp.sum(wide * wide)
 
 
 def adam_update(weight_in, first_in, second_in, gradient, factor):
@@ -303,16 +352,16 @@
         attn_pack = jnp.concatenate(
             [heads_weight[0, 0], heads_weight[0, 1], heads_weight[0, 2], output_weight[0].T], axis=1
         ).astype(BF)
-        packs = (attn_pack, up_weight[0].astype(BF), down_weight[0].T.astype(BF))
-        shares = [send_shares(pack, section) for pack in packs]
-        enc_half = [jnp.where(core == 0, same, other) for same, other in shares]
-        dec_half = [jnp.where(core == 0, other, same) for same, other in shares]
-
-        def gather_weight(half):
-            return lax.all_gather(half, ROWS_BY, axis=0, tiled=True)
-
-        enc_w = [gather_weight(half) for half in enc_half]
-        dec_w = [gather_weight(half) for half in dec_half]
+        *halves, feed_parts = send_shares(attn_pack, section, core, (up_weight[0], down_weight[0]))
+        attn_half = jnp.concatenate(halves, axis=1)
+        feed_pack = jnp.concatenate([feed_parts[0], feed_parts[1].T], axis=1).astype(BF)
+        feed_pack, attn_half = tie(feed_pack, attn_half)
+        attn_all = gather_weight(attn_half)
+        attn_width = attn_pack.shape[1]
+        enc_attn, dec_attn = attn_all[:, :attn_width], attn_all[:, attn_width:]
+        enc_feed_half, dec_feed_half, _ = send_shares(feed_pack, section, core)
+        feed_width = feed_pack.shape[1] // 2
+        enc_feed = gather_weight(enc_feed_half)
 
     with jax.named_scope("modulation"):
         codes = planes_gather(jnp.stack([labels, timesteps], axis=1))
@@ -349,95 +398,149 @@
         restore = (ids[:, None] == plain_ids[None, :]).astype(BF)
         enc_in = mm(place_plain, image_tokens)
 
+    def feed_up(normed_b, feed):
+        up_value = mm(normed_b, feed[:, :feed_width])
+        return up_value, gelu_tanh(up_value).astype(BF)
+
+    def feed_down(activated, feed):
+        return sum_rows(mm_nt(activated, feed[:, feed_width:]))
+
     with jax.named_scope("encoder"):
         normed, stacked, attended, log_total, branch_a, hidden, normed_b = block_attention(
-            enc_in, enc_mod, live, enc_w[0], quarter
-        )
-        up_value = mm(normed_b, enc_w[1])
-        activated = gelu_tanh(up_value).astype(BF)
-        branch_b = sum_rows(mm_nt(activated, enc_w[2]))
+            enc_in, enc_mod, live, enc_attn, quarter
+        )
+        normed_b, dec_feed_half = tie(normed_b, dec_feed_half)
+        dec_feed = gather_weight(dec_feed_half)
+        enc_up_value, enc_act = feed_up(normed_b, enc_feed)
+        branch_b = feed_down(enc_act, enc_feed)
+        enc_branch_b = branch_b
         enc_out = (hidden + enc_mod[5][None] * branch_b) * live[:quarter, None]
         sent = gather_rows(enc_out.astype(BF))
         enc_attn_saved = (normed, stacked, attended, log_total)
-        enc_feed_saved = (hidden, normed_b, branch_b, branch_a)
-        enc_up, enc_act = up_value, activated
+        enc_feed_saved = (hidden, normed_b, branch_a)
 
     with jax.named_scope("decoder"):
         dec_in = mm_tn(place, sent) + uncovered[:, None] * mask_token[None, :]
         all_live = jnp.ones_like(live)
         normed, stacked, attended, log_total, branch_a, hidden, normed_b = block_attention(
-            dec_in, dec_mod, all_live, dec_w[0], quarter
-        )
-        up_value = mm(normed_b, dec_w[1])
-        activated = gelu_tanh(up_value).astype(BF)
-        branch_b = sum_rows(mm_nt(activated, dec_w[2]))
-        dec_out = gather_rows((hidden + dec_mod[5][None] * branch_b).astype(BF))
+            dec_in, dec_mod, all_live, dec_attn, quarter
+        )
+        dec_up_value, dec_act = feed_up(normed_b, dec_feed)
         dec_attn_saved = (normed, stacked, attended, log_total)
-        dec_feed_saved = (hidden, normed_b, branch_b, branch_a)
-
-    def reduce_grad(grad):
-        return lax.psum_scatter(grad, ROWS_BY, scatter_dimension=0, tiled=True)
+        dec_feed_saved = (hidden, normed_b, branch_a)
 
     with jax.named_scope("decoder_back"):
-        hidden_grad, output_in, grad_up, grad_down, mods = block_back_feed(
-            image_cot.astype(F32), dec_mod, dec_feed_saved, dec_w[1], dec_w[2], up_value, activated
-        )
-        dec_sums = [None, reduce_grad(grad_up), reduce_grad(grad_down)]
-        dec_grad, grad_attn, shift_grad, scale_grad = block_back_attention(
-            output_in, hidden_grad, dec_in[:quarter], dec_mod, all_live, dec_attn_saved, dec_w[0]
-        )
-        dec_sums[0] = reduce_grad(grad_attn)
-        dec_mods = (shift_grad, scale_grad) + mods
+        hidden_grad, output_in, dec_up_sum, mods, (dec_down_sum,) = block_back_feed(
+            image_cot.astype(F32),
+            dec_mod,
+            dec_feed_saved,
+            dec_feed[:, :feed_width],
+            dec_feed[:, feed_width:],
+            dec_up_value,
+            dec_act,
+            True,
+            core,
+            [],
+        )
+        dec_grad, dec_low, dec_attn_sum, shift_grad, scale_grad, _ = block_back_attention(
+            output_in,
+            hidden_grad,
+            dec_in[:quarter],
+            dec_mod,
+            all_live,
+            dec_attn_saved,
+            dec_attn,
+            core,
+            [],
+        )
+        dec_low, dec_up_sum, dec_act = tie(dec_low, dec_up_sum, dec_act)
+        branch_b = feed_down(dec_act, dec_feed)
+        dec_out = dec_feed_saved[0] + dec_mod[5][None] * branch_b
+        gate_grad = jnp.sum(image_cot[:quarter].astype(F32) * branch_b, axis=0)
+        dec_mods = (shift_grad, scale_grad) + mods + (gate_grad,)
         mask_part = jnp.sum(uncovered[:quarter, None] * dec_grad, axis=0)
-        dec_low = gather_rows(dec_grad.astype(BF))
+
+    is_first = section == 0
+
+    def both_images(mine):
+        other = swap_cores(mine)
+        pair = jnp.where(core == 0, jnp.stack([mine, other]), jnp.stack([other, mine]))
+        return pair[None]
 
     with jax.named_scope("encoder_back"):
         enc_cot = mm(place, dec_low)
-        hidden_grad, output_in, grad_up, grad_down, mods = block_back_feed(
-            enc_cot, enc_mod, enc_feed_saved, enc_w[1], enc_w[2], enc_up, enc_act
-        )
-        enc_sums = [None, reduce_grad(grad_up), reduce_grad(grad_down)]
-        enc_grad, grad_attn, shift_grad, scale_grad = block_back_attention(
-            output_in, hidden_grad, enc_in[:quarter], enc_mod, live, enc_attn_saved, enc_w[0]
-        )
-        enc_sums[0] = reduce_grad(grad_attn)
-        enc_mods = (shift_grad, scale_grad) + mods
-        enc_low = gather_rows(enc_grad.astype(BF))
+        enc_gate_grad = jnp.sum(enc_cot[:quarter] * enc_branch_b, axis=0)
+        hidden_grad, output_in, enc_feed_sum, mods, (dec_attn_sum,) = block_back_feed(
+            enc_cot,
+            enc_mod,
+            enc_feed_saved,
+            enc_feed[:, :feed_width],
+            enc_feed[:, feed_width:],
+            enc_up_value,
+            enc_act,
+            False,
+            core,
+            [dec_attn_sum],
+        )
+        output_in, dec_out = tie(output_in, dec_out.astype(BF))
+        dec_out = gather_rows(dec_out)
+        layer_out = both_images(mm_tn(restore, jnp.where(is_first, sent, dec_out), BF))
+        enc_grad, enc_low, enc_attn_sum, shift_grad, scale_grad, (enc_feed_sum, layer_out) = block_back_attention(
+            output_in,
+            hidden_grad,
+            enc_in[:quarter],
+            enc_mod,
+            live,
+            enc_attn_saved,
+            enc_attn,
+            core,
+            [enc_feed_sum, layer_out],
+        )
+        enc_mods = (shift_grad, scale_grad) + mods + (enc_gate_grad,)
 
     with jax.named_scope("modulation_back"):
         mod_parts = jnp.stack([jnp.concatenate(enc_mods), jnp.concatenate(dec_mods)])
-        mod_parts = mod_parts.reshape(8, -1)
-        mod_parts = lax.all_to_all(mod_parts, PLANE, 0, 0, tiled=True)
-        mod_grad = jnp.sum(mod_parts.reshape(4, 2, -1), axis=0)
-        mod_grad = planes_gather(mod_grad)
+        mod_parts = lax.all_to_all(mod_parts.reshape(8, -1), PLANE, 0, 0, tiled=True)
+        mod_parts, enc_feed_sum = tie(mod_parts, enc_feed_sum)
+        mod_grad = planes_gather(jnp.sum(mod_parts.reshape(4, 2, -1), axis=0))
+
+    with jax.named_scope("outputs"):
+        arrange = jnp.where(is_first, place_plain, restore)
+        in_grads = both_images(mm_tn(arrange, jnp.where(is_first, enc_low, dec_low), BF))
+
+    with jax.named_scope("returns"):
+        dec_feed_sum = jnp.concatenate([dec_up_sum, dec_down_sum], axis=1)
+        feed_grad = return_shares(enc_feed_sum, dec_feed_sum, section, core)
+        down_grad = turned(feed_grad[:, feed_width:])
+        up_grad = feed_grad[:, :feed_width]
+
+    with jax.named_scope("modulation_back"):
         grad_adaln = lax.dot_general(
             cond_rows.astype(F32), mod_grad, (((0,), (0,)), ((), ())), precision=PRECISE
         )
 
     with jax.named_scope("norm"):
         square = jnp.sum(grad_adaln * grad_adaln)
-        for part in enc_sums + dec_sums:
-            wide = part.astype(F32)
-            square = square + jnp.sum(wide * wide)
+        for part in (dec_attn_sum, up_grad, down_grad):
+            square = square + squared(part)
+        square, grad_adaln, up_grad, down_grad, dec_attn_sum, enc_attn_sum = tie(
+            square, grad_adaln, up_grad, down_grad, dec_attn_sum, enc_attn_sum
+        )
+        square = square + squared(enc_attn_sum)
         totals = jnp.concatenate([mask_part, jnp.full((128,), square / 128.0, F32)])
         totals = sum_everywhere(totals.reshape(1, -1))[0]
+        attn_grad = return_shares(enc_attn_sum, dec_attn_sum, section, core)
+        heads_grad = jnp.stack([attn_grad[:, i * columns : (i + 1) * columns] for i in range(3)])
+        output_grad = turned(attn_grad[:, 3 * columns :])
+        totals, heads_grad, output_grad = tie(totals, heads_grad, output_grad)
         mask_total = totals[:model_width]
         grad_norm = jnp.sqrt(jnp.sum(totals[model_width:]) + jnp.sum(mask_total * mask_total))
         factor = jnp.minimum(1.0, CLIP_NORM / (grad_norm + NORM_EPS))
 
     with jax.named_scope("update"):
-        own = [
-            return_shares(first, second, section, core).astype(F32)
-            for first, second in zip(enc_sums, dec_sums)
-        ]
-        heads_grad = own[0][:, : 3 * columns].reshape(shard, 3, columns).transpose(1, 0, 2)
-        gradients = (
-            heads_grad[None],
-            own[0][:, 3 * columns :].T[None],
-            own[1][None],
-            own[2].T[None],
-            grad_adaln[None],
-        )
+        gradients = [
+            part.astype(F32)[None] for part in (heads_grad, output_grad, up_grad, down_grad)
+        ] + [grad_adaln[None]]
         masters = (heads_weight, output_weight, up_weight, down_weight, adaln_weight)
         firsts = (heads_first, output_first, up_first, down_first, adaln_first)
         seconds = (heads_second, output_second, up_second, down_second, adaln_second)
@@ -447,19 +550,6 @@
                 masters[position], firsts[position], seconds[position], gradients[position], factor
             )
         mask_next = adam_update(mask_token, mask_first, mask_second, mask_total, factor)
-
-    with jax.named_scope("outputs"):
-
-        def both_images(mine):
-            other = swap_cores(mine)
-            pair = jnp.where(core == 0, jnp.stack([mine, other]), jnp.stack([other, mine]))
-            return pair[None]
-
-        is_first = section == 0
-        layer_out = mm_tn(restore, jnp.where(is_first, sent, dec_out), BF)
-        arrange = jnp.where(is_first, place_plain, restore)
-        in_grads = mm_tn(arrange, jnp.where(is_first, enc_low, dec_low), BF)
-        layer_out, in_grads = both_images(layer_out), both_images(in_grads)
 
     return (layer_out, in_grads, *updated, *mask_next, grad_norm)
 

time: 575 us -> 481 us (0.84)
  waiting for transfers between devices: 227 us -> 177 us
  local copies, waits for them, and re-layouts: 62.9 us -> 33.9 us
  starting transfers between devices: 103 us -> 89.3 us
  other arithmetic: 66.1 us -> 72.1 us
    all_gather x6 -> x3, waiting for transfers between devices: 69.8 us -> 36.3 us  [gather_weight(): return lax.all_gather(half, ROWS_BY, axis=0, tiled=True)]
    unnamed x350 -> x273, local copies, waits for them, and re-layouts: 54.6 us -> 21.7 us
    reduce_scatter x6 -> x5, waiting for transfers between devices: 50.4 us -> 18.9 us  [sum_planes(): summed = lax.psum_scatter(grad, 'dp', scatter_dimension=0, tiled=True)]
    ppermute x12 -> x4, starting transfers between devices: 21.5 us -> 7.16 us  [the longest x2 4.73 us: send_shares(): given = lax.ppermute(give, 'section', [(0, 1), (1, 0)])]
    convert_element_type x4 -> x14, other arithmetic: 3.04 us -> 11.6 us  [the longest x6 7.62 us: sum_cores(): sums.append((mine.astype(F32) + theirs.astype(F32)).astype(BF))]
    ppermute x5, waiting for transfers between devices: 2.24 us -> 8.99 us  [sum_everywhere(): values = values + lax.ppermute(values, axis, xor_route(size, step))]
    ppermute x12 -> x4, waiting for transfers between devices: 26.9 us -> 32.9 us  [the longest x2 22.1 us: send_shares(): given = lax.ppermute(give, 'section', [(0, 1), (1, 0)])]
  transfers between devices with their start and end apart: 89 -> 87, of which waited for: 45 -> 45; matrix products, arithmetic and copies ran while one was open for 27% -> 26% of each run, Pallas kernels for 0% -> 0%
where the time goes in v2:
time: 481 us; the launch traced here: 472 us
  waiting for transfers between devices  177 us (37%)
  starting transfers between devices  89.3 us (19%)
  other arithmetic  72.1 us (15%)
  matrix products  68.4 us (14%)
  local copies, waits for them, and re-layouts  33.9 us (7%)
  between operations  23 us (5%)
  blocking collectives  9.15 us (2%)
    ppermute x48, waiting for transfers between devices, swap_chips(): return lax.ppermute(block, CHIPS, chip_route(offset))  67.1 us
    dot_general x31, matrix products, dot(): lax.dot_general(left, right, (dims, ((), ())), preferred_element_type=F32)  60.9 us
    ppermute x48, starting transfers between devices, swap_chips(): return lax.ppermute(block, CHIPS, chip_route(offset))  56.7 us
    all_gather x3, waiting for transfers between devices, gather_weight(): return lax.all_gather(half, ROWS_BY, axis=0, tiled=True)  36.3 us
    ppermute x2, waiting for transfers between devices, send_shares(): given = lax.ppermute(give, 'section', [(0, 1), (1, 0)])  22.1 us
    unnamed x273, local copies, waits for them, and re-layouts  21.7 us
    reduce_scatter x5, waiting for transfers between devices, sum_planes(): summed = lax.psum_scatter(grad, 'dp', scatter_dimension=0, tiled=True)  18.9 us
    sub x6, other arithmetic, adam_update(): weight_out = weight_in - LEARN_RATE * (ratio + WEIGHT_DECAY * weight_in)  15.4 us
  transfers between devices with their start and end apart: 87, of which 45 were waited for; matrix products, arithmetic and copies ran while one was open for 26% of the time, Pallas kernels for 0%

profile of v2, /device:TPU:0, one launch (start us, length us, event | category | flops | bytes accessed | tf_op | source)
XLA Modules:
  0.0 472.3 jit_solution(1580316335618834817)
XLA Ops:
  16.3 2.9 collective-permute-start.7
  20.4 7.0 %collective-permute-done.7 = bf16[144,1152]{1,0:T(8,128)(2,1)S(1)} collective-permute-done((bf16[144,1152]{1,0:T(8,128)(2,1)S(1)}, bf16[144,1152]{1,0:T(8,128)(2,1)S(1)}, u32[]{:S(2)}, u32[]{:S(2)}) %collective-permute-start.7) | collective-permute-done | bytes 331808 | tf_op jit(solution)/shard_map/weights_in/ppermute | solution.py:127
  34.0 15.2 %collective-permute-done.15 = bf16[144,2304]{1,0:T(8,128)(2,1)S(1)} collective-permute-done((bf16[144,2304]{1,0:T(8,128)(2,1)S(1)}, bf16[144,2304]{1,0:T(8,128)(2,1)S(1)}, u32[]{:S(2)}, u32[]{:S(2)}) %collective-permute-start.15) | collective-permute-done | bytes 663584 | tf_op jit(solution)/shard_map/weights_in/ppermute | solution.py:127
  50.7 3.9 collective-permute-start.2
  61.3 3.8 collective-permute-start.5
  67.2 3.7 collective-permute-done.4
  70.9 9.2 %all-gather.1 = f32[8,2,1728]{2,1,0:T(2,128)S(1)} all-gather(f32[1,2,1728]{2,1,0:T(2,128)S(1)} %fusion.185), channel_id=2, replica_groups=mesh['section'=2,'row'=2,'core'=2,'dp'=4] {'section','row','core'}, dimensions={0}, use_global_device_ids=true | all-gather | bytes 124416 | tf_op jit(solution)/shard_map/modulation/all_gather | solution.py:374
  80.7 7.2 %all-gather.6.cloned.1.call-done = bf16[1152,2304]{1,0:T(8,128)(2,1)} async-done(((bf16[144,2304]{1,0:T(8,128)(2,1)}), bf16[1152,2304]{1,0:T(8,128)(2,1)}) %all-gather.6.cloned.1.call-update) | async-done | bytes 5308432 | tf_op jit(solution)/shard_map/weights_in/all_gather | solution.py:147
  97.1 4.1 collective-permute-done.10
  108.3 4.2 collective-permute-done.13
  117.2 28.2 %all-gather.8.cloned.1.call-done = bf16[1152,2304]{1,0:T(8,128)(2,1)} async-done(((bf16[144,2304]{1,0:T(8,128)(2,1)}), bf16[1152,2304]{1,0:T(8,128)(2,1)}) %all-gather.8.cloned.1.call-update) | async-done | bytes 5308432 | tf_op jit(solution)/shard_map/weights_in/all_gather | solution.py:147
  148.2 3.3 fusion.233
  155.3 3.9 collective-permute-done.18
  165.6 4.0 collective-permute-done.21
  183.6 4.0 collective-permute-done.24
  196.0 3.2 collective-permute-done.27
  203.0 3.1 multiply_convert_fusion.1
  213.1 4.1 fusion.14
  227.5 4.1 collective-permute-done.31
  238.6 4.6 reduce-scatter.6.cloned.1.call-done
  250.5 3.6 collective-permute-done.35
  271.4 4.1 collective-permute-done.38
  296.1 3.7 fusion.55
  356.3 14.3 %reduce-scatter.12.cloned.1.call-done = bf16[1,144,2304]{2,1,0:T(8,128)(2,1)} async-done(((bf16[4,144,2304]{2,1,0:T(8,128)(2,1)}), bf16[1,144,2304]{2,1,0:T(8,128)(2,1)}) %reduce-scatter.12.cloned.1.call-update) | async-done | bytes 663568 | tf_op jit(solution)/shard_map/encoder_back/reduce_scatter | solution.py:162
  371.8 3.7 all-to-all-start
  376.7 3.5 all-to-all-done
  387.3 10.8 %collective-permute-done.69 = bf16[144,2304]{1,0:T(8,128)(2,1)} collective-permute-done((bf16[144,2304]{1,0:T(8,128)(2,1)}, bf16[144,2304]{1,0:T(8,128)(2,1)}, u32[]{:S(2)}, u32[]{:S(2)}) %collective-permute-start.69) | collective-permute-done | bytes 663584 | tf_op jit(solution)/shard_map/returns/ppermute | solution.py:134
  404.4 3.7 multiply_reduce_fusion
  434.1 2.9 collective-permute-done.74
  437.8 2.9 maximum_select_fusion.1
  444.9 4.5 multiply_subtract_fusion.3
  460.2 3.7 multiply_subtract_fusion
  (633 shorter events, 264.2 us)
Async XLA Ops:
  7.2 80.7 %all-gather.6.cloned.1.call-start = ((), (), s32[]{:S(2)}) async-start(), calls=%async_computation.6 | async-start | bytes 5971968 | tf_op jit(solution)/shard_map/weights_in/all_gather | solution.py:147
  16.3 11.0 %collective-permute-start.7 = (bf16[144,1152]{1,0:T(8,128)(2,1)S(1)}, bf16[144,1152]{1,0:T(8,128)(2,1)S(1)}, u32[]{:S(2)}, u32[]{:S(2)}) collective-permute-start(bf16[144,1152]{1,0:T(8,128)(2,1)S(1)} %broadcast_select_fusion.19), channel_id=1, source_target_pairs={{0,16},{16,0},{1,17},{17,1},{2,18},{18,2},{3,19},{19,3},{4,20},{20... | collective-permute-start | bytes 995336 | tf_op jit(solution)/shard_map/weights_in/ppermute | solution.py:127
  28.5 116.9 %all-gather.8.cloned.1.call-start = ((), (), s32[]{:S(2)}) async-start(), calls=%async_computation.7 | async-start | bytes 5971968 | tf_op jit(solution)/shard_map/weights_in/all_gather | solution.py:147
  32.2 17.0 %collective-permute-start.15 = (bf16[144,2304]{1,0:T(8,128)(2,1)S(1)}, bf16[144,2304]{1,0:T(8,128)(2,1)S(1)}, u32[]{:S(2)}, u32[]{:S(2)}) collective-permute-start(bf16[144,2304]{1,0:T(8,128)(2,1)S(1)} %broadcast_select_fusion.5), channel_id=1, source_target_pairs={{0,16},{16,0},{1,17},{17,1},{2,18},{18,2},{3,19},{19,3},{4,20},{20... | collective-permute-start | bytes 1990664 | tf_op jit(solution)/shard_map/weights_in/ppermute | solution.py:127
  50.6 152.4 %all-gather.10.cloned.1.call-start = ((), (), s32[]{:S(2)}) async-start(), calls=%async_computation.8 | async-start | bytes 5971968 | tf_op jit(solution)/shard_map/encoder/all_gather | solution.py:147
  114.9 128.3 %reduce-scatter.6.cloned.1.call-start = ((), (), s32[]{:S(2)}) async-start(), calls=%async_computation.9 | async-start | bytes 1658880 | tf_op jit(solution)/shard_map/decoder_back/reduce_scatter | solution.py:162
  212.5 81.8 %reduce-scatter.8.cloned.1.call-start = ((), (), s32[]{:S(2)}) async-start(), calls=%async_computation.10 | async-start | bytes 1658880 | tf_op jit(solution)/shard_map/decoder_back/reduce_scatter | solution.py:162
  221.0 14.9 %collective-permute-start.32 = (bf16[4,144,1152]{2,1,0:T(8,128)(2,1)}, bf16[4,144,1152]{2,1,0:T(8,128)(2,1)}, u32[]{:S(2)}, u32[]{:S(2)}) collective-permute-start(bf16[4,144,1152]{2,1,0:T(8,128)(2,1)} %dynamic-slice_bitcast_fusion.4), channel_id=1, source_target_pairs={{0,4},{4,0},{1,5},{5,1},{2,6},{6,2},{3,7},{7,3},{8,12},{12,8},{9,1... | collective-permute-start | bytes 3981320 | tf_op jit(solution)/shard_map/decoder_back/ppermute | solution.py:71
  250.4 67.5 %reduce-scatter.10.cloned.1.call-start = ((), (), s32[]{:S(2)}) async-start(), calls=%async_computation.11 | async-start | bytes 1658880 | tf_op jit(solution)/shard_map/decoder_back/reduce_scatter | solution.py:162
  266.6 11.9 %collective-permute-start.39 = (bf16[4,144,1152]{2,1,0:T(8,128)(2,1)S(1)}, bf16[4,144,1152]{2,1,0:T(8,128)(2,1)S(1)}, u32[]{:S(2)}, u32[]{:S(2)}) collective-permute-start(bf16[4,144,1152]{2,1,0:T(8,128)(2,1)S(1)} %dynamic-slice_bitcast_fusion.3), channel_id=1, source_target_pairs={{0,4},{4,0},{1,5},{5,1},{2,6},{6,2},{3,7},{7,3},{8,12},{12,8},{9,1... | collective-permute-start | bytes 3981320 | tf_op jit(solution)/shard_map/decoder_back/ppermute | solution.py:71
  283.1 10.3 %collective-permute-start.42 = (bf16[64,1152]{1,0:T(8,128)(2,1)}, bf16[64,1152]{1,0:T(8,128)(2,1)S(1)}, u32[]{:S(2)}, u32[]{:S(2)}) collective-permute-start(bf16[64,1152]{1,0:T(8,128)(2,1)} %get-tuple-element.186), channel_id=1, source_target_pairs={{0,24},{8,16},{16,8},{24,0},{1,25},{9,17},{17,9},{25,1},{2,26},{10... | collective-permute-start | bytes 442376 | tf_op jit(solution)/shard_map/decoder_back/ppermute | solution.py:67
  286.6 84.0 %reduce-scatter.12.cloned.1.call-start = ((), (), s32[]{:S(2)}) async-start(), calls=%async_computation.12 | async-start | bytes 3317760 | tf_op jit(solution)/shard_map/encoder_back/reduce_scatter | solution.py:162
  301.0 10.8 %collective-permute-start.45 = (bf16[64,1152]{1,0:T(8,128)(2,1)S(1)}, bf16[64,1152]{1,0:T(8,128)(2,1)S(1)}, u32[]{:S(2)}, u32[]{:S(2)}) collective-permute-start(bf16[64,1152]{1,0:T(8,128)(2,1)S(1)} %get-tuple-element.221), channel_id=1, source_target_pairs={{0,24},{8,16},{16,8},{24,0},{1,25},{9,17},{17,9},{25,1},{2,26},{10... | collective-permute-start | bytes 442376 | tf_op jit(solution)/shard_map/encoder_back/ppermute | solution.py:67
  302.7 10.8 %collective-permute-start.44 = (bf16[64,1152]{1,0:T(8,128)(2,1)S(1)}, bf16[64,1152]{1,0:T(8,128)(2,1)S(1)}, u32[]{:S(2)}, u32[]{:S(2)}) collective-permute-start(bf16[64,1152]{1,0:T(8,128)(2,1)S(1)} %get-tuple-element.222), channel_id=1, source_target_pairs={{0,8},{8,0},{16,24},{24,16},{1,9},{9,1},{17,25},{25,17},{2,10},{10... | collective-permute-start | bytes 442376 | tf_op jit(solution)/shard_map/encoder_back/ppermute | solution.py:67
  304.0 10.8 %collective-permute-start.43 = (bf16[64,1152]{1,0:T(8,128)(2,1)S(1)}, bf16[64,1152]{1,0:T(8,128)(2,1)S(1)}, u32[]{:S(2)}, u32[]{:S(2)}) collective-permute-start(bf16[64,1152]{1,0:T(8,128)(2,1)S(1)} %get-tuple-element.220), channel_id=1, source_target_pairs={{0,16},{8,24},{16,0},{24,8},{1,17},{9,25},{17,1},{25,9},{2,18},{10... | collective-permute-start | bytes 442376 | tf_op jit(solution)/shard_map/encoder_back/ppermute | solution.py:67
  305.7 9.7 %collective-permute-start.47 = (bf16[4,144,1152]{2,1,0:T(8,128)(2,1)S(1)}, bf16[4,144,1152]{2,1,0:T(8,128)(2,1)S(1)}, u32[]{:S(2)}, u32[]{:S(2)}) collective-permute-start(bf16[4,144,1152]{2,1,0:T(8,128)(2,1)S(1)} %dynamic-slice_bitcast_fusion.1), channel_id=1, source_target_pairs={{0,4},{4,0},{1,5},{5,1},{2,6},{6,2},{3,7},{7,3},{8,12},{12,8},{9,1... | collective-permute-start | bytes 3981320 | tf_op jit(solution)/shard_map/encoder_back/ppermute | solution.py:71
  311.8 12.8 %collective-permute-start.53 = (bf16[64,1152]{1,0:T(8,128)(2,1)}, bf16[64,1152]{1,0:T(8,128)(2,1)}, u32[]{:S(2)}, u32[]{:S(2)}) collective-permute-start(bf16[64,1152]{1,0:T(8,128)(2,1)} %get-tuple-element.218), channel_id=1, source_target_pairs={{0,24},{8,16},{16,8},{24,0},{1,25},{9,17},{17,9},{25,1},{2,26},{10... | collective-permute-start | bytes 442376 | tf_op jit(solution)/shard_map/decoder_back/ppermute | solution.py:67
  313.5 11.7 %collective-permute-start.52 = (bf16[64,1152]{1,0:T(8,128)(2,1)}, bf16[64,1152]{1,0:T(8,128)(2,1)}, u32[]{:S(2)}, u32[]{:S(2)}) collective-permute-start(bf16[64,1152]{1,0:T(8,128)(2,1)} %get-tuple-element.219), channel_id=1, source_target_pairs={{0,8},{8,0},{16,24},{24,16},{1,9},{9,1},{17,25},{25,17},{2,10},{10... | collective-permute-start | bytes 442376 | tf_op jit(solution)/shard_map/decoder_back/ppermute | solution.py:67
  314.8 10.4 %collective-permute-start.51 = (bf16[64,1152]{1,0:T(8,128)(2,1)}, bf16[64,1152]{1,0:T(8,128)(2,1)}, u32[]{:S(2)}, u32[]{:S(2)}) collective-permute-start(bf16[64,1152]{1,0:T(8,128)(2,1)} %get-tuple-element.217), channel_id=1, source_target_pairs={{0,16},{8,24},{16,0},{24,8},{1,17},{9,25},{17,1},{25,9},{2,18},{10... | collective-permute-start | bytes 442376 | tf_op jit(solution)/shard_map/decoder_back/ppermute | solution.py:67
  330.2 14.6 %collective-permute-start.60 = (bf16[64,1152]{1,0:T(8,128)(2,1)S(1)}, bf16[64,1152]{1,0:T(8,128)(2,1)S(1)}, u32[]{:S(2)}, u32[]{:S(2)}) collective-permute-start(bf16[64,1152]{1,0:T(8,128)(2,1)S(1)} %get-tuple-element.108), channel_id=1, source_target_pairs={{0,24},{8,16},{16,8},{24,0},{1,25},{9,17},{17,9},{25,1},{2,26},{10... | collective-permute-start | bytes 442376 | tf_op jit(solution)/shard_map/encoder_back/ppermute | solution.py:67
  331.9 14.2 %collective-permute-start.59 = (bf16[64,1152]{1,0:T(8,128)(2,1)S(1)}, bf16[64,1152]{1,0:T(8,128)(2,1)S(1)}, u32[]{:S(2)}, u32[]{:S(2)}) collective-permute-start(bf16[64,1152]{1,0:T(8,128)(2,1)S(1)} %get-tuple-element.108), channel_id=1, source_target_pairs={{0,8},{8,0},{16,24},{24,16},{1,9},{9,1},{17,25},{25,17},{2,10},{10... | collective-permute-start | bytes 442376 | tf_op jit(solution)/shard_map/encoder_back/ppermute | solution.py:67
  333.2 13.5 %collective-permute-start.58 = (bf16[64,1152]{1,0:T(8,128)(2,1)S(1)}, bf16[64,1152]{1,0:T(8,128)(2,1)S(1)}, u32[]{:S(2)}, u32[]{:S(2)}) collective-permute-start(bf16[64,1152]{1,0:T(8,128)(2,1)S(1)} %get-tuple-element.108), channel_id=1, source_target_pairs={{0,16},{8,24},{16,0},{24,8},{1,17},{9,25},{17,1},{25,9},{2,18},{10... | collective-permute-start | bytes 442376 | tf_op jit(solution)/shard_map/encoder_back/ppermute | solution.py:67
  343.0 11.9 %collective-permute-start.57 = (bf16[4,144,1152]{2,1,0:T(8,128)(2,1)S(1)}, bf16[4,144,1152]{2,1,0:T(8,128)(2,1)S(1)}, u32[]{:S(2)}, u32[]{:S(2)}) collective-permute-start(bf16[4,144,1152]{2,1,0:T(8,128)(2,1)S(1)} %dynamic-slice_bitcast_fusion), channel_id=1, source_target_pairs={{0,4},{4,0},{1,5},{5,1},{2,6},{6,2},{3,7},{7,3},{8,12},{12,8},{9,1... | collective-permute-start | bytes 3981320 | tf_op jit(solution)/shard_map/encoder_back/ppermute | solution.py:71
  375.4 43.4 %reduce-scatter.14.cloned.1.call-start = ((), (), s32[]{:S(2)}) async-start(), calls=%async_computation.13 | async-start | bytes 1658880 | tf_op jit(solution)/shard_map/encoder_back/reduce_scatter | solution.py:162
  381.2 16.9 %collective-permute-start.69 = (bf16[144,2304]{1,0:T(8,128)(2,1)}, bf16[144,2304]{1,0:T(8,128)(2,1)}, u32[]{:S(2)}, u32[]{:S(2)}) collective-permute-start(bf16[144,2304]{1,0:T(8,128)(2,1)} %broadcast_select_fusion.6), channel_id=1, source_target_pairs={{0,16},{16,0},{1,17},{17,1},{2,18},{18,2},{3,19},{19,3},{4,20},{20... | collective-permute-start | bytes 1990664 | tf_op jit(solution)/shard_map/returns/ppermute | solution.py:134
  382.8 18.1 %collective-permute-start.68 = (f32[2,1728]{1,0:T(2,128)S(1)}, f32[2,1728]{1,0:T(2,128)S(1)}, u32[]{:S(2)}, u32[]{:S(2)}) collective-permute-start(f32[2,1728]{1,0:T(2,128)S(1)} %reduce_sum.468), channel_id=1, source_target_pairs={{0,3},{1,2},{2,1},{3,0},{4,7},{5,6},{6,5},{7,4},{8,11},{9,10},{10,... | collective-permute-start | bytes 41480 | tf_op jit(solution)/shard_map/modulation_back/ppermute | solution.py:94
  384.9 17.5 %collective-permute-start.67 = (f32[2,1728]{1,0:T(2,128)S(1)}, f32[2,1728]{1,0:T(2,128)S(1)}, u32[]{:S(2)}, u32[]{:S(2)}) collective-permute-start(f32[2,1728]{1,0:T(2,128)S(1)} %reduce_sum.468), channel_id=1, source_target_pairs={{0,2},{1,3},{2,0},{3,1},{4,6},{5,7},{6,4},{7,5},{8,10},{9,11},{10,... | collective-permute-start | bytes 41480 | tf_op jit(solution)/shard_map/modulation_back/ppermute | solution.py:94
  385.1 19.3 %collective-permute-start.66 = (f32[2,1728]{1,0:T(2,128)S(1)}, f32[2,1728]{1,0:T(2,128)S(1)}, u32[]{:S(2)}, u32[]{:S(2)}) collective-permute-start(f32[2,1728]{1,0:T(2,128)S(1)} %reduce_sum.468), channel_id=1, source_target_pairs={{0,1},{1,0},{2,3},{3,2},{4,5},{5,4},{6,7},{7,6},{8,9},{9,8},{10,11... | collective-permute-start | bytes 41480 | tf_op jit(solution)/shard_map/modulation_back/ppermute | solution.py:94
  400.1 13.2 %collective-permute-start.70 = (bf16[144,2304]{1,0:T(8,128)(2,1)}, bf16[144,2304]{1,0:T(8,128)(2,1)}, u32[]{:S(2)}, u32[]{:S(2)}) collective-permute-start(bf16[144,2304]{1,0:T(8,128)(2,1)} %broadcast_select_fusion.2), channel_id=1, source_target_pairs={{0,4},{4,0},{1,5},{5,1},{2,6},{6,2},{3,7},{7,3},{8,12},{12,8},{9,1... | collective-permute-start | bytes 1990664 | tf_op jit(solution)/shard_map/returns/ppermute | solution.py:71
  400.9 9.7 %collective-permute-start.63 = (bf16[64,1152]{1,0:T(8,128)(2,1)}, bf16[64,1152]{1,0:T(8,128)(2,1)S(1)}, u32[]{:S(2)}, u32[]{:S(2)}) collective-permute-start(bf16[64,1152]{1,0:T(8,128)(2,1)} %add_convert_fusion.2), channel_id=1, source_target_pairs={{0,8},{8,0},{16,24},{24,16},{1,9},{9,1},{17,25},{25,17},{2,10},{10... | collective-permute-start | bytes 442376 | tf_op jit(solution)/shard_map/encoder_back/ppermute | solution.py:67
  413.2 24.5 %collective-permute-start.65 = (bf16[256,1152]{1,0:T(8,128)(2,1)}, bf16[256,1152]{1,0:T(8,128)(2,1)}, u32[]{:S(2)}, u32[]{:S(2)}) collective-permute-start(bf16[256,1152]{1,0:T(8,128)(2,1)} %convolution_convert_fusion.7), channel_id=1, source_target_pairs={{0,4},{4,0},{1,5},{5,1},{2,6},{6,2},{3,7},{7,3},{8,12},{12,8},{9,1... | collective-permute-start | bytes 1769480 | tf_op jit(solution)/shard_map/outputs/ppermute | solution.py:71
  422.2 14.9 %collective-permute-start.76 = (bf16[144,1152]{1,0:T(8,128)(2,1)S(1)}, bf16[144,1152]{1,0:T(8,128)(2,1)S(1)}, u32[]{:S(2)}, u32[]{:S(2)}) collective-permute-start(bf16[144,1152]{1,0:T(8,128)(2,1)S(1)} %broadcast_select_fusion.12), channel_id=1, source_target_pairs={{0,16},{16,0},{1,17},{17,1},{2,18},{18,2},{3,19},{19,3},{4,20},{20... | collective-permute-start | bytes 995336 | tf_op jit(solution)/shard_map/norm/ppermute | solution.py:134
  (186 other events, 2287.0 us)
Sparse Core Ops, SparseCore 0:
  28.6 59.2 all-gather.5
  90.1 55.2 all-gather.7
  147.6 55.3 all-gather.9
  212.7 30.4 reduce-scatter.5
  250.5 30.4 reduce-scatter.7
  286.7 30.0 reduce-scatter.9
  319.1 51.4 reduce-scatter.11
  382.8 30.4 reduce-scatter.13

commit v3 on v2

--- a/solution.py
+++ b/solution.py
@@ -3,6 +3,8 @@
 import jax
 import jax.numpy as jnp
 from jax import lax
+from jax.experimental import pallas as pl
+from jax.experimental.pallas import tpu as pltpu
 from jax.sharding import Mesh
 from jax.sharding import PartitionSpec as P
 
@@ -46,15 +48,6 @@
     return mm_tn(values, jnp.eye(values.shape[0], dtype=values.dtype), values.dtype)
 
 
-def paired(left_one, right_one, left_two, right_two):
-    one, two = right_one.shape[1], right_two.shape[1]
-    lefts = jnp.concatenate([left_one, left_two], axis=0)
-    rights = jnp.concatenate(
-        [jnp.pad(right_one, ((0, 0), (0, two))), jnp.pad(right_two, ((0, 0), (one, 0)))], axis=0
-    )
-    return mm_tn(lefts, rights, BF)
-
-
 def chip_route(offset):
     return [
         (s * 2 + r, (s ^ (offset & 1)) * 2 + (r ^ (offset >> 1)))
@@ -75,13 +68,16 @@
     return jnp.concatenate([own] + [swap_chips(own, offset) for offset in (1, 2, 3)], axis=0)
 
 
+def spread_rows(partial):
+    count = partial.shape[0] // 4
+    parts = [
+        swap_chips(partial[offset * count : (offset + 1) * count], offset) for offset in (3, 2, 1)
+    ]
+    return [partial[:count]] + parts
+
+
 def sum_rows(partial):
-    count = partial.shape[0] // 4
-    low = partial.astype(BF)
-    total = partial[:count]
-    for offset in (1, 2, 3):
-        total = total + swap_chips(low[offset * count : (offset + 1) * count], offset).astype(F32)
-    return total
+    return sum(part.astype(F32) for part in spread_rows(partial))
 
 
 def xor_route(size, offset):
@@ -106,8 +102,8 @@
     return total
 
 
-def sum_everywhere(values):
-    for axis in ("dp", "row", "section", "core"):
+def sum_over(values, axes):
+    for axis in axes:
         size = lax.axis_size(axis)
         step = 1
         while step < size:
@@ -128,10 +124,13 @@
     return (jnp.where(section == 0, keep, given), jnp.where(section == 0, given, keep), later)
 
 
-def return_shares(first, second, section, core):
+def return_over_section(first, second, section):
     keep = jnp.where(section == 0, first, second)
     give = jnp.where(section == 0, second, first)
-    given = lax.ppermute(give, "section", [(0, 1), (1, 0)])
+    return (keep, lax.ppermute(give, "section", [(0, 1), (1, 0)]))
+
+
+def return_over_core(keep, given, section, core):
     mine = jnp.where(core == section, keep, given)
     other = swap_cores(jnp.where(core == section, given, keep))
     top = jnp.where(core == 0, mine, other)
@@ -174,14 +173,101 @@
     return normalize(values)[0] * (1.0 + scale) + shift
 
 
-def modulate_back(grad, values, scale):
-    unit, inverse = normalize(values)
-    shift_grad = jnp.sum(grad, axis=0)
-    scale_grad = jnp.sum(grad * unit, axis=0)
-    inner = grad * (1.0 + scale)
+def modulate_back_kernel(
+    own, first, second, third, values_ref, residual, branch, scale, gate, grad_out, low_out, sums_out
+):
+    grad = own[...].astype(F32) + first[...].astype(F32)
+    grad = grad + second[...].astype(F32) + third[...].astype(F32)
+    unit, inverse = normalize(values_ref[...])
+    inner = grad * (1.0 + scale[...])
     mean_one = jnp.mean(inner, axis=-1, keepdims=True)
     mean_two = jnp.mean(inner * unit, axis=-1, keepdims=True)
-    return ((inner - mean_one - unit * mean_two) * inverse, shift_grad, scale_grad)
+    result = (inner - mean_one - unit * mean_two) * inverse + residual[...]
+    grad_out[...] = result
+    low_out[...] = (result * gate[...]).astype(BF)
+    sums_out[0:1, :] = jnp.sum(grad, axis=0, keepdims=True)
+    sums_out[1:2, :] = jnp.sum(grad * unit, axis=0, keepdims=True)
+    sums_out[2:3, :] = jnp.sum(result * branch[...], axis=0, keepdims=True)
+
+
+def modulate_back(parts, values, residual, branch, scale, gate):
+    rows, width = values.shape
+    whole = pl.BlockSpec(memory_space=pltpu.VMEM)
+    return pl.pallas_call(
+        modulate_back_kernel,
+        out_shape=(
+            jax.ShapeDtypeStruct((rows, width), F32),
+            jax.ShapeDtypeStruct((rows, width), BF),
+            jax.ShapeDtypeStruct((8, width), F32),
+        ),
+        in_specs=[whole] * 9,
+        out_specs=(whole, whole, whole),
+        compiler_params=pltpu.CompilerParams(vmem_limit_bytes=16 * 2**20),
+        cost_estimate=pl.CostEstimate(
+            flops=30 * rows * width, bytes_accessed=26 * rows * width, transcendentals=rows
+        ),
+    )(*parts, values, residual, branch, scale, gate)
+
+
+def feed_both_kernel(normed, up_ref, down_ref, down_in, act_out, grad_out, part_out, total):
+    step = pl.program_id(0)
+    up_value = jnp.dot(normed[...], up_ref[...], preferred_element_type=F32)
+    inner = math.sqrt(2.0 / math.pi) * (up_value + 0.044715 * up_value * up_value * up_value)
+    bend = jnp.tanh(inner)
+    act_out[...] = (0.5 * up_value * (1.0 + bend)).astype(BF)
+    slope = math.sqrt(2.0 / math.pi) * (1.0 + 3 * 0.044715 * up_value * up_value)
+    slope = 0.5 * (1.0 + bend) + 0.5 * up_value * (1.0 - bend * bend) * slope
+    act_grad = jnp.dot(down_in[...], down_ref[...], preferred_element_type=F32)
+    up_grad = (slope * act_grad).astype(BF)
+    grad_out[...] = up_grad
+    part = mm_nt(up_grad, up_ref[...])
+
+    @pl.when(step == 0)
+    def _():
+        total[...] = part
+
+    @pl.when(step > 0)
+    def _():
+        total[...] += part
+
+    @pl.when(step == pl.num_programs(0) - 1)
+    def _():
+        part_out[...] = total[...].astype(BF)
+
+
+def feed_both(normed, feed, down_in):
+    rows, width = normed.shape
+    units = feed.shape[1] // 2
+    tile = units // 3
+    return pl.pallas_call(
+        feed_both_kernel,
+        grid=(3,),
+        out_shape=(
+            jax.ShapeDtypeStruct((rows, units), BF),
+            jax.ShapeDtypeStruct((rows, units), BF),
+            jax.ShapeDtypeStruct((rows, width), BF),
+        ),
+        in_specs=[
+            pl.BlockSpec((rows, width), lambda j: (0, 0)),
+            pl.BlockSpec((width, tile), lambda j: (0, j)),
+            pl.BlockSpec((width, tile), lambda j: (0, j + 3)),
+            pl.BlockSpec((rows, width), lambda j: (0, 0)),
+        ],
+        out_specs=(
+            pl.BlockSpec((rows, tile), lambda j: (0, j)),
+            pl.BlockSpec((rows, tile), lambda j: (0, j)),
+            pl.BlockSpec((rows, width), lambda j: (0, 0)),
+        ),
+        scratch_shapes=[pltpu.VMEM((rows, width), F32)],
+        compiler_params=pltpu.CompilerParams(
+            dimension_semantics=("arbitrary",), vmem_limit_bytes=32 * 2**20
+        ),
+        cost_estimate=pl.CostEstimate(
+            flops=6 * rows * width * units,
+            bytes_accessed=4 * width * units + 10 * rows * width,
+            transcendentals=rows * units,
+        ),
+    )(normed, feed, feed, down_in)
 
 
 def gelu_tanh(values):
@@ -239,59 +325,37 @@
     normed = modulate(inputs, shift_a, scale_a).astype(BF)
     stacked = mm(normed, w_attn[:, : 3 * columns], BF)
     attended, log_total = attend(stacked, live)
-    branch_a = sum_rows(mm_nt(attended, w_attn[:, 3 * columns :]))
+    branch_a = sum_rows(mm_nt(attended, w_attn[:, 3 * columns :], BF))
     hidden = inputs[:own_count] + gate_a * branch_a
     normed_b = gather_rows(modulate(hidden, shift_b, scale_b).astype(BF))
-    return (normed, stacked, attended, log_total, branch_a, hidden, normed_b)
-
-
-def block_back_feed(grad_all, mod, saved, w_up, w_down, up_value, activated, split, core, earlier):
+    padded = jnp.pad(attended, ((0, 0), (3 * columns, 0)))
+    normed_b, padded = tie(normed_b, padded)
+    return (normed, stacked, padded, log_total, branch_a, hidden, normed_b)
+
+
+def block_back_feed(up_grad, partial, down_in, activated, grad_own, mod, saved, core):
     hidden, normed_b, branch_a = saved
-    own_count = hidden.shape[0]
-    gate_a, scale_b, gate_b = (mod[i][None] for i in (2, 4, 5))
-    grad_own = grad_all[:own_count]
-    down_in = (gate_b * grad_all).astype(BF)
-    if split:
-        grad_down = mm_tn(down_in, activated, BF)
-        down_in, grad_down = tie(down_in, grad_down)
-        grad_down = sum_cores(core, grad_down)
-    act_grad = mm(down_in, w_down)
-    up_grad = jax.vjp(gelu_tanh, up_value)[1](act_grad)[0].astype(BF)
-    sums = []
-    if split:
-        up_grad, grad_down = tie(up_grad, grad_down)
-        sums.append(sum_planes(grad_down))
-        earlier = sums
-    partial, up_grad, down_in = tie(mm_nt(up_grad, w_up), up_grad, down_in)
-    grads = [mm_tn(normed_b, up_grad, BF)]
-    if not split:
-        grads.append(mm_tn(down_in, activated, BF))
-    normed_grad, grad_up = tie(sum_rows(partial), sum_cores(core, *grads))
-    up_sum = sum_planes(grad_up)
-    normed_grad, *earlier = tie(normed_grad, *earlier)
-    hidden_grad, shift_b_grad, scale_b_grad = modulate_back(normed_grad, hidden, scale_b)
-    hidden_grad = hidden_grad + grad_own
-    gate_a_grad = jnp.sum(hidden_grad * branch_a, axis=0)
-    output_in = gather_rows((gate_a * hidden_grad).astype(BF))
-    mods = (gate_a_grad, shift_b_grad, scale_b_grad)
-    return (hidden_grad, output_in, up_sum, mods, earlier)
-
-
-def block_back_attention(output_in, hidden_grad, inputs_own, mod, live, saved, w_attn, core, earlier):
-    normed, stacked, attended, log_total = saved
+    partial, up_grad, down_in, activated = tie(partial, up_grad, down_in, activated)
+    grad_down = mm_tn(down_in, activated, BF)
+    grad_up = mm_tn(normed_b, up_grad, BF)
+    parts, grads = tie(spread_rows(partial), sum_cores(core, grad_up, grad_down))
+    feed_sum = sum_planes(grads)
+    return modulate_back(parts, hidden, grad_own, branch_a, mod[4][None], mod[2][None]), feed_sum
+
+
+def block_back_attention(output_in, hidden_grad, inputs_own, mod, live, saved, w_attn, core):
+    normed, stacked, padded, log_total = saved
     columns = w_attn.shape[1] // 4
     attended_grad = mm(output_in, w_attn[:, 3 * columns :], BF)
     stacked_grad = attend_back(attended_grad, stacked, live, log_total)
-    partial = mm_nt(stacked_grad, w_attn[:, : 3 * columns])
+    partial = mm_nt(stacked_grad, w_attn[:, : 3 * columns], BF)
     partial, stacked_grad, output_in = tie(partial, stacked_grad, output_in)
-    grad_attn = paired(normed, stacked_grad, output_in, attended)
-    normed_grad, grad_attn = tie(sum_rows(partial), sum_cores(core, grad_attn))
+    lefts = jnp.concatenate([normed, output_in], axis=0)
+    wide_grad = jnp.pad(stacked_grad, ((0, 0), (0, columns)))
+    grad_attn = mm_tn(lefts, jnp.concatenate([wide_grad, padded], axis=0), BF)
+    parts, grad_attn = tie(spread_rows(partial), sum_cores(core, grad_attn))
     attn_sum = sum_planes(grad_attn)
-    normed_grad, *earlier = tie(normed_grad, *earlier)
-    input_grad, shift_a_grad, scale_a_grad = modulate_back(normed_grad, inputs_own, mod[1][None])
-    input_grad = input_grad + hidden_grad
-    low_grad = gather_rows(input_grad.astype(BF))
-    return (input_grad, low_grad, attn_sum, shift_a_grad, scale_a_grad, earlier)
+    return parts, attn_sum
 
 
 def squared(values):
@@ -403,7 +467,7 @@
         return up_value, gelu_tanh(up_value).astype(BF)
 
     def feed_down(activated, feed):
-        return sum_rows(mm_nt(activated, feed[:, feed_width:]))
+        return sum_rows(mm_nt(activated, feed[:, feed_width:], BF))
 
     with jax.named_scope("encoder"):
         normed, stacked, attended, log_total, branch_a, hidden, normed_b = block_attention(
@@ -425,24 +489,33 @@
         normed, stacked, attended, log_total, branch_a, hidden, normed_b = block_attention(
             dec_in, dec_mod, all_live, dec_attn, quarter
         )
-        dec_up_value, dec_act = feed_up(normed_b, dec_feed)
+        dec_down_in = (dec_mod[5][None] * image_cot.astype(F32)).astype(BF)
+        dec_act, dec_up_grad, dec_partial = feed_both(normed_b, dec_feed, dec_down_in)
         dec_attn_saved = (normed, stacked, attended, log_total)
         dec_feed_saved = (hidden, normed_b, branch_a)
 
+    is_first = section == 0
+
+    def both_images(mine):
+        other = swap_cores(mine)
+        pair = jnp.where(core == 0, jnp.stack([mine, other]), jnp.stack([other, mine]))
+        return pair[None]
+
+    ones = jnp.ones((1, model_width), F32)
+
     with jax.named_scope("decoder_back"):
-        hidden_grad, output_in, dec_up_sum, mods, (dec_down_sum,) = block_back_feed(
-            image_cot.astype(F32),
+        (hidden_grad, output_in, mods_b), dec_feed_sum = block_back_feed(
+            dec_up_grad,
+            dec_partial,
+            dec_down_in,
+            dec_act,
+            image_cot[:quarter].astype(F32),
             dec_mod,
             dec_feed_saved,
-            dec_feed[:, :feed_width],
-            dec_feed[:, feed_width:],
-            dec_up_value,
-            dec_act,
-            True,
             core,
-            [],
-        )
-        dec_grad, dec_low, dec_attn_sum, shift_grad, scale_grad, _ = block_back_attention(
+        )
+        output_in = gather_rows(output_in)
+        parts, dec_attn_sum = block_back_attention(
             output_in,
             hidden_grad,
             dec_in[:quarter],
@@ -451,41 +524,47 @@
             dec_attn_saved,
             dec_attn,
             core,
-            [],
-        )
-        dec_low, dec_up_sum, dec_act = tie(dec_low, dec_up_sum, dec_act)
+        )
+        parts, dec_feed_sum = tie(parts, dec_feed_sum)
+        dec_grad, dec_low, mods_a = modulate_back(
+            parts,
+            dec_in[:quarter],
+            hidden_grad,
+            jnp.broadcast_to(uncovered[:quarter, None], hidden_grad.shape),
+            dec_mod[1][None],
+            ones,
+        )
+        mask_part = mods_a[2]
+        dec_mods = (mods_a[0:2], mods_b[2:3], mods_b[0:2])
+        dec_low = gather_rows(dec_low)
+
+    with jax.named_scope("encoder_back"):
+        enc_cot = mm(place, dec_low)
+        down_in = (enc_mod[5][None] * enc_cot).astype(BF)
+        act_grad = mm(down_in, enc_feed[:, feed_width:])
+        up_grad = jax.vjp(gelu_tanh, enc_up_value)[1](act_grad)[0].astype(BF)
+        partial = mm_nt(up_grad, enc_feed[:, :feed_width], BF)
+        partial, dec_act = tie(partial, dec_act)
+        (hidden_grad, output_in, mods_b), enc_feed_sum = block_back_feed(
+            up_grad,
+            partial,
+            down_in,
+            enc_act,
+            enc_cot[:quarter],
+            enc_mod,
+            enc_feed_saved,
+            core,
+        )
+        output_in, dec_attn_sum = tie(output_in, dec_attn_sum)
+        output_in = gather_rows(output_in)
         branch_b = feed_down(dec_act, dec_feed)
         dec_out = dec_feed_saved[0] + dec_mod[5][None] * branch_b
-        gate_grad = jnp.sum(image_cot[:quarter].astype(F32) * branch_b, axis=0)
-        dec_mods = (shift_grad, scale_grad) + mods + (gate_grad,)
-        mask_part = jnp.sum(uncovered[:quarter, None] * dec_grad, axis=0)
-
-    is_first = section == 0
-
-    def both_images(mine):
-        other = swap_cores(mine)
-        pair = jnp.where(core == 0, jnp.stack([mine, other]), jnp.stack([other, mine]))
-        return pair[None]
-
-    with jax.named_scope("encoder_back"):
-        enc_cot = mm(place, dec_low)
-        enc_gate_grad = jnp.sum(enc_cot[:quarter] * enc_branch_b, axis=0)
-        hidden_grad, output_in, enc_feed_sum, mods, (dec_attn_sum,) = block_back_feed(
-            enc_cot,
-            enc_mod,
-            enc_feed_saved,
-            enc_feed[:, :feed_width],
-            enc_feed[:, feed_width:],
-            enc_up_value,
-            enc_act,
-            False,
-            core,
-            [dec_attn_sum],
-        )
-        output_in, dec_out = tie(output_in, dec_out.astype(BF))
-        dec_out = gather_rows(dec_out)
+        gate_grad = jnp.sum(image_cot[:quarter].astype(F32) * branch_b, axis=0, keepdims=True)
+        dec_mods = dec_mods + (gate_grad,)
+        enc_gate_grad = jnp.sum(enc_cot[:quarter] * enc_branch_b, axis=0, keepdims=True)
+        dec_out = gather_rows(dec_out.astype(BF))
         layer_out = both_images(mm_tn(restore, jnp.where(is_first, sent, dec_out), BF))
-        enc_grad, enc_low, enc_attn_sum, shift_grad, scale_grad, (enc_feed_sum, layer_out) = block_back_attention(
+        parts, enc_attn_sum = block_back_attention(
             output_in,
             hidden_grad,
             enc_in[:quarter],
@@ -494,14 +573,18 @@
             enc_attn_saved,
             enc_attn,
             core,
-            [enc_feed_sum, layer_out],
-        )
-        enc_mods = (shift_grad, scale_grad) + mods + (enc_gate_grad,)
+        )
+        parts, enc_feed_sum, layer_out = tie(parts, enc_feed_sum, layer_out)
+        _, enc_low, mods_a = modulate_back(
+            parts, enc_in[:quarter], hidden_grad, hidden_grad, enc_mod[1][None], ones
+        )
+        enc_low = gather_rows(enc_low)
+        enc_mods = (mods_a[0:2], mods_b[2:3], mods_b[0:2], enc_gate_grad)
 
     with jax.named_scope("modulation_back"):
-        mod_parts = jnp.stack([jnp.concatenate(enc_mods), jnp.concatenate(dec_mods)])
+        mod_parts = jnp.concatenate(enc_mods + dec_mods, axis=0)
         mod_parts = lax.all_to_all(mod_parts.reshape(8, -1), PLANE, 0, 0, tiled=True)
-        mod_parts, enc_feed_sum = tie(mod_parts, enc_feed_sum)
+        mod_parts, enc_feed_sum, enc_low = tie(mod_parts, enc_feed_sum, enc_low)
         mod_grad = planes_gather(jnp.sum(mod_parts.reshape(4, 2, -1), axis=0))
 
     with jax.named_scope("outputs"):
@@ -509,10 +592,7 @@
         in_grads = both_images(mm_tn(arrange, jnp.where(is_first, enc_low, dec_low), BF))
 
     with jax.named_scope("returns"):
-        dec_feed_sum = jnp.concatenate([dec_up_sum, dec_down_sum], axis=1)
-        feed_grad = return_shares(enc_feed_sum, dec_feed_sum, section, core)
-        down_grad = turned(feed_grad[:, feed_width:])
-        up_grad = feed_grad[:, :feed_width]
+        keep, given = return_over_section(enc_feed_sum, dec_feed_sum, section)
 
     with jax.named_scope("modulation_back"):
         grad_adaln = lax.dot_general(
@@ -521,18 +601,26 @@
 
     with jax.named_scope("norm"):
         square = jnp.sum(grad_adaln * grad_adaln)
-        for part in (dec_attn_sum, up_grad, down_grad):
+        for part in (dec_attn_sum, dec_feed_sum, enc_feed_sum):
             square = square + squared(part)
-        square, grad_adaln, up_grad, down_grad, dec_attn_sum, enc_attn_sum = tie(
-            square, grad_adaln, up_grad, down_grad, dec_attn_sum, enc_attn_sum
-        )
+        square, grad_adaln, keep, given, in_grads, dec_attn_sum, enc_attn_sum = tie(
+            square, grad_adaln, keep, given, in_grads, dec_attn_sum, enc_attn_sum
+        )
+        feed_grad = return_over_core(keep, given, section, core)
+        down_grad = turned(feed_grad[:, feed_width:])
+        up_grad = feed_grad[:, :feed_width]
         square = square + squared(enc_attn_sum)
         totals = jnp.concatenate([mask_part, jnp.full((128,), square / 128.0, F32)])
-        totals = sum_everywhere(totals.reshape(1, -1))[0]
-        attn_grad = return_shares(enc_attn_sum, dec_attn_sum, section, core)
+        totals = sum_over(totals.reshape(1, -1), ("dp",))
+        keep, given = return_over_section(enc_attn_sum, dec_attn_sum, section)
+        totals, keep, given = tie(totals, keep, given)
+        totals = sum_over(totals, ("row", "section", "core"))[0]
+        attn_grad = return_over_core(keep, given, section, core)
         heads_grad = jnp.stack([attn_grad[:, i * columns : (i + 1) * columns] for i in range(3)])
         output_grad = turned(attn_grad[:, 3 * columns :])
-        totals, heads_grad, output_grad = tie(totals, heads_grad, output_grad)
+        totals, heads_grad, output_grad, up_grad, down_grad = tie(
+            totals, heads_grad, output_grad, up_grad, down_grad
+        )
         mask_total = totals[:model_width]
         grad_norm = jnp.sqrt(jnp.sum(totals[model_width:]) + jnp.sum(mask_total * mask_total))
         factor = jnp.minimum(1.0, CLIP_NORM / (grad_norm + NORM_EPS))

time: 481 us -> 459 us (0.954)
  waiting for transfers between devices: 177 us -> 203 us
  other arithmetic: 72.1 us -> 48.5 us
  matrix products: 68.4 us -> 50.5 us
  local copies, waits for them, and re-layouts: 33.9 us -> 20 us
  Pallas kernels: 0 us -> 7.98 us
    dot_general x31 -> x28, matrix products: 60.9 us -> 43.7 us  [dot(): lax.dot_general(left, right, (dims, ((), ())), preferred_element_type=F32)]
    ppermute x48, waiting for transfers between devices: 67.1 us -> 83.3 us  [swap_chips(): return lax.ppermute(block, CHIPS, chip_route(offset))]
    unnamed x273 -> x181, local copies, waits for them, and re-layouts: 21.7 us -> 10.2 us
    ppermute x7, waiting for transfers between devices: 19.8 us -> 10.5 us  [the longest x5 8.23 us: sum_over(): values = values + lax.ppermute(values, axis, xor_route(size, step))]
    reduce_sum x8 -> x2, other arithmetic: 10.2 us -> 1.16 us  [the longest x1 1.02 us: per_device(): jnp.sum(enc_cot[:quarter] * enc_branch_b, axis=0, keepdims=True)]
    pallas_call x0 -> x5, Pallas kernels: none -> 7.98 us  [the longest x1 4.97 us: feed_both(): pl.pallas_call(feed_both_kernel, grid=(3,), out_shape=(jax.ShapeDtypeStru...]
    reduce_scatter x5 -> x4, waiting for transfers between devices: 18.9 us -> 26.4 us  [sum_planes(): summed = lax.psum_scatter(grad, 'dp', scatter_dimension=0, tiled=True)]
    all_gather x3, waiting for transfers between devices: 36.3 us -> 43.8 us  [gather_weight(): return lax.all_gather(half, ROWS_BY, axis=0, tiled=True)]
  transfers between devices with their start and end apart: 87 -> 86, of which waited for: 45 -> 54; matrix products, arithmetic and copies ran while one was open for 26% -> 18% of each run, Pallas kernels for 0% -> 1%
where the time goes in v3:
time: 459 us; the launch traced here: 452 us
  waiting for transfers between devices  203 us (44%)
  starting transfers between devices  90.4 us (20%)
  matrix products  50.5 us (11%)
  other arithmetic  48.5 us (11%)
  between operations  22.5 us (5%)
  local copies, waits for them, and re-layouts  20 us (4%)
  blocking collectives  9.19 us (2%)
  Pallas kernels  7.98 us (2%)
    ppermute x48, waiting for transfers between devices, swap_chips(): return lax.ppermute(block, CHIPS, chip_route(offset))  83.3 us
    ppermute x48, starting transfers between devices, swap_chips(): return lax.ppermute(block, CHIPS, chip_route(offset))  56.7 us
    all_gather x3, waiting for transfers between devices, gather_weight(): return lax.all_gather(half, ROWS_BY, axis=0, tiled=True)  43.8 us
    dot_general x28, matrix products, dot(): lax.dot_general(left, right, (dims, ((), ())), preferred_element_type=F32)  43.7 us
    reduce_scatter x4, waiting for transfers between devices, sum_planes(): summed = lax.psum_scatter(grad, 'dp', scatter_dimension=0, tiled=True)  26.4 us
    ppermute x2, waiting for transfers between devices, send_shares(): given = lax.ppermute(give, 'section', [(0, 1), (1, 0)])  22.2 us
    sub x6, other arithmetic, adam_update(): weight_out = weight_in - LEARN_RATE * (ratio + WEIGHT_DECAY * weight_in)  15.5 us
    unnamed x181, local copies, waits for them, and re-layouts  10.2 us
  transfers between devices with their start and end apart: 86, of which 54 were waited for; matrix products, arithmetic and copies ran while one was open for 18% of the time, Pallas kernels for 1%

profile of v3, /device:TPU:0, one launch (start us, length us, event | category | flops | bytes accessed | tf_op | source)
XLA Modules:
  0.0 451.9 jit_solution(12599913145026598816)
XLA Ops:
  15.6 2.9 collective-permute-start.7
  19.6 7.0 %collective-permute-done.7 = bf16[144,1152]{1,0:T(8,128)(2,1)S(1)} collective-permute-done((bf16[144,1152]{1,0:T(8,128)(2,1)S(1)}, bf16[144,1152]{1,0:T(8,128)(2,1)S(1)}, u32[]{:S(2)}, u32[]{:S(2)}) %collective-permute-start.7) | collective-permute-done | bytes 331808 | tf_op jit(solution)/shard_map/weights_in/ppermute | solution.py:123
  33.2 15.2 %collective-permute-done.15 = bf16[144,2304]{1,0:T(8,128)(2,1)S(1)} collective-permute-done((bf16[144,2304]{1,0:T(8,128)(2,1)S(1)}, bf16[144,2304]{1,0:T(8,128)(2,1)S(1)}, u32[]{:S(2)}, u32[]{:S(2)}) %collective-permute-start.15) | collective-permute-done | bytes 663584 | tf_op jit(solution)/shard_map/weights_in/ppermute | solution.py:123
  49.9 3.9 collective-permute-start.2
  60.2 3.8 collective-permute-start.5
  66.1 3.9 collective-permute-done.4
  70.1 9.2 %all-gather.1 = f32[8,2,1728]{2,1,0:T(2,128)S(1)} all-gather(f32[1,2,1728]{2,1,0:T(2,128)S(1)} %fusion.150), channel_id=2, replica_groups=mesh['section'=2,'row'=2,'core'=2,'dp'=4] {'section','row','core'}, dimensions={0}, use_global_device_ids=true | all-gather | bytes 124416 | tf_op jit(solution)/shard_map/modulation/all_gather | solution.py:438
  79.9 7.2 %all-gather.6.cloned.1.call-done = bf16[1152,2304]{1,0:T(8,128)(2,1)} async-done(((bf16[144,2304]{1,0:T(8,128)(2,1)}), bf16[1152,2304]{1,0:T(8,128)(2,1)}) %all-gather.6.cloned.1.call-update) | async-done | bytes 5308432 | tf_op jit(solution)/shard_map/weights_in/all_gather | solution.py:146
  96.6 3.2 collective-permute-done.10
  99.8 3.7 collective-permute-done.9
  108.5 3.2 collective-permute-done.13
  114.0 30.6 %all-gather.8.cloned.1.call-done = bf16[1152,2304]{1,0:T(8,128)(2,1)} async-done(((bf16[144,2304]{1,0:T(8,128)(2,1)}), bf16[1152,2304]{1,0:T(8,128)(2,1)}) %all-gather.8.cloned.1.call-update) | async-done | bytes 5308432 | tf_op jit(solution)/shard_map/weights_in/all_gather | solution.py:146
  144.6 4.0 multiply_convert_fusion.2
  153.4 3.1 collective-permute-done.18
  156.5 3.7 collective-permute-done.17
  163.9 4.0 collective-permute-done.21
  183.1 3.9 collective-permute-done.23
  196.2 6.0 %all-gather.10.cloned.1.call-done.up_ref.down_ref = bf16[1152,2304]{1,0:T(8,128)(2,1)} async-done(((bf16[144,2304]{1,0:T(8,128)(2,1)}), bf16[1152,2304]{1,0:T(8,128)(2,1)}) %all-gather.10.cloned.1.call-update) | async-done | bytes 5308432 | tf_op jit(solution)/shard_map/encoder/all_gather | solution.py:146
  204.7 5.0 %decoder.1 = (bf16[256,1152]{1,0:T(8,128)(2,1)S(1)}, bf16[256,1152]{1,0:T(8,128)(2,1)S(1)}, bf16[256,1152]{1,0:T(8,128)(2,1)S(1)}) custom-call(bf16[256,1152]{1,0:T(8,128)(2,1)S(1)} %pad_maximum_fusion.9.normed, bf16[1152,2304]{1,0:T(8,128)(2,1)S(1)} %copy-done.2, bf16[1152,2304]{1,0:T(8,128)(2,1)S(1)} %copy-done.2, ...), custom_call_target="tpu_custom_call" | custom-call | flops 2038431744 | bytes 8257536 | tf_op jit(solution)/shard_map/decoder/pallas_call | solution.py:242
  226.9 2.9 collective-permute-done.33
  229.9 3.6 collective-permute-done.34
  252.5 21.2 %reduce-scatter.5.cloned.1.call-done = bf16[1,144,2304]{2,1,0:T(8,128)(2,1)} async-done(((bf16[4,144,2304]{2,1,0:T(8,128)(2,1)}), bf16[1,144,2304]{2,1,0:T(8,128)(2,1)}) %reduce-scatter.5.cloned.1.call-update) | async-done | bytes 663568 | tf_op jit(solution)/shard_map/decoder_back/reduce_scatter | solution.py:161
  281.2 3.6 collective-permute-done.41
  286.2 3.4 fusion.46
  313.4 4.8 %collective-permute-done.49 = bf16[64,1152]{1,0:T(8,128)(2,1)S(1)} collective-permute-done((bf16[64,1152]{1,0:T(8,128)(2,1)S(1)}, bf16[64,1152]{1,0:T(8,128)(2,1)S(1)}, u32[]{:S(2)}, u32[]{:S(2)}) %collective-permute-start.49) | collective-permute-done | bytes 147488 | tf_op jit(solution)/shard_map/encoder_back/ppermute | solution.py:60
  330.2 3.2 collective-permute-done.57
  340.7 4.2 collective-permute-done.60
  367.8 3.9 all-to-all-start
  371.8 4.8 %all-to-all-done = f32[8,1,1728]{2,1,0:T(1,128)S(1)} async-done(((f32[8,1,1728]{2,1,0:T(1,128)}), f32[8,1,1728]{2,1,0:T(1,128)S(1)}, u32[]{:S(2)}, u32[]{:S(2)}) %all-to-all-start) | async-done | bytes 55328 | tf_op jit(solution)/shard_map/modulation_back/all_to_all | solution.py:586
  388.4 3.0 multiply_reduce_fusion
  424.7 4.5 %multiply_subtract_fusion.3 = (f32[1,3,288,288]{3,2,1,0:T(8,128)}, f32[1,3,288,288]{3,2,1,0:T(8,128)}, f32[1,3,288,288]{3,2,1,0:T(8,128)}) fusion(f32[1,3,288,288]{3,2,1,0:T(8,128)S(1)} %copy-done.13, f32[]{:T(128)S(6)} %min.3, bf16[3,288,288]{2,1,0:T(8,128)(2,1)S(1)} %pad_maximum_fusion.6, f32[1,3,288,288]{3,2,1,0:T(8,128)} %param.33, ...), kind=kLoop, calls=%fused_computation.79 | loop fusion | flops 4230144 | bytes 6469636 | tf_op jit(solution)/shard_map/update/sub | solution.py:375
  440.0 3.7 multiply_subtract_fusion
  (519 shorter events, 239.5 us)
Async XLA Ops:
  7.2 79.9 %all-gather.6.cloned.1.call-start = ((), (), s32[]{:S(2)}) async-start(), calls=%async_computation.5 | async-start | bytes 5971968 | tf_op jit(solution)/shard_map/weights_in/all_gather | solution.py:146
  15.6 11.0 %collective-permute-start.7 = (bf16[144,1152]{1,0:T(8,128)(2,1)S(1)}, bf16[144,1152]{1,0:T(8,128)(2,1)S(1)}, u32[]{:S(2)}, u32[]{:S(2)}) collective-permute-start(bf16[144,1152]{1,0:T(8,128)(2,1)S(1)} %broadcast_select_fusion.19), channel_id=1, source_target_pairs={{0,16},{16,0},{1,17},{17,1},{2,18},{18,2},{3,19},{19,3},{4,20},{20... | collective-permute-start | bytes 995336 | tf_op jit(solution)/shard_map/weights_in/ppermute | solution.py:123
  27.7 116.9 %all-gather.8.cloned.1.call-start = ((), (), s32[]{:S(2)}) async-start(), calls=%async_computation.6 | async-start | bytes 5971968 | tf_op jit(solution)/shard_map/weights_in/all_gather | solution.py:146
  31.4 17.0 %collective-permute-start.15 = (bf16[144,2304]{1,0:T(8,128)(2,1)S(1)}, bf16[144,2304]{1,0:T(8,128)(2,1)S(1)}, u32[]{:S(2)}, u32[]{:S(2)}) collective-permute-start(bf16[144,2304]{1,0:T(8,128)(2,1)S(1)} %broadcast_select_fusion.5), channel_id=1, source_target_pairs={{0,16},{16,0},{1,17},{17,1},{2,18},{18,2},{3,19},{19,3},{4,20},{20... | collective-permute-start | bytes 1990664 | tf_op jit(solution)/shard_map/weights_in/ppermute | solution.py:123
  49.8 152.4 %all-gather.10.cloned.1.call-start = ((), (), s32[]{:S(2)}) async-start(), calls=%async_computation.7 | async-start | bytes 5971968 | tf_op jit(solution)/shard_map/encoder/all_gather | solution.py:146
  49.9 8.4 %collective-permute-start.2 = (s32[2,2]{0,1:T(2,128)S(1)}, s32[2,2]{0,1:T(2,128)S(1)}, u32[]{:S(2)}, u32[]{:S(2)}) collective-permute-start(s32[2,2]{0,1:T(2,128)S(1)} %pad_add_fusion.1), channel_id=1, source_target_pairs={{0,3},{1,2},{2,1},{3,0},{4,7},{5,6},{6,5},{7,4},{8,11},{9,10},{10,... | collective-permute-start | bytes 56 | tf_op jit(solution)/shard_map/modulation/ppermute | solution.py:90
  94.6 8.9 %collective-permute-start.9 = (bf16[64,1152]{1,0:T(8,128)(2,1)S(1)}, bf16[64,1152]{1,0:T(8,128)(2,1)S(1)}, u32[]{:S(2)}, u32[]{:S(2)}) collective-permute-start(bf16[64,1152]{1,0:T(8,128)(2,1)S(1)} %get-tuple-element.299), channel_id=1, source_target_pairs={{0,8},{8,0},{16,24},{24,16},{1,9},{9,1},{17,25},{25,17},{2,10},{10... | collective-permute-start | bytes 442376 | tf_op jit(solution)/shard_map/encoder/ppermute | solution.py:60
  113.3 160.4 %reduce-scatter.5.cloned.1.call-start = ((), (), s32[]{:S(2)}) async-start(), calls=%async_computation.8 | async-start | bytes 3317760 | tf_op jit(solution)/shard_map/decoder_back/reduce_scatter | solution.py:161
  151.3 8.9 %collective-permute-start.17 = (bf16[64,1152]{1,0:T(8,128)(2,1)S(1)}, bf16[64,1152]{1,0:T(8,128)(2,1)S(1)}, u32[]{:S(2)}, u32[]{:S(2)}) collective-permute-start(bf16[64,1152]{1,0:T(8,128)(2,1)S(1)} %get-tuple-element.296), channel_id=1, source_target_pairs={{0,8},{8,0},{16,24},{24,16},{1,9},{9,1},{17,25},{25,17},{2,10},{10... | collective-permute-start | bytes 442376 | tf_op jit(solution)/shard_map/encoder/ppermute | solution.py:60
  178.4 8.5 %collective-permute-start.23 = (bf16[64,1152]{1,0:T(8,128)(2,1)S(1)}, bf16[64,1152]{1,0:T(8,128)(2,1)S(1)}, u32[]{:S(2)}, u32[]{:S(2)}) collective-permute-start(bf16[64,1152]{1,0:T(8,128)(2,1)S(1)} %get-tuple-element.293), channel_id=1, source_target_pairs={{0,8},{8,0},{16,24},{24,16},{1,9},{9,1},{17,25},{25,17},{2,10},{10... | collective-permute-start | bytes 442376 | tf_op jit(solution)/shard_map/decoder/ppermute | solution.py:60
  222.8 85.0 %reduce-scatter.7.cloned.1.call-start = ((), (), s32[]{:S(2)}) async-start(), calls=%async_computation.9 | async-start | bytes 1658880 | tf_op jit(solution)/shard_map/decoder_back/reduce_scatter | solution.py:161
  224.9 8.6 %collective-permute-start.34 = (bf16[64,1152]{1,0:T(8,128)(2,1)S(1)}, bf16[64,1152]{1,0:T(8,128)(2,1)S(1)}, u32[]{:S(2)}, u32[]{:S(2)}) collective-permute-start(bf16[64,1152]{1,0:T(8,128)(2,1)S(1)} %get-tuple-element.132), channel_id=1, source_target_pairs={{0,8},{8,0},{16,24},{24,16},{1,9},{9,1},{17,25},{25,17},{2,10},{10... | collective-permute-start | bytes 442376 | tf_op jit(solution)/shard_map/decoder_back/ppermute | solution.py:60
  243.3 8.9 %collective-permute-start.37 = (bf16[64,1152]{1,0:T(8,128)(2,1)S(1)}, bf16[64,1152]{1,0:T(8,128)(2,1)S(1)}, u32[]{:S(2)}, u32[]{:S(2)}) collective-permute-start(bf16[64,1152]{1,0:T(8,128)(2,1)S(1)} %get-tuple-element.284), channel_id=1, source_target_pairs={{0,8},{8,0},{16,24},{24,16},{1,9},{9,1},{17,25},{25,17},{2,10},{10... | collective-permute-start | bytes 442376 | tf_op jit(solution)/shard_map/decoder_back/ppermute | solution.py:60
  243.9 8.3 %collective-permute-start.38 = (bf16[64,1152]{1,0:T(8,128)(2,1)S(1)}, bf16[64,1152]{1,0:T(8,128)(2,1)S(1)}, u32[]{:S(2)}, u32[]{:S(2)}) collective-permute-start(bf16[64,1152]{1,0:T(8,128)(2,1)S(1)} %get-tuple-element.283), channel_id=1, source_target_pairs={{0,16},{8,24},{16,0},{24,8},{1,17},{9,25},{17,1},{25,9},{2,18},{10... | collective-permute-start | bytes 442376 | tf_op jit(solution)/shard_map/decoder_back/ppermute | solution.py:60
  252.2 109.2 %reduce-scatter.9.cloned.1.call-start = ((), (), s32[]{:S(2)}) async-start(), calls=%async_computation.10 | async-start | bytes 3317760 | tf_op jit(solution)/shard_map/encoder_back/reduce_scatter | solution.py:161
  276.4 8.3 %collective-permute-start.41 = (bf16[64,1152]{1,0:T(8,128)(2,1)S(1)}, bf16[64,1152]{1,0:T(8,128)(2,1)S(1)}, u32[]{:S(2)}, u32[]{:S(2)}) collective-permute-start(bf16[64,1152]{1,0:T(8,128)(2,1)S(1)} %get-tuple-element.147), channel_id=1, source_target_pairs={{0,8},{8,0},{16,24},{24,16},{1,9},{9,1},{17,25},{25,17},{2,10},{10... | collective-permute-start | bytes 442376 | tf_op jit(solution)/shard_map/decoder_back/ppermute | solution.py:60
  291.9 8.2 %collective-permute-start.47 = (bf16[4,144,1152]{2,1,0:T(8,128)(2,1)S(1)}, bf16[4,144,1152]{2,1,0:T(8,128)(2,1)S(1)}, u32[]{:S(2)}, u32[]{:S(2)}) collective-permute-start(bf16[4,144,1152]{2,1,0:T(8,128)(2,1)S(1)} %dynamic-slice_bitcast_fusion.1), channel_id=1, source_target_pairs={{0,4},{4,0},{1,5},{5,1},{2,6},{6,2},{3,7},{7,3},{8,12},{12,8},{9,1... | collective-permute-start | bytes 3981320 | tf_op jit(solution)/shard_map/encoder_back/ppermute | solution.py:64
  295.9 8.6 %collective-permute-start.44 = (bf16[64,1152]{1,0:T(8,128)(2,1)}, bf16[64,1152]{1,0:T(8,128)(2,1)S(1)}, u32[]{:S(2)}, u32[]{:S(2)}) collective-permute-start(bf16[64,1152]{1,0:T(8,128)(2,1)} %get-tuple-element.280), channel_id=1, source_target_pairs={{0,8},{8,0},{16,24},{24,16},{1,9},{9,1},{17,25},{25,17},{2,10},{10... | collective-permute-start | bytes 442376 | tf_op jit(solution)/shard_map/encoder_back/ppermute | solution.py:60
  309.3 87.5 %reduce-scatter.11.cloned.1.call-start = ((), (), s32[]{:S(2)}) async-start(), calls=%async_computation.11 | async-start | bytes 1658880 | tf_op jit(solution)/shard_map/encoder_back/reduce_scatter | solution.py:161
  309.8 8.4 %collective-permute-start.49 = (bf16[64,1152]{1,0:T(8,128)(2,1)S(1)}, bf16[64,1152]{1,0:T(8,128)(2,1)S(1)}, u32[]{:S(2)}, u32[]{:S(2)}) collective-permute-start(bf16[64,1152]{1,0:T(8,128)(2,1)S(1)} %get-tuple-element.159), channel_id=1, source_target_pairs={{0,8},{8,0},{16,24},{24,16},{1,9},{9,1},{17,25},{25,17},{2,10},{10... | collective-permute-start | bytes 442376 | tf_op jit(solution)/shard_map/encoder_back/ppermute | solution.py:60
  326.5 24.5 %collective-permute-start.54 = (bf16[4,144,1152]{2,1,0:T(8,128)(2,1)S(1)}, bf16[4,144,1152]{2,1,0:T(8,128)(2,1)S(1)}, u32[]{:S(2)}, u32[]{:S(2)}) collective-permute-start(bf16[4,144,1152]{2,1,0:T(8,128)(2,1)S(1)} %dynamic-slice_bitcast_fusion), channel_id=1, source_target_pairs={{0,4},{4,0},{1,5},{5,1},{2,6},{6,2},{3,7},{7,3},{8,12},{12,8},{9,1... | collective-permute-start | bytes 3981320 | tf_op jit(solution)/shard_map/encoder_back/ppermute | solution.py:64
  328.8 8.2 %collective-permute-start.55 = (bf16[64,1152]{1,0:T(8,128)(2,1)S(1)}, bf16[64,1152]{1,0:T(8,128)(2,1)S(1)}, u32[]{:S(2)}, u32[]{:S(2)}) collective-permute-start(bf16[64,1152]{1,0:T(8,128)(2,1)S(1)} %get-tuple-element.272), channel_id=1, source_target_pairs={{0,24},{8,16},{16,8},{24,0},{1,25},{9,17},{17,9},{25,1},{2,26},{10... | collective-permute-start | bytes 442376 | tf_op jit(solution)/shard_map/encoder_back/ppermute | solution.py:60
  347.2 10.6 %collective-permute-start.61 = (bf16[256,1152]{1,0:T(8,128)(2,1)S(1)}, bf16[256,1152]{1,0:T(8,128)(2,1)S(1)}, u32[]{:S(2)}, u32[]{:S(2)}) collective-permute-start(bf16[256,1152]{1,0:T(8,128)(2,1)S(1)} %convolution_convert_fusion.12), channel_id=1, source_target_pairs={{0,4},{4,0},{1,5},{5,1},{2,6},{6,2},{3,7},{7,3},{8,12},{12,8},{9,1... | collective-permute-start | bytes 1769480 | tf_op jit(solution)/shard_map/encoder_back/ppermute | solution.py:64
  349.1 8.7 %collective-permute-start.52 = (bf16[64,1152]{1,0:T(8,128)(2,1)S(1)}, bf16[64,1152]{1,0:T(8,128)(2,1)S(1)}, u32[]{:S(2)}, u32[]{:S(2)}) collective-permute-start(bf16[64,1152]{1,0:T(8,128)(2,1)S(1)} %get-tuple-element.276), channel_id=1, source_target_pairs={{0,8},{8,0},{16,24},{24,16},{1,9},{9,1},{17,25},{25,17},{2,10},{10... | collective-permute-start | bytes 442376 | tf_op jit(solution)/shard_map/encoder_back/ppermute | solution.py:60
  349.6 8.2 %collective-permute-start.53 = (bf16[64,1152]{1,0:T(8,128)(2,1)S(1)}, bf16[64,1152]{1,0:T(8,128)(2,1)S(1)}, u32[]{:S(2)}, u32[]{:S(2)}) collective-permute-start(bf16[64,1152]{1,0:T(8,128)(2,1)S(1)} %get-tuple-element.275), channel_id=1, source_target_pairs={{0,16},{8,24},{16,0},{24,8},{1,17},{9,25},{17,1},{25,9},{2,18},{10... | collective-permute-start | bytes 442376 | tf_op jit(solution)/shard_map/encoder_back/ppermute | solution.py:60
  362.5 14.0 %collective-permute-start.64 = (bf16[64,1152]{1,0:T(8,128)(2,1)S(1)}, bf16[64,1152]{1,0:T(8,128)(2,1)S(1)}, u32[]{:S(2)}, u32[]{:S(2)}) collective-permute-start(bf16[64,1152]{1,0:T(8,128)(2,1)S(1)} %get-tuple-element.181), channel_id=1, source_target_pairs={{0,24},{8,16},{16,8},{24,0},{1,25},{9,17},{17,9},{25,1},{2,26},{10... | collective-permute-start | bytes 442376 | tf_op jit(solution)/shard_map/encoder_back/ppermute | solution.py:60
  364.9 11.6 %collective-permute-start.63 = (bf16[64,1152]{1,0:T(8,128)(2,1)S(1)}, bf16[64,1152]{1,0:T(8,128)(2,1)S(1)}, u32[]{:S(2)}, u32[]{:S(2)}) collective-permute-start(bf16[64,1152]{1,0:T(8,128)(2,1)S(1)} %get-tuple-element.181), channel_id=1, source_target_pairs={{0,8},{8,0},{16,24},{24,16},{1,9},{9,1},{17,25},{25,17},{2,10},{10... | collective-permute-start | bytes 442376 | tf_op jit(solution)/shard_map/encoder_back/ppermute | solution.py:60
  365.5 11.1 %collective-permute-start.62 = (bf16[64,1152]{1,0:T(8,128)(2,1)S(1)}, bf16[64,1152]{1,0:T(8,128)(2,1)S(1)}, u32[]{:S(2)}, u32[]{:S(2)}) collective-permute-start(bf16[64,1152]{1,0:T(8,128)(2,1)S(1)} %get-tuple-element.181), channel_id=1, source_target_pairs={{0,16},{8,24},{16,0},{24,8},{1,17},{9,25},{17,1},{25,9},{2,18},{10... | collective-permute-start | bytes 442376 | tf_op jit(solution)/shard_map/encoder_back/ppermute | solution.py:60
  367.8 8.7 %all-to-all-start = ((f32[8,1,1728]{2,1,0:T(1,128)}), f32[8,1,1728]{2,1,0:T(1,128)S(1)}, u32[]{:S(2)}, u32[]{:S(2)}) async-start(f32[8,1,1728]{2,1,0:T(1,128)} %all_to_all.11), calls=%async_computation.3 | async-start | bytes 114688 | tf_op jit(solution)/shard_map/modulation_back/all_to_all | solution.py:586
  378.0 16.0 %collective-permute-start.69 = (bf16[256,1152]{1,0:T(8,128)(2,1)}, bf16[256,1152]{1,0:T(8,128)(2,1)}, u32[]{:S(2)}, u32[]{:S(2)}) collective-permute-start(bf16[256,1152]{1,0:T(8,128)(2,1)} %convolution_convert_fusion.11), channel_id=1, source_target_pairs={{0,4},{4,0},{1,5},{5,1},{2,6},{6,2},{3,7},{7,3},{8,12},{12,8},{9,1... | collective-permute-start | bytes 1769480 | tf_op jit(solution)/shard_map/outputs/ppermute | solution.py:64
  379.0 17.8 %collective-permute-start.68 = (bf16[144,2304]{1,0:T(8,128)(2,1)}, bf16[144,2304]{1,0:T(8,128)(2,1)S(1)}, u32[]{:S(2)}, u32[]{:S(2)}) collective-permute-start(bf16[144,2304]{1,0:T(8,128)(2,1)} %get-tuple-element.249), channel_id=1, source_target_pairs={{0,16},{16,0},{1,17},{17,1},{2,18},{18,2},{3,19},{19,3},{4,20},{20... | collective-permute-start | bytes 1990664 | tf_op jit(solution)/shard_map/returns/ppermute | solution.py:130
  401.3 8.6 %collective-permute-start.72 = (bf16[144,1152]{1,0:T(8,128)(2,1)S(1)}, bf16[144,1152]{1,0:T(8,128)(2,1)S(1)}, u32[]{:S(2)}, u32[]{:S(2)}) collective-permute-start(bf16[144,1152]{1,0:T(8,128)(2,1)S(1)} %get-tuple-element.267), channel_id=1, source_target_pairs={{0,16},{16,0},{1,17},{17,1},{2,18},{18,2},{3,19},{19,3},{4,20},{20... | collective-permute-start | bytes 995336 | tf_op jit(solution)/shard_map/norm/ppermute | solution.py:130
  (140 other events, 1123.1 us)
Sparse Core Ops, SparseCore 0:
  27.8 59.2 all-gather.5
  89.3 55.2 all-gather.7
  146.8 55.3 all-gather.9
  223.0 50.6 reduce-scatter.4
  276.4 31.3 reduce-scatter.6
  310.0 51.4 reduce-scatter.8
  364.3 32.2 reduce-scatter.10

commit v4 on v3

--- a/solution.py
+++ b/solution.py
@@ -112,16 +112,43 @@
     return values
 
 
-def send_shares(pack, section, core, later=None):
+def send_shares(pack, section, core):
     half = pack.shape[0] // 2
     mine = lax.dynamic_slice_in_dim(pack, core * half, half, 0)
     other = swap_cores(lax.dynamic_slice_in_dim(pack, (1 - core) * half, half, 0))
     keep = jnp.where(core == section, mine, other)
     give = jnp.where(core == section, other, mine)
-    if later is not None:
-        give, later = tie(give, later)
-    given = lax.ppermute(give, "section", [(0, 1), (1, 0)])
-    return (jnp.where(section == 0, keep, given), jnp.where(section == 0, given, keep), later)
+    return keep, lax.ppermute(give, "section", [(0, 1), (1, 0)])
+
+
+def by_block(keep, given, section):
+    return (jnp.where(section == 0, keep, given), jnp.where(section == 0, given, keep))
+
+
+def assemble_kernel(order_ref, mine_ref, other_ref, out_ref):
+    count = mine_ref.shape[1]
+    for part in range(4):
+        for which, source in enumerate((mine_ref, other_ref)):
+            start = pl.multiple_of(order_ref[which * 4 + part] * count, count)
+            out_ref[pl.ds(start, count), :] = source[part]
+
+
+def assemble(parts, plane, core):
+    mine = jnp.stack(parts)
+    other = swap_cores(mine)
+    planes = jnp.stack([plane ^ offset for offset in range(4)]).astype(jnp.int32)
+    order = jnp.concatenate([planes * 2 + core, planes * 2 + 1 - core])
+    whole = pl.BlockSpec(memory_space=pltpu.VMEM)
+    return pl.pallas_call(
+        assemble_kernel,
+        out_shape=jax.ShapeDtypeStruct((8 * mine.shape[1], mine.shape[2]), mine.dtype),
+        in_specs=[pl.BlockSpec(memory_space=pltpu.SMEM), whole, whole],
+        out_specs=whole,
+        compiler_params=pltpu.CompilerParams(vmem_limit_bytes=24 * 2**20),
+        cost_estimate=pl.CostEstimate(
+            flops=0, bytes_accessed=8 * mine.size, transcendentals=0
+        ),
+    )(order, mine, other)
 
 
 def return_over_section(first, second, section):
@@ -333,12 +360,17 @@
     return (normed, stacked, padded, log_total, branch_a, hidden, normed_b)
 
 
-def block_back_feed(up_grad, partial, down_in, activated, grad_own, mod, saved, core):
+def block_back_feed(up_grad, partial, down_in, activated, grad_own, mod, saved, core, late):
     hidden, normed_b, branch_a = saved
     partial, up_grad, down_in, activated = tie(partial, up_grad, down_in, activated)
     grad_down = mm_tn(down_in, activated, BF)
     grad_up = mm_tn(normed_b, up_grad, BF)
-    parts, grads = tie(spread_rows(partial), sum_cores(core, grad_up, grad_down))
+    grads = sum_cores(core, grad_up, grad_down)
+    if late:
+        parts, grads = tie(spread_rows(partial), grads)
+    else:
+        partial, grads = tie(partial, grads)
+        parts = spread_rows(partial)
     feed_sum = sum_planes(grads)
     return modulate_back(parts, hidden, grad_own, branch_a, mod[4][None], mod[2][None]), feed_sum
 
@@ -416,14 +448,18 @@
         attn_pack = jnp.concatenate(
             [heads_weight[0, 0], heads_weight[0, 1], heads_weight[0, 2], output_weight[0].T], axis=1
         ).astype(BF)
-        *halves, feed_parts = send_shares(attn_pack, section, core, (up_weight[0], down_weight[0]))
-        attn_half = jnp.concatenate(halves, axis=1)
-        feed_pack = jnp.concatenate([feed_parts[0], feed_parts[1].T], axis=1).astype(BF)
-        feed_pack, attn_half = tie(feed_pack, attn_half)
-        attn_all = gather_weight(attn_half)
-        attn_width = attn_pack.shape[1]
-        enc_attn, dec_attn = attn_all[:, :attn_width], attn_all[:, attn_width:]
-        enc_feed_half, dec_feed_half, _ = send_shares(feed_pack, section, core)
+        keep, given = send_shares(attn_pack, section, core)
+        if lax.axis_size("dp") == 4:
+            parts = [keep] + [lax.ppermute(keep, "dp", xor_route(4, m)) for m in (1, 2, 3)]
+            given, *parts = tie(given, *parts)
+            given_all = gather_weight(given)
+            keep_all = assemble(parts, plane, core)
+        else:
+            given_all, keep_all = gather_weight(given), gather_weight(keep)
+        enc_attn, dec_attn = by_block(keep_all, given_all, section)
+        feed_pack = jnp.concatenate([up_weight[0], down_weight[0].T], axis=1).astype(BF)
+        feed_pack, given = tie(feed_pack, given)
+        enc_feed_half, dec_feed_half = by_block(*send_shares(feed_pack, section, core), section)
         feed_width = feed_pack.shape[1] // 2
         enc_feed = gather_weight(enc_feed_half)
 
@@ -513,6 +549,7 @@
             dec_mod,
             dec_feed_saved,
             core,
+            False,
         )
         output_in = gather_rows(output_in)
         parts, dec_attn_sum = block_back_attention(
@@ -554,6 +591,7 @@
             enc_mod,
             enc_feed_saved,
             core,
+            True,
         )
         output_in, dec_attn_sum = tie(output_in, dec_attn_sum)
         output_in = gather_rows(output_in)

time: 459 us -> 453 us (0.987)
  waiting for transfers between devices: 203 us -> 183 us
  other arithmetic: 48.5 us -> 57.6 us
  local copies, waits for them, and re-layouts: 20 us -> 28.8 us
  matrix products: 50.5 us -> 42.4 us
    all_gather x3, waiting for transfers between devices: 43.8 us -> 10.9 us  [gather_weight(): return lax.all_gather(half, ROWS_BY, axis=0, tiled=True)]
    ppermute x2 -> x5, waiting for transfers between devices: 22.2 us -> 37.5 us  [the longest x3 26.3 us: per_device(): lax.ppermute(keep, 'dp', xor_route(4, m))]
    unnamed x181 -> x203, local copies, waits for them, and re-layouts: 10.2 us -> 18.9 us
    dot_general x28, matrix products: 43.7 us -> 35.7 us  [dot(): lax.dot_general(left, right, (dims, ((), ())), preferred_element_type=F32)]
    reduce_scatter x4, waiting for transfers between devices: 26.4 us -> 19.2 us  [sum_planes(): summed = lax.psum_scatter(grad, 'dp', scatter_dimension=0, tiled=True)]
    select_n x2 -> x3, other arithmetic: 1.57 us -> 7.57 us  [the longest x1 3.79 us: by_block(): jnp.where(section == 0, given, keep)]
  transfers between devices with their start and end apart: 86 -> 90, of which waited for: 54 -> 55; matrix products, arithmetic and copies ran while one was open for 18% -> 18% of each run, Pallas kernels for 1% -> 1%
where the time goes in v4:
time: 453 us; the launch traced here: 445 us
  waiting for transfers between devices  183 us (40%)
  starting transfers between devices  92.3 us (20%)
  other arithmetic  57.6 us (13%)
  matrix products  42.4 us (9%)
  local copies, waits for them, and re-layouts  28.8 us (6%)
  between operations  22.7 us (5%)
  blocking collectives  9.24 us (2%)
  Pallas kernels  8.87 us (2%)
    ppermute x48, waiting for transfers between devices, swap_chips(): return lax.ppermute(block, CHIPS, chip_route(offset))  85.1 us
    ppermute x48, starting transfers between devices, swap_chips(): return lax.ppermute(block, CHIPS, chip_route(offset))  56.7 us
    dot_general x28, matrix products, dot(): lax.dot_general(left, right, (dims, ((), ())), preferred_element_type=F32)  35.7 us
    ppermute x3, waiting for transfers between devices, per_device(): lax.ppermute(keep, 'dp', xor_route(4, m))  26.3 us
    reduce_scatter x4, waiting for transfers between devices, sum_planes(): summed = lax.psum_scatter(grad, 'dp', scatter_dimension=0, tiled=True)  19.2 us
    unnamed x203, local copies, waits for them, and re-layouts  18.9 us
    sub x6, other arithmetic, adam_update(): weight_out = weight_in - LEARN_RATE * (ratio + WEIGHT_DECAY * weight_in)  16.4 us
    ppermute x5, waiting for transfers between devices, sum_over(): values = values + lax.ppermute(values, axis, xor_route(size, step))  12.2 us
  transfers between devices with their start and end apart: 90, of which 55 were waited for; matrix products, arithmetic and copies ran while one was open for 18% of the time, Pallas kernels for 1%

profile of v4, /device:TPU:0, one launch (start us, length us, event | category | flops | bytes accessed | tf_op | source)
XLA Modules:
  0.0 444.5 jit_solution(421215252696158203)
XLA Ops:
  14.3 5.0 %collective-permute-start.10 = (bf16[144,1152]{1,0:T(8,128)(2,1)S(1)}, bf16[144,1152]{1,0:T(8,128)(2,1)S(1)}, u32[]{:S(2)}, u32[]{:S(2)}) collective-permute-start(bf16[144,1152]{1,0:T(8,128)(2,1)S(1)} %get-tuple-element.110), channel_id=1, source_target_pairs={{0,3},{1,2},{2,1},{3,0},{4,7},{5,6},{6,5},{7,4},{8,11},{9,10},{10,... | collective-permute-start | bytes 995336 | tf_op jit(solution)/shard_map/weights_in/ppermute | solution.py:453
  21.7 6.4 %collective-permute-done.10 = bf16[144,1152]{1,0:T(8,128)(2,1)S(1)} collective-permute-done((bf16[144,1152]{1,0:T(8,128)(2,1)S(1)}, bf16[144,1152]{1,0:T(8,128)(2,1)S(1)}, u32[]{:S(2)}, u32[]{:S(2)}) %collective-permute-start.10) | collective-permute-done | bytes 331808 | tf_op jit(solution)/shard_map/weights_in/ppermute | solution.py:453
  28.1 7.7 %collective-permute-done.8 = bf16[144,1152]{1,0:T(8,128)(2,1)S(1)} collective-permute-done((bf16[144,1152]{1,0:T(8,128)(2,1)S(1)}, bf16[144,1152]{1,0:T(8,128)(2,1)S(1)}, u32[]{:S(2)}, u32[]{:S(2)}) %collective-permute-start.8) | collective-permute-done | bytes 331808 | tf_op jit(solution)/shard_map/weights_in/ppermute | solution.py:453
  35.7 12.2 %collective-permute-done.9 = bf16[144,1152]{1,0:T(8,128)(2,1)S(1)} collective-permute-done((bf16[144,1152]{1,0:T(8,128)(2,1)S(1)}, bf16[144,1152]{1,0:T(8,128)(2,1)S(1)}, u32[]{:S(2)}, u32[]{:S(2)}) %collective-permute-start.9) | collective-permute-done | bytes 331808 | tf_op jit(solution)/shard_map/weights_in/ppermute | solution.py:453
  54.6 3.0 collective-permute-start.1
  68.0 11.2 %collective-permute-done.19 = bf16[144,2304]{1,0:T(8,128)(2,1)} collective-permute-done((bf16[144,2304]{1,0:T(8,128)(2,1)}, bf16[144,2304]{1,0:T(8,128)(2,1)}, u32[]{:S(2)}, u32[]{:S(2)}) %collective-permute-start.19) | collective-permute-done | bytes 663584 | tf_op jit(solution)/shard_map/weights_in/ppermute | solution.py:121
  84.0 3.0 collective-permute-start.4
  88.8 3.8 collective-permute-done.5
  92.6 9.2 %all-gather.1 = f32[8,2,1728]{2,1,0:T(2,128)S(1)} all-gather(f32[1,2,1728]{2,1,0:T(2,128)S(1)} %fusion.150), channel_id=2, replica_groups=mesh['section'=2,'row'=2,'core'=2,'dp'=4] {'section','row','core'}, dimensions={0}, use_global_device_ids=true | all-gather | bytes 124416 | tf_op jit(solution)/shard_map/modulation/all_gather | solution.py:474
  109.1 3.8 broadcast_select_fusion
  119.6 4.1 collective-permute-done.12
  134.3 3.7 collective-permute-done.16
  138.5 3.2 all-gather.8.cloned.1.call-done
  141.7 3.9 multiply_convert_fusion.2
  150.4 4.0 collective-permute-done.20
  163.7 3.6 collective-permute-done.24
  176.8 3.7 collective-permute-done.26
  191.7 7.7 %all-gather.10.cloned.1.call-done.up_ref.down_ref = bf16[1152,2304]{1,0:T(8,128)(2,1)} async-done(((bf16[144,2304]{1,0:T(8,128)(2,1)}), bf16[1152,2304]{1,0:T(8,128)(2,1)}) %all-gather.10.cloned.1.call-update) | async-done | bytes 5308432 | tf_op jit(solution)/shard_map/encoder/all_gather | solution.py:173
  201.8 5.2 %decoder.1 = (bf16[256,1152]{1,0:T(8,128)(2,1)S(1)}, bf16[256,1152]{1,0:T(8,128)(2,1)S(1)}, bf16[256,1152]{1,0:T(8,128)(2,1)S(1)}) custom-call(bf16[256,1152]{1,0:T(8,128)(2,1)S(1)} %pad_maximum_fusion.9.normed, bf16[1152,2304]{1,0:T(8,128)(2,1)S(1)} %copy-done.2, bf16[1152,2304]{1,0:T(8,128)(2,1)S(1)} %copy-done.2, ...), custom_call_target="tpu_custom_call" | custom-call | flops 2038431744 | bytes 8257536 | tf_op jit(solution)/shard_map/decoder/pallas_call | solution.py:269
  219.8 4.1 collective-permute-done.34.first
  233.5 3.6 collective-permute-done.38
  253.5 13.3 %reduce-scatter.5.cloned.1.call-done = bf16[1,144,2304]{2,1,0:T(8,128)(2,1)} async-done(((bf16[4,144,2304]{2,1,0:T(8,128)(2,1)}), bf16[1,144,2304]{2,1,0:T(8,128)(2,1)}) %reduce-scatter.5.cloned.1.call-update) | async-done | bytes 663568 | tf_op jit(solution)/shard_map/decoder_back/reduce_scatter | solution.py:188
  274.1 3.6 collective-permute-done.45
  279.2 3.4 fusion.46
  306.6 4.4 collective-permute-done.53
  323.5 4.2 collective-permute-done.59
  333.2 3.2 collective-permute-done.62
  351.4 3.0 reduce-scatter.9.cloned.1.call-done
  360.9 3.9 all-to-all-start
  364.8 4.8 %all-to-all-done = f32[8,1,1728]{2,1,0:T(1,128)S(1)} async-done(((f32[8,1,1728]{2,1,0:T(1,128)}), f32[8,1,1728]{2,1,0:T(1,128)S(1)}, u32[]{:S(2)}, u32[]{:S(2)}) %all-to-all-start) | async-done | bytes 55328 | tf_op jit(solution)/shard_map/modulation_back/all_to_all | solution.py:624
  398.4 3.5 collective-permute-done.75
  418.4 6.6 %multiply_subtract_fusion = (f32[1,288,1728]{2,1,0:T(8,128)}, f32[1,288,1728]{2,1,0:T(8,128)}, f32[1,288,1728]{2,1,0:T(8,128)}) fusion(f32[1,288,1728]{2,1,0:T(8,128)S(1)} %copy-done.16, f32[288,1728]{1,0:T(8,128)} %get-tuple-element.198, f32[]{:T(128)S(6)} %min.3, f32[1,288,1728]{2,1,0:T(8,128)} %param.45, f32[1,288,1728]{2,1,0:T(8,128)} %param.46), kind=kLoop, calls=%fused_computation.49 | loop fusion | flops 7962624 | bytes 13934596 | tf_op jit(solution)/shard_map/update/sub | solution.py:407
  (553 shorter events, 255.7 us)
Async XLA Ops:
  7.2 101.9 %all-gather.6.cloned.1.call-start = ((), (), s32[]{:S(2)}) async-start(), calls=%async_computation.5 | async-start | bytes 2985984 | tf_op jit(solution)/shard_map/weights_in/all_gather | solution.py:173
  14.3 13.7 %collective-permute-start.10 = (bf16[144,1152]{1,0:T(8,128)(2,1)S(1)}, bf16[144,1152]{1,0:T(8,128)(2,1)S(1)}, u32[]{:S(2)}, u32[]{:S(2)}) collective-permute-start(bf16[144,1152]{1,0:T(8,128)(2,1)S(1)} %get-tuple-element.110), channel_id=1, source_target_pairs={{0,3},{1,2},{2,1},{3,0},{4,7},{5,6},{6,5},{7,4},{8,11},{9,10},{10,... | collective-permute-start | bytes 995336 | tf_op jit(solution)/shard_map/weights_in/ppermute | solution.py:453
  19.4 16.3 %collective-permute-start.8 = (bf16[144,1152]{1,0:T(8,128)(2,1)S(1)}, bf16[144,1152]{1,0:T(8,128)(2,1)S(1)}, u32[]{:S(2)}, u32[]{:S(2)}) collective-permute-start(bf16[144,1152]{1,0:T(8,128)(2,1)S(1)} %get-tuple-element.110), channel_id=1, source_target_pairs={{0,1},{1,0},{2,3},{3,2},{4,5},{5,4},{6,7},{7,6},{8,9},{9,8},{10,11... | collective-permute-start | bytes 995336 | tf_op jit(solution)/shard_map/weights_in/ppermute | solution.py:453
  19.4 28.6 %collective-permute-start.9 = (bf16[144,1152]{1,0:T(8,128)(2,1)S(1)}, bf16[144,1152]{1,0:T(8,128)(2,1)S(1)}, u32[]{:S(2)}, u32[]{:S(2)}) collective-permute-start(bf16[144,1152]{1,0:T(8,128)(2,1)S(1)} %get-tuple-element.110), channel_id=1, source_target_pairs={{0,2},{1,3},{2,0},{3,1},{4,6},{5,7},{6,4},{7,5},{8,10},{9,11},{10,... | collective-permute-start | bytes 995336 | tf_op jit(solution)/shard_map/weights_in/ppermute | solution.py:453
  20.0 28.7 %collective-permute-start.7 = (bf16[144,1152]{1,0:T(8,128)(2,1)S(1)}, bf16[144,1152]{1,0:T(8,128)(2,1)S(1)}, u32[]{:S(2)}, u32[]{:S(2)}) collective-permute-start(bf16[144,1152]{1,0:T(8,128)(2,1)S(1)} %get-tuple-element.263), channel_id=1, source_target_pairs={{0,16},{16,0},{1,17},{17,1},{2,18},{18,2},{3,19},{19,3},{4,20},{20... | collective-permute-start | bytes 995336 | tf_op jit(solution)/shard_map/weights_in/ppermute | solution.py:121
  49.4 92.3 %all-gather.8.cloned.1.call-start = ((), (), s32[]{:S(2)}) async-start(), calls=%async_computation.6 | async-start | bytes 5971968 | tf_op jit(solution)/shard_map/weights_in/all_gather | solution.py:173
  54.5 27.6 %collective-permute-start = (s32[2,2]{0,1:T(2,128)S(1)}, s32[2,2]{0,1:T(2,128)S(1)}, u32[]{:S(2)}, u32[]{:S(2)}) collective-permute-start(s32[2,2]{0,1:T(2,128)S(1)} %pad_add_fusion.1), channel_id=1, source_target_pairs={{0,1},{1,0},{2,3},{3,2},{4,5},{5,4},{6,7},{7,6},{8,9},{9,8},{10,11... | collective-permute-start | bytes 56 | tf_op jit(solution)/shard_map/modulation/ppermute | solution.py:90
  54.6 27.5 %collective-permute-start.1 = (s32[2,2]{0,1:T(2,128)S(1)}, s32[2,2]{0,1:T(2,128)S(1)}, u32[]{:S(2)}, u32[]{:S(2)}) collective-permute-start(s32[2,2]{0,1:T(2,128)S(1)} %pad_add_fusion.1), channel_id=1, source_target_pairs={{0,2},{1,3},{2,0},{3,1},{4,6},{5,7},{6,4},{7,5},{8,10},{9,11},{10,... | collective-permute-start | bytes 56 | tf_op jit(solution)/shard_map/modulation/ppermute | solution.py:90
  57.6 24.5 %collective-permute-start.2 = (s32[2,2]{0,1:T(2,128)S(1)}, s32[2,2]{0,1:T(2,128)S(1)}, u32[]{:S(2)}, u32[]{:S(2)}) collective-permute-start(s32[2,2]{0,1:T(2,128)S(1)} %pad_add_fusion.1), channel_id=1, source_target_pairs={{0,3},{1,2},{2,1},{3,0},{4,7},{5,6},{6,5},{7,4},{8,11},{9,10},{10,... | collective-permute-start | bytes 56 | tf_op jit(solution)/shard_map/modulation/ppermute | solution.py:90
  62.4 16.8 %collective-permute-start.19 = (bf16[144,2304]{1,0:T(8,128)(2,1)}, bf16[144,2304]{1,0:T(8,128)(2,1)}, u32[]{:S(2)}, u32[]{:S(2)}) collective-permute-start(bf16[144,2304]{1,0:T(8,128)(2,1)} %broadcast_select_fusion.7), channel_id=1, source_target_pairs={{0,16},{16,0},{1,17},{17,1},{2,18},{18,2},{3,19},{19,3},{4,20},{20... | collective-permute-start | bytes 1990664 | tf_op jit(solution)/shard_map/weights_in/ppermute | solution.py:121
  81.9 117.4 %all-gather.10.cloned.1.call-start = ((), (), s32[]{:S(2)}) async-start(), calls=%async_computation.7 | async-start | bytes 5971968 | tf_op jit(solution)/shard_map/encoder/all_gather | solution.py:173
  88.6 16.0 %collective-permute-start.11 = (bf16[4,144,1152]{2,1,0:T(8,128)(2,1)S(1)}, bf16[4,144,1152]{2,1,0:T(8,128)(2,1)S(1)}, u32[]{:S(2)}, u32[]{:S(2)}) collective-permute-start(bf16[4,144,1152]{2,1,0:T(8,128)(2,1)S(1)} %pad_maximum_fusion.2.mine_ref), channel_id=1, source_target_pairs={{0,4},{4,0},{1,5},{5,1},{2,6},{6,2},{3,7},{7,3},{8,12},{12,8},{9,1... | collective-permute-start | bytes 3981320 | tf_op jit(solution)/shard_map/weights_in/ppermute | solution.py:64
  129.2 8.8 %collective-permute-start.16 = (bf16[64,1152]{1,0:T(8,128)(2,1)S(1)}, bf16[64,1152]{1,0:T(8,128)(2,1)S(1)}, u32[]{:S(2)}, u32[]{:S(2)}) collective-permute-start(bf16[64,1152]{1,0:T(8,128)(2,1)S(1)} %add_convert_fusion.4), channel_id=1, source_target_pairs={{0,8},{8,0},{16,24},{24,16},{1,9},{9,1},{17,25},{25,17},{2,10},{10... | collective-permute-start | bytes 442376 | tf_op jit(solution)/shard_map/encoder/ppermute | solution.py:60
  138.1 128.6 %reduce-scatter.5.cloned.1.call-start = ((), (), s32[]{:S(2)}) async-start(), calls=%async_computation.8 | async-start | bytes 3317760 | tf_op jit(solution)/shard_map/decoder_back/reduce_scatter | solution.py:188
  158.6 8.7 %collective-permute-start.24 = (bf16[64,1152]{1,0:T(8,128)(2,1)S(1)}, bf16[64,1152]{1,0:T(8,128)(2,1)S(1)}, u32[]{:S(2)}, u32[]{:S(2)}) collective-permute-start(bf16[64,1152]{1,0:T(8,128)(2,1)S(1)} %multiply_convert_fusion.5), channel_id=1, source_target_pairs={{0,8},{8,0},{16,24},{24,16},{1,9},{9,1},{17,25},{25,17},{2,10},{10... | collective-permute-start | bytes 442376 | tf_op jit(solution)/shard_map/encoder/ppermute | solution.py:60
  215.2 85.6 %reduce-scatter.7.cloned.1.call-start = ((), (), s32[]{:S(2)}) async-start(), calls=%async_computation.9 | async-start | bytes 1658880 | tf_op jit(solution)/shard_map/decoder_back/reduce_scatter | solution.py:188
  244.4 8.8 %collective-permute-start.41 = (bf16[64,1152]{1,0:T(8,128)(2,1)S(1)}, bf16[64,1152]{1,0:T(8,128)(2,1)S(1)}, u32[]{:S(2)}, u32[]{:S(2)}) collective-permute-start(bf16[64,1152]{1,0:T(8,128)(2,1)S(1)} %get-tuple-element.284), channel_id=1, source_target_pairs={{0,8},{8,0},{16,24},{24,16},{1,9},{9,1},{17,25},{25,17},{2,10},{10... | collective-permute-start | bytes 442376 | tf_op jit(solution)/shard_map/decoder_back/ppermute | solution.py:60
  253.3 101.2 %reduce-scatter.9.cloned.1.call-start = ((), (), s32[]{:S(2)}) async-start(), calls=%async_computation.10 | async-start | bytes 3317760 | tf_op jit(solution)/shard_map/encoder_back/reduce_scatter | solution.py:188
  284.9 8.9 %collective-permute-start.50 = (bf16[4,144,1152]{2,1,0:T(8,128)(2,1)S(1)}, bf16[4,144,1152]{2,1,0:T(8,128)(2,1)S(1)}, u32[]{:S(2)}, u32[]{:S(2)}) collective-permute-start(bf16[4,144,1152]{2,1,0:T(8,128)(2,1)S(1)} %dynamic-slice_bitcast_fusion.2), channel_id=1, source_target_pairs={{0,4},{4,0},{1,5},{5,1},{2,6},{6,2},{3,7},{7,3},{8,12},{12,8},{9,1... | collective-permute-start | bytes 3981320 | tf_op jit(solution)/shard_map/encoder_back/ppermute | solution.py:64
  287.4 8.8 %collective-permute-start.47 = (bf16[64,1152]{1,0:T(8,128)(2,1)}, bf16[64,1152]{1,0:T(8,128)(2,1)S(1)}, u32[]{:S(2)}, u32[]{:S(2)}) collective-permute-start(bf16[64,1152]{1,0:T(8,128)(2,1)} %get-tuple-element.281), channel_id=1, source_target_pairs={{0,24},{8,16},{16,8},{24,0},{1,25},{9,17},{17,9},{25,1},{2,26},{10... | collective-permute-start | bytes 442376 | tf_op jit(solution)/shard_map/encoder_back/ppermute | solution.py:60
  302.3 88.9 %reduce-scatter.11.cloned.1.call-start = ((), (), s32[]{:S(2)}) async-start(), calls=%async_computation.11 | async-start | bytes 1658880 | tf_op jit(solution)/shard_map/encoder_back/reduce_scatter | solution.py:188
  319.0 24.3 %collective-permute-start.58 = (bf16[4,144,1152]{2,1,0:T(8,128)(2,1)S(1)}, bf16[4,144,1152]{2,1,0:T(8,128)(2,1)S(1)}, u32[]{:S(2)}, u32[]{:S(2)}) collective-permute-start(bf16[4,144,1152]{2,1,0:T(8,128)(2,1)S(1)} %dynamic-slice_bitcast_fusion), channel_id=1, source_target_pairs={{0,4},{4,0},{1,5},{5,1},{2,6},{6,2},{3,7},{7,3},{8,12},{12,8},{9,1... | collective-permute-start | bytes 3981320 | tf_op jit(solution)/shard_map/encoder_back/ppermute | solution.py:64
  339.6 10.6 %collective-permute-start.65 = (bf16[256,1152]{1,0:T(8,128)(2,1)S(1)}, bf16[256,1152]{1,0:T(8,128)(2,1)S(1)}, u32[]{:S(2)}, u32[]{:S(2)}) collective-permute-start(bf16[256,1152]{1,0:T(8,128)(2,1)S(1)} %convolution_convert_fusion.12), channel_id=1, source_target_pairs={{0,4},{4,0},{1,5},{5,1},{2,6},{6,2},{3,7},{7,3},{8,12},{12,8},{9,1... | collective-permute-start | bytes 1769480 | tf_op jit(solution)/shard_map/encoder_back/ppermute | solution.py:64
  341.2 8.9 %collective-permute-start.56 = (bf16[64,1152]{1,0:T(8,128)(2,1)S(1)}, bf16[64,1152]{1,0:T(8,128)(2,1)S(1)}, u32[]{:S(2)}, u32[]{:S(2)}) collective-permute-start(bf16[64,1152]{1,0:T(8,128)(2,1)S(1)} %get-tuple-element.276), channel_id=1, source_target_pairs={{0,8},{8,0},{16,24},{24,16},{1,9},{9,1},{17,25},{25,17},{2,10},{10... | collective-permute-start | bytes 442376 | tf_op jit(solution)/shard_map/encoder_back/ppermute | solution.py:60
  355.5 14.0 %collective-permute-start.66 = (bf16[64,1152]{1,0:T(8,128)(2,1)S(1)}, bf16[64,1152]{1,0:T(8,128)(2,1)S(1)}, u32[]{:S(2)}, u32[]{:S(2)}) collective-permute-start(bf16[64,1152]{1,0:T(8,128)(2,1)S(1)} %get-tuple-element.177), channel_id=1, source_target_pairs={{0,16},{8,24},{16,0},{24,8},{1,17},{9,25},{17,1},{25,9},{2,18},{10... | collective-permute-start | bytes 442376 | tf_op jit(solution)/shard_map/encoder_back/ppermute | solution.py:60
  357.0 12.6 %collective-permute-start.67 = (bf16[64,1152]{1,0:T(8,128)(2,1)S(1)}, bf16[64,1152]{1,0:T(8,128)(2,1)S(1)}, u32[]{:S(2)}, u32[]{:S(2)}) collective-permute-start(bf16[64,1152]{1,0:T(8,128)(2,1)S(1)} %get-tuple-element.177), channel_id=1, source_target_pairs={{0,8},{8,0},{16,24},{24,16},{1,9},{9,1},{17,25},{25,17},{2,10},{10... | collective-permute-start | bytes 442376 | tf_op jit(solution)/shard_map/encoder_back/ppermute | solution.py:60
  358.5 11.1 %collective-permute-start.68 = (bf16[64,1152]{1,0:T(8,128)(2,1)S(1)}, bf16[64,1152]{1,0:T(8,128)(2,1)S(1)}, u32[]{:S(2)}, u32[]{:S(2)}) collective-permute-start(bf16[64,1152]{1,0:T(8,128)(2,1)S(1)} %get-tuple-element.177), channel_id=1, source_target_pairs={{0,24},{8,16},{16,8},{24,0},{1,25},{9,17},{17,9},{25,1},{2,26},{10... | collective-permute-start | bytes 442376 | tf_op jit(solution)/shard_map/encoder_back/ppermute | solution.py:60
  360.9 8.7 %all-to-all-start = ((f32[8,1,1728]{2,1,0:T(1,128)}), f32[8,1,1728]{2,1,0:T(1,128)S(1)}, u32[]{:S(2)}, u32[]{:S(2)}) async-start(f32[8,1,1728]{2,1,0:T(1,128)} %all_to_all.11), calls=%async_computation.3 | async-start | bytes 114688 | tf_op jit(solution)/shard_map/modulation_back/all_to_all | solution.py:624
  371.0 17.4 %collective-permute-start.73 = (bf16[256,1152]{1,0:T(8,128)(2,1)}, bf16[256,1152]{1,0:T(8,128)(2,1)}, u32[]{:S(2)}, u32[]{:S(2)}) collective-permute-start(bf16[256,1152]{1,0:T(8,128)(2,1)} %convolution_convert_fusion.11), channel_id=1, source_target_pairs={{0,4},{4,0},{1,5},{5,1},{2,6},{6,2},{3,7},{7,3},{8,12},{12,8},{9,1... | collective-permute-start | bytes 1769480 | tf_op jit(solution)/shard_map/outputs/ppermute | solution.py:64
  371.3 20.0 %collective-permute-start.72 = (bf16[144,2304]{1,0:T(8,128)(2,1)S(1)}, bf16[144,2304]{1,0:T(8,128)(2,1)S(1)}, u32[]{:S(2)}, u32[]{:S(2)}) collective-permute-start(bf16[144,2304]{1,0:T(8,128)(2,1)S(1)} %get-tuple-element.249), channel_id=1, source_target_pairs={{0,16},{16,0},{1,17},{17,1},{2,18},{18,2},{3,19},{19,3},{4,20},{20... | collective-permute-start | bytes 1990664 | tf_op jit(solution)/shard_map/returns/ppermute | solution.py:157
  391.3 20.5 %collective-permute-start.81 = (bf16[144,2304]{1,0:T(8,128)(2,1)S(1)}, bf16[144,2304]{1,0:T(8,128)(2,1)S(1)}, u32[]{:S(2)}, u32[]{:S(2)}) collective-permute-start(bf16[144,2304]{1,0:T(8,128)(2,1)S(1)} %broadcast_select_fusion.4), channel_id=1, source_target_pairs={{0,4},{4,0},{1,5},{5,1},{2,6},{6,2},{3,7},{7,3},{8,12},{12,8},{9,1... | collective-permute-start | bytes 1990664 | tf_op jit(solution)/shard_map/norm/ppermute | solution.py:64
  393.8 9.5 %collective-permute-start.76 = (bf16[144,1152]{1,0:T(8,128)(2,1)S(1)}, bf16[144,1152]{1,0:T(8,128)(2,1)S(1)}, u32[]{:S(2)}, u32[]{:S(2)}) collective-permute-start(bf16[144,1152]{1,0:T(8,128)(2,1)S(1)} %get-tuple-element.267), channel_id=1, source_target_pairs={{0,16},{16,0},{1,17},{17,1},{2,18},{18,2},{3,19},{19,3},{4,20},{20... | collective-permute-start | bytes 995336 | tf_op jit(solution)/shard_map/norm/ppermute | solution.py:157
  (155 other events, 1018.8 us)
Sparse Core Ops, SparseCore 0:
  49.6 34.3 all-gather.5
  86.1 55.5 all-gather.7
  143.9 55.3 all-gather.9
  215.3 51.3 reduce-scatter.4
  269.5 31.3 reduce-scatter.6
  303.0 51.4 reduce-scatter.8
  357.3 32.2 reduce-scatter.10

commit v5 on v4

--- a/solution.py
+++ b/solution.py
@@ -449,14 +449,18 @@
             [heads_weight[0, 0], heads_weight[0, 1], heads_weight[0, 2], output_weight[0].T], axis=1
         ).astype(BF)
         keep, given = send_shares(attn_pack, section, core)
+        attn_width = attn_pack.shape[1]
         if lax.axis_size("dp") == 4:
-            parts = [keep] + [lax.ppermute(keep, "dp", xor_route(4, m)) for m in (1, 2, 3)]
+            cut = attn_width // 3
+            first = keep[:, :cut]
+            parts = [first] + [lax.ppermute(first, "dp", xor_route(4, m)) for m in (1, 2, 3)]
             given, *parts = tie(given, *parts)
-            given_all = gather_weight(given)
-            keep_all = assemble(parts, plane, core)
+            rest = gather_weight(jnp.concatenate([given, keep[:, cut:]], axis=1))
+            keep_all = jnp.concatenate([assemble(parts, plane, core), rest[:, attn_width:]], axis=1)
         else:
-            given_all, keep_all = gather_weight(given), gather_weight(keep)
-        enc_attn, dec_attn = by_block(keep_all, given_all, section)
+            rest = gather_weight(jnp.concatenate([given, keep], axis=1))
+            keep_all = rest[:, attn_width:]
+        enc_attn, dec_attn = by_block(keep_all, rest[:, :attn_width], section)
         feed_pack = jnp.concatenate([up_weight[0], down_weight[0].T], axis=1).astype(BF)
         feed_pack, given = tie(feed_pack, given)
         enc_feed_half, dec_feed_half = by_block(*send_shares(feed_pack, section, core), section)

time: 453 us -> 450 us (level)
  waiting for transfers between devices: 183 us -> 191 us
  local copies, waits for them, and re-layouts: 28.8 us -> 24.1 us
    all_gather x3, waiting for transfers between devices: 10.9 us -> 30.7 us  [gather_weight(): return lax.all_gather(half, ROWS_BY, axis=0, tiled=True)]
    ppermute x3, waiting for transfers between devices: 26.3 us -> 8.5 us  [per_device(): lax.ppermute(first, 'dp', xor_route(4, m))]
    unnamed x203 -> x221, local copies, waits for them, and re-layouts: 18.9 us -> 13.8 us
  transfers between devices with their start and end apart: 90 -> 90, of which waited for: 55 -> 56; matrix products, arithmetic and copies ran while one was open for 18% -> 16% of each run, Pallas kernels for 1% -> 1%
where the time goes in v5:
time: 450 us; the launch traced here: 442 us
  waiting for transfers between devices  191 us (42%)
  starting transfers between devices  92.1 us (20%)
  other arithmetic  54.9 us (12%)
  matrix products  39 us (9%)
  local copies, waits for them, and re-layouts  24.1 us (5%)
  between operations  23 us (5%)
  blocking collectives  9.52 us (2%)
  Pallas kernels  8.84 us (2%)
    ppermute x48, waiting for transfers between devices, swap_chips(): return lax.ppermute(block, CHIPS, chip_route(offset))  86.9 us
    ppermute x48, starting transfers between devices, swap_chips(): return lax.ppermute(block, CHIPS, chip_route(offset))  56.7 us
    dot_general x28, matrix products, dot(): lax.dot_general(left, right, (dims, ((), ())), preferred_element_type=F32)  32.2 us
    all_gather x3, waiting for transfers between devices, gather_weight(): return lax.all_gather(half, ROWS_BY, axis=0, tiled=True)  30.7 us
    reduce_scatter x4, waiting for transfers between devices, sum_planes(): summed = lax.psum_scatter(grad, 'dp', scatter_dimension=0, tiled=True)  19 us
    sub x6, other arithmetic, adam_update(): weight_out = weight_in - LEARN_RATE * (ratio + WEIGHT_DECAY * weight_in)  16.5 us
    ppermute x2, waiting for transfers between devices, send_shares(): return (keep, lax.ppermute(give, 'section', [(0, 1), (1, 0)]))  15.2 us
    unnamed x221, local copies, waits for them, and re-layouts  13.8 us
  transfers between devices with their start and end apart: 90, of which 56 were waited for; matrix products, arithmetic and copies ran while one was open for 16% of the time, Pallas kernels for 1%

profile of v5, /device:TPU:0, one launch (start us, length us, event | category | flops | bytes accessed | tf_op | source)
XLA Modules:
  0.0 442.3 jit_solution(8749618117201868000)
XLA Ops:
  17.3 3.7 collective-permute-start.10
  21.8 3.3 collective-permute-done.10
  35.8 3.0 collective-permute-start.1
  44.4 15.2 %collective-permute-done.19 = bf16[144,2304]{1,0:T(8,128)(2,1)S(1)} collective-permute-done((bf16[144,2304]{1,0:T(8,128)(2,1)S(1)}, bf16[144,2304]{1,0:T(8,128)(2,1)S(1)}, u32[]{:S(2)}, u32[]{:S(2)}) %collective-permute-start.19) | collective-permute-done | bytes 663584 | tf_op jit(solution)/shard_map/weights_in/ppermute | solution.py:121
  64.0 3.0 collective-permute-start.4
  72.8 9.5 %all-gather.1 = f32[8,2,1728]{2,1,0:T(2,128)S(1)} all-gather(f32[1,2,1728]{2,1,0:T(2,128)S(1)} %fusion.150), channel_id=2, replica_groups=mesh['section'=2,'row'=2,'core'=2,'dp'=4] {'section','row','core'}, dimensions={0}, use_global_device_ids=true | all-gather | bytes 124416 | tf_op jit(solution)/shard_map/modulation/all_gather | solution.py:478
  86.8 3.5 broadcast_select_fusion
  96.9 4.1 collective-permute-done.12
  111.8 3.7 collective-permute-done.16
  116.0 23.0 %all-gather.8.cloned.1.call-done = bf16[1152,2304]{1,0:T(8,128)(2,1)} async-done(((bf16[144,2304]{1,0:T(8,128)(2,1)}), bf16[1152,2304]{1,0:T(8,128)(2,1)}) %all-gather.8.cloned.1.call-update) | async-done | bytes 5308432 | tf_op jit(solution)/shard_map/weights_in/all_gather | solution.py:173
  139.1 4.0 multiply_convert_fusion.2
  147.8 4.0 collective-permute-done.20
  158.1 3.0 collective-permute-done.23
  161.1 3.6 collective-permute-done.24
  174.2 3.7 collective-permute-done.26
  189.1 7.6 %all-gather.10.cloned.1.call-done.up_ref.down_ref = bf16[1152,2304]{1,0:T(8,128)(2,1)} async-done(((bf16[144,2304]{1,0:T(8,128)(2,1)}), bf16[1152,2304]{1,0:T(8,128)(2,1)}) %all-gather.10.cloned.1.call-update) | async-done | bytes 5308432 | tf_op jit(solution)/shard_map/encoder/all_gather | solution.py:173
  199.2 5.2 %decoder.1 = (bf16[256,1152]{1,0:T(8,128)(2,1)S(1)}, bf16[256,1152]{1,0:T(8,128)(2,1)S(1)}, bf16[256,1152]{1,0:T(8,128)(2,1)S(1)}) custom-call(bf16[256,1152]{1,0:T(8,128)(2,1)S(1)} %pad_maximum_fusion.9.normed, bf16[1152,2304]{1,0:T(8,128)(2,1)S(1)} %copy-done.2, bf16[1152,2304]{1,0:T(8,128)(2,1)S(1)} %copy-done.2, ...), custom_call_target="tpu_custom_call" | custom-call | flops 2038431744 | bytes 8257536 | tf_op jit(solution)/shard_map/decoder/pallas_call | solution.py:269
  217.2 4.1 collective-permute-done.34.first
  227.8 3.0 collective-permute-done.37
  230.8 3.6 collective-permute-done.38
  250.9 13.3 %reduce-scatter.5.cloned.1.call-done = bf16[1,144,2304]{2,1,0:T(8,128)(2,1)} async-done(((bf16[4,144,2304]{2,1,0:T(8,128)(2,1)}), bf16[1,144,2304]{2,1,0:T(8,128)(2,1)}) %reduce-scatter.5.cloned.1.call-update) | async-done | bytes 663568 | tf_op jit(solution)/shard_map/decoder_back/reduce_scatter | solution.py:188
  271.6 3.6 collective-permute-done.45
  276.6 3.5 fusion.46
  304.0 4.4 collective-permute-done.53
  320.1 4.1 collective-permute-done.59
  330.6 3.2 collective-permute-done.62
  348.9 2.9 reduce-scatter.9.cloned.1.call-done
  358.3 3.9 all-to-all-start
  362.2 4.8 %all-to-all-done = f32[8,1,1728]{2,1,0:T(1,128)S(1)} async-done(((f32[8,1,1728]{2,1,0:T(1,128)}), f32[8,1,1728]{2,1,0:T(1,128)S(1)}, u32[]{:S(2)}, u32[]{:S(2)}) %all-to-all-start) | async-done | bytes 55328 | tf_op jit(solution)/shard_map/modulation_back/all_to_all | solution.py:628
  379.7 3.0 multiply_reduce_fusion
  395.7 3.1 collective-permute-done.75
  416.3 6.6 %multiply_subtract_fusion = (f32[1,288,1728]{2,1,0:T(8,128)}, f32[1,288,1728]{2,1,0:T(8,128)}, f32[1,288,1728]{2,1,0:T(8,128)}) fusion(f32[1,288,1728]{2,1,0:T(8,128)S(1)} %copy-done.16, f32[288,1728]{1,0:T(8,128)} %get-tuple-element.198, f32[]{:T(128)S(6)} %min.3, f32[1,288,1728]{2,1,0:T(8,128)} %param.45, f32[1,288,1728]{2,1,0:T(8,128)} %param.46), kind=kLoop, calls=%fused_computation.50 | loop fusion | flops 7962624 | bytes 13934596 | tf_op jit(solution)/shard_map/update/sub | solution.py:407
  (576 shorter events, 249.1 us)
Async XLA Ops:
  7.2 78.1 %all-gather.6.cloned.1.call-start = ((), (), s32[]{:S(2)}) async-start(), calls=%async_computation.5 | async-start | bytes 4976640 | tf_op jit(solution)/shard_map/weights_in/all_gather | solution.py:173
  14.4 16.6 %collective-permute-start.7 = (bf16[144,1152]{1,0:T(8,128)(2,1)S(1)}, bf16[144,1152]{1,0:T(8,128)(2,1)S(1)}, u32[]{:S(2)}, u32[]{:S(2)}) collective-permute-start(bf16[144,1152]{1,0:T(8,128)(2,1)S(1)} %get-tuple-element.262), channel_id=1, source_target_pairs={{0,16},{16,0},{1,17},{17,1},{2,18},{18,2},{3,19},{19,3},{4,20},{20... | collective-permute-start | bytes 995336 | tf_op jit(solution)/shard_map/weights_in/ppermute | solution.py:121
  21.0 9.3 %collective-permute-start.9 = (bf16[144,384]{1,0:T(8,128)(2,1)S(1)}, bf16[144,384]{1,0:T(8,128)(2,1)S(1)}, u32[]{:S(2)}, u32[]{:S(2)}) collective-permute-start(bf16[144,384]{1,0:T(8,128)(2,1)S(1)} %slice.406), channel_id=1, source_target_pairs={{0,2},{1,3},{2,0},{3,1},{4,6},{5,7},{6,4},{7,5},{8,10},{9,11},{10,... | collective-permute-start | bytes 331784 | tf_op jit(solution)/shard_map/weights_in/ppermute | solution.py:456
  31.8 107.2 %all-gather.8.cloned.1.call-start = ((), (), s32[]{:S(2)}) async-start(), calls=%async_computation.6 | async-start | bytes 5971968 | tf_op jit(solution)/shard_map/weights_in/all_gather | solution.py:173
  35.8 26.2 %collective-permute-start = (s32[2,2]{0,1:T(2,128)S(1)}, s32[2,2]{0,1:T(2,128)S(1)}, u32[]{:S(2)}, u32[]{:S(2)}) collective-permute-start(s32[2,2]{0,1:T(2,128)S(1)} %pad_add_fusion.1), channel_id=1, source_target_pairs={{0,1},{1,0},{2,3},{3,2},{4,5},{5,4},{6,7},{7,6},{8,9},{9,8},{10,11... | collective-permute-start | bytes 56 | tf_op jit(solution)/shard_map/modulation/ppermute | solution.py:90
  35.8 26.1 %collective-permute-start.1 = (s32[2,2]{0,1:T(2,128)S(1)}, s32[2,2]{0,1:T(2,128)S(1)}, u32[]{:S(2)}, u32[]{:S(2)}) collective-permute-start(s32[2,2]{0,1:T(2,128)S(1)} %pad_add_fusion.1), channel_id=1, source_target_pairs={{0,2},{1,3},{2,0},{3,1},{4,6},{5,7},{6,4},{7,5},{8,10},{9,11},{10,... | collective-permute-start | bytes 56 | tf_op jit(solution)/shard_map/modulation/ppermute | solution.py:90
  38.9 23.1 %collective-permute-start.2 = (s32[2,2]{0,1:T(2,128)S(1)}, s32[2,2]{0,1:T(2,128)S(1)}, u32[]{:S(2)}, u32[]{:S(2)}) collective-permute-start(s32[2,2]{0,1:T(2,128)S(1)} %pad_add_fusion.1), channel_id=1, source_target_pairs={{0,3},{1,2},{2,1},{3,0},{4,7},{5,6},{6,5},{7,4},{8,11},{9,10},{10,... | collective-permute-start | bytes 56 | tf_op jit(solution)/shard_map/modulation/ppermute | solution.py:90
  43.0 16.5 %collective-permute-start.19 = (bf16[144,2304]{1,0:T(8,128)(2,1)S(1)}, bf16[144,2304]{1,0:T(8,128)(2,1)S(1)}, u32[]{:S(2)}, u32[]{:S(2)}) collective-permute-start(bf16[144,2304]{1,0:T(8,128)(2,1)S(1)} %broadcast_select_fusion.7), channel_id=1, source_target_pairs={{0,16},{16,0},{1,17},{17,1},{2,18},{18,2},{3,19},{19,3},{4,20},{20... | collective-permute-start | bytes 1990664 | tf_op jit(solution)/shard_map/weights_in/ppermute | solution.py:121
  61.0 135.7 %all-gather.10.cloned.1.call-start = ((), (), s32[]{:S(2)}) async-start(), calls=%async_computation.7 | async-start | bytes 5971968 | tf_op jit(solution)/shard_map/encoder/all_gather | solution.py:173
  94.9 8.7 %collective-permute-start.13 = (bf16[64,1152]{1,0:T(8,128)(2,1)S(1)}, bf16[64,1152]{1,0:T(8,128)(2,1)S(1)}, u32[]{:S(2)}, u32[]{:S(2)}) collective-permute-start(bf16[64,1152]{1,0:T(8,128)(2,1)S(1)} %get-tuple-element.299), channel_id=1, source_target_pairs={{0,8},{8,0},{16,24},{24,16},{1,9},{9,1},{17,25},{25,17},{2,10},{10... | collective-permute-start | bytes 442376 | tf_op jit(solution)/shard_map/encoder/ppermute | solution.py:60
  106.7 8.8 %collective-permute-start.16 = (bf16[64,1152]{1,0:T(8,128)(2,1)S(1)}, bf16[64,1152]{1,0:T(8,128)(2,1)S(1)}, u32[]{:S(2)}, u32[]{:S(2)}) collective-permute-start(bf16[64,1152]{1,0:T(8,128)(2,1)S(1)} %add_convert_fusion.4), channel_id=1, source_target_pairs={{0,8},{8,0},{16,24},{24,16},{1,9},{9,1},{17,25},{25,17},{2,10},{10... | collective-permute-start | bytes 442376 | tf_op jit(solution)/shard_map/encoder/ppermute | solution.py:60
  115.6 148.5 %reduce-scatter.5.cloned.1.call-start = ((), (), s32[]{:S(2)}) async-start(), calls=%async_computation.8 | async-start | bytes 3317760 | tf_op jit(solution)/shard_map/decoder_back/reduce_scatter | solution.py:188
  156.0 8.7 %collective-permute-start.24 = (bf16[64,1152]{1,0:T(8,128)(2,1)S(1)}, bf16[64,1152]{1,0:T(8,128)(2,1)S(1)}, u32[]{:S(2)}, u32[]{:S(2)}) collective-permute-start(bf16[64,1152]{1,0:T(8,128)(2,1)S(1)} %multiply_convert_fusion.5), channel_id=1, source_target_pairs={{0,8},{8,0},{16,24},{24,16},{1,9},{9,1},{17,25},{25,17},{2,10},{10... | collective-permute-start | bytes 442376 | tf_op jit(solution)/shard_map/encoder/ppermute | solution.py:60
  212.6 85.7 %reduce-scatter.7.cloned.1.call-start = ((), (), s32[]{:S(2)}) async-start(), calls=%async_computation.9 | async-start | bytes 1658880 | tf_op jit(solution)/shard_map/decoder_back/reduce_scatter | solution.py:188
  225.8 8.7 %collective-permute-start.38 = (bf16[64,1152]{1,0:T(8,128)(2,1)S(1)}, bf16[64,1152]{1,0:T(8,128)(2,1)S(1)}, u32[]{:S(2)}, u32[]{:S(2)}) collective-permute-start(bf16[64,1152]{1,0:T(8,128)(2,1)S(1)} %get-tuple-element.128), channel_id=1, source_target_pairs={{0,8},{8,0},{16,24},{24,16},{1,9},{9,1},{17,25},{25,17},{2,10},{10... | collective-permute-start | bytes 442376 | tf_op jit(solution)/shard_map/decoder_back/ppermute | solution.py:60
  241.8 8.8 %collective-permute-start.41 = (bf16[64,1152]{1,0:T(8,128)(2,1)S(1)}, bf16[64,1152]{1,0:T(8,128)(2,1)S(1)}, u32[]{:S(2)}, u32[]{:S(2)}) collective-permute-start(bf16[64,1152]{1,0:T(8,128)(2,1)S(1)} %get-tuple-element.284), channel_id=1, source_target_pairs={{0,8},{8,0},{16,24},{24,16},{1,9},{9,1},{17,25},{25,17},{2,10},{10... | collective-permute-start | bytes 442376 | tf_op jit(solution)/shard_map/decoder_back/ppermute | solution.py:60
  250.7 101.2 %reduce-scatter.9.cloned.1.call-start = ((), (), s32[]{:S(2)}) async-start(), calls=%async_computation.10 | async-start | bytes 3317760 | tf_op jit(solution)/shard_map/encoder_back/reduce_scatter | solution.py:188
  286.3 8.6 %collective-permute-start.48 = (bf16[64,1152]{1,0:T(8,128)(2,1)}, bf16[64,1152]{1,0:T(8,128)(2,1)S(1)}, u32[]{:S(2)}, u32[]{:S(2)}) collective-permute-start(bf16[64,1152]{1,0:T(8,128)(2,1)} %get-tuple-element.280), channel_id=1, source_target_pairs={{0,8},{8,0},{16,24},{24,16},{1,9},{9,1},{17,25},{25,17},{2,10},{10... | collective-permute-start | bytes 442376 | tf_op jit(solution)/shard_map/encoder_back/ppermute | solution.py:60
  299.7 88.5 %reduce-scatter.11.cloned.1.call-start = ((), (), s32[]{:S(2)}) async-start(), calls=%async_computation.11 | async-start | bytes 1658880 | tf_op jit(solution)/shard_map/encoder_back/reduce_scatter | solution.py:188
  316.4 24.4 %collective-permute-start.58 = (bf16[4,144,1152]{2,1,0:T(8,128)(2,1)S(1)}, bf16[4,144,1152]{2,1,0:T(8,128)(2,1)S(1)}, u32[]{:S(2)}, u32[]{:S(2)}) collective-permute-start(bf16[4,144,1152]{2,1,0:T(8,128)(2,1)S(1)} %dynamic-slice_bitcast_fusion), channel_id=1, source_target_pairs={{0,4},{4,0},{1,5},{5,1},{2,6},{6,2},{3,7},{7,3},{8,12},{12,8},{9,1... | collective-permute-start | bytes 3981320 | tf_op jit(solution)/shard_map/encoder_back/ppermute | solution.py:64
  318.0 8.9 %collective-permute-start.60 = (bf16[64,1152]{1,0:T(8,128)(2,1)S(1)}, bf16[64,1152]{1,0:T(8,128)(2,1)S(1)}, u32[]{:S(2)}, u32[]{:S(2)}) collective-permute-start(bf16[64,1152]{1,0:T(8,128)(2,1)S(1)} %get-tuple-element.274), channel_id=1, source_target_pairs={{0,8},{8,0},{16,24},{24,16},{1,9},{9,1},{17,25},{25,17},{2,10},{10... | collective-permute-start | bytes 442376 | tf_op jit(solution)/shard_map/encoder_back/ppermute | solution.py:60
  327.8 8.8 %collective-permute-start.63 = (bf16[64,1152]{1,0:T(8,128)(2,1)S(1)}, bf16[64,1152]{1,0:T(8,128)(2,1)S(1)}, u32[]{:S(2)}, u32[]{:S(2)}) collective-permute-start(bf16[64,1152]{1,0:T(8,128)(2,1)S(1)} %get-tuple-element.259), channel_id=1, source_target_pairs={{0,8},{8,0},{16,24},{24,16},{1,9},{9,1},{17,25},{25,17},{2,10},{10... | collective-permute-start | bytes 442376 | tf_op jit(solution)/shard_map/encoder_back/ppermute | solution.py:60
  337.1 10.6 %collective-permute-start.65 = (bf16[256,1152]{1,0:T(8,128)(2,1)S(1)}, bf16[256,1152]{1,0:T(8,128)(2,1)S(1)}, u32[]{:S(2)}, u32[]{:S(2)}) collective-permute-start(bf16[256,1152]{1,0:T(8,128)(2,1)S(1)} %convolution_convert_fusion.12), channel_id=1, source_target_pairs={{0,4},{4,0},{1,5},{5,1},{2,6},{6,2},{3,7},{7,3},{8,12},{12,8},{9,1... | collective-permute-start | bytes 1769480 | tf_op jit(solution)/shard_map/encoder_back/ppermute | solution.py:64
  338.6 9.0 %collective-permute-start.56 = (bf16[64,1152]{1,0:T(8,128)(2,1)S(1)}, bf16[64,1152]{1,0:T(8,128)(2,1)S(1)}, u32[]{:S(2)}, u32[]{:S(2)}) collective-permute-start(bf16[64,1152]{1,0:T(8,128)(2,1)S(1)} %get-tuple-element.276), channel_id=1, source_target_pairs={{0,8},{8,0},{16,24},{24,16},{1,9},{9,1},{17,25},{25,17},{2,10},{10... | collective-permute-start | bytes 442376 | tf_op jit(solution)/shard_map/encoder_back/ppermute | solution.py:60
  353.0 14.0 %collective-permute-start.66 = (bf16[64,1152]{1,0:T(8,128)(2,1)S(1)}, bf16[64,1152]{1,0:T(8,128)(2,1)S(1)}, u32[]{:S(2)}, u32[]{:S(2)}) collective-permute-start(bf16[64,1152]{1,0:T(8,128)(2,1)S(1)} %get-tuple-element.177), channel_id=1, source_target_pairs={{0,16},{8,24},{16,0},{24,8},{1,17},{9,25},{17,1},{25,9},{2,18},{10... | collective-permute-start | bytes 442376 | tf_op jit(solution)/shard_map/encoder_back/ppermute | solution.py:60
  354.4 12.6 %collective-permute-start.67 = (bf16[64,1152]{1,0:T(8,128)(2,1)S(1)}, bf16[64,1152]{1,0:T(8,128)(2,1)S(1)}, u32[]{:S(2)}, u32[]{:S(2)}) collective-permute-start(bf16[64,1152]{1,0:T(8,128)(2,1)S(1)} %get-tuple-element.177), channel_id=1, source_target_pairs={{0,8},{8,0},{16,24},{24,16},{1,9},{9,1},{17,25},{25,17},{2,10},{10... | collective-permute-start | bytes 442376 | tf_op jit(solution)/shard_map/encoder_back/ppermute | solution.py:60
  355.9 11.1 %collective-permute-start.68 = (bf16[64,1152]{1,0:T(8,128)(2,1)S(1)}, bf16[64,1152]{1,0:T(8,128)(2,1)S(1)}, u32[]{:S(2)}, u32[]{:S(2)}) collective-permute-start(bf16[64,1152]{1,0:T(8,128)(2,1)S(1)} %get-tuple-element.177), channel_id=1, source_target_pairs={{0,24},{8,16},{16,8},{24,0},{1,25},{9,17},{17,9},{25,1},{2,26},{10... | collective-permute-start | bytes 442376 | tf_op jit(solution)/shard_map/encoder_back/ppermute | solution.py:60
  358.3 8.7 %all-to-all-start = ((f32[8,1,1728]{2,1,0:T(1,128)}), f32[8,1,1728]{2,1,0:T(1,128)S(1)}, u32[]{:S(2)}, u32[]{:S(2)}) async-start(f32[8,1,1728]{2,1,0:T(1,128)} %all_to_all.11), calls=%async_computation.3 | async-start | bytes 114688 | tf_op jit(solution)/shard_map/modulation_back/all_to_all | solution.py:628
  368.4 16.9 %collective-permute-start.73 = (bf16[256,1152]{1,0:T(8,128)(2,1)}, bf16[256,1152]{1,0:T(8,128)(2,1)}, u32[]{:S(2)}, u32[]{:S(2)}) collective-permute-start(bf16[256,1152]{1,0:T(8,128)(2,1)} %convolution_convert_fusion.11), channel_id=1, source_target_pairs={{0,4},{4,0},{1,5},{5,1},{2,6},{6,2},{3,7},{7,3},{8,12},{12,8},{9,1... | collective-permute-start | bytes 1769480 | tf_op jit(solution)/shard_map/outputs/ppermute | solution.py:64
  369.5 18.7 %collective-permute-start.72 = (bf16[144,2304]{1,0:T(8,128)(2,1)}, bf16[144,2304]{1,0:T(8,128)(2,1)S(1)}, u32[]{:S(2)}, u32[]{:S(2)}) collective-permute-start(bf16[144,2304]{1,0:T(8,128)(2,1)} %get-tuple-element.249), channel_id=1, source_target_pairs={{0,16},{16,0},{1,17},{17,1},{2,18},{18,2},{3,19},{19,3},{4,20},{20... | collective-permute-start | bytes 1990664 | tf_op jit(solution)/shard_map/returns/ppermute | solution.py:157
  389.1 20.5 %collective-permute-start.81 = (bf16[144,2304]{1,0:T(8,128)(2,1)}, bf16[144,2304]{1,0:T(8,128)(2,1)S(1)}, u32[]{:S(2)}, u32[]{:S(2)}) collective-permute-start(bf16[144,2304]{1,0:T(8,128)(2,1)} %broadcast_select_fusion.4), channel_id=1, source_target_pairs={{0,4},{4,0},{1,5},{5,1},{2,6},{6,2},{3,7},{7,3},{8,12},{12,8},{9,1... | collective-permute-start | bytes 1990664 | tf_op jit(solution)/shard_map/norm/ppermute | solution.py:64
  390.8 10.2 %collective-permute-start.76 = (bf16[144,1152]{1,0:T(8,128)(2,1)S(1)}, bf16[144,1152]{1,0:T(8,128)(2,1)S(1)}, u32[]{:S(2)}, u32[]{:S(2)}) collective-permute-start(bf16[144,1152]{1,0:T(8,128)(2,1)S(1)} %get-tuple-element.267), channel_id=1, source_target_pairs={{0,16},{16,0},{1,17},{17,1},{2,18},{18,2},{3,19},{19,3},{4,20},{20... | collective-permute-start | bytes 995336 | tf_op jit(solution)/shard_map/norm/ppermute | solution.py:157
  (165 other events, 1245.9 us)
Sparse Core Ops, SparseCore 0:
  31.9 49.6 all-gather.5
  83.8 55.1 all-gather.7
  141.3 55.3 all-gather.9
  212.7 51.3 reduce-scatter.4
  266.9 31.3 reduce-scatter.6
  300.4 51.4 reduce-scatter.8
  354.7 32.2 reduce-scatter.10

commit v6 on v5

--- a/solution.py
+++ b/solution.py
@@ -112,10 +112,9 @@
     return values
 
 
-def send_shares(pack, section, core):
-    half = pack.shape[0] // 2
-    mine = lax.dynamic_slice_in_dim(pack, core * half, half, 0)
-    other = swap_cores(lax.dynamic_slice_in_dim(pack, (1 - core) * half, half, 0))
+def send_shares(rows_of, half, section, core):
+    other = swap_cores(rows_of((1 - core) * half))
+    mine = rows_of(core * half)
     keep = jnp.where(core == section, mine, other)
     give = jnp.where(core == section, other, mine)
     return keep, lax.ppermute(give, "section", [(0, 1), (1, 0)])
@@ -445,11 +444,15 @@
     columns = heads_weight.shape[-1]
 
     with jax.named_scope("weights_in"):
-        attn_pack = jnp.concatenate(
-            [heads_weight[0, 0], heads_weight[0, 1], heads_weight[0, 2], output_weight[0].T], axis=1
-        ).astype(BF)
-        keep, given = send_shares(attn_pack, section, core)
-        attn_width = attn_pack.shape[1]
+        half = shard // 2
+        attn_parts = [heads_weight[0, 0], heads_weight[0, 1], heads_weight[0, 2], output_weight[0].T]
+
+        def attn_rows(start):
+            parts = [lax.dynamic_slice_in_dim(part, start, half, 0) for part in attn_parts]
+            return jnp.concatenate(parts, axis=1).astype(BF)
+
+        keep, given = send_shares(attn_rows, half, section, core)
+        attn_width = keep.shape[1]
         if lax.axis_size("dp") == 4:
             cut = attn_width // 3
             first = keep[:, :cut]
@@ -463,7 +466,11 @@
         enc_attn, dec_attn = by_block(keep_all, rest[:, :attn_width], section)
         feed_pack = jnp.concatenate([up_weight[0], down_weight[0].T], axis=1).astype(BF)
         feed_pack, given = tie(feed_pack, given)
-        enc_feed_half, dec_feed_half = by_block(*send_shares(feed_pack, section, core), section)
+
+        def feed_rows(start):
+            return lax.dynamic_slice_in_dim(feed_pack, start, half, 0)
+
+        enc_feed_half, dec_feed_half = by_block(*send_shares(feed_rows, half, section, core), section)
         feed_width = feed_pack.shape[1] // 2
         enc_feed = gather_weight(enc_feed_half)
 

time: 450 us -> 451 us (level)
    unnamed x221 -> x224, local copies, waits for them, and re-layouts: 13.8 us -> 13.9 us
  transfers between devices with their start and end apart: 90 -> 90, of which waited for: 56 -> 57; matrix products, arithmetic and copies ran while one was open for 16% -> 17% of each run, Pallas kernels for 1% -> 1%
where the time goes in v6:
time: 451 us; the launch traced here: 443 us
  waiting for transfers between devices  190 us (42%)
  starting transfers between devices  92.1 us (20%)
  other arithmetic  53.3 us (12%)
  matrix products  39 us (9%)
  local copies, waits for them, and re-layouts  27.2 us (6%)
  between operations  23 us (5%)
  blocking collectives  9.52 us (2%)
  Pallas kernels  8.83 us (2%)
    ppermute x48, waiting for transfers between devices, swap_chips(): return lax.ppermute(block, CHIPS, chip_route(offset))  86.9 us
    ppermute x48, starting transfers between devices, swap_chips(): return lax.ppermute(block, CHIPS, chip_route(offset))  56.7 us
    dot_general x28, matrix products, dot(): lax.dot_general(left, right, (dims, ((), ())), preferred_element_type=F32)  32.2 us
    all_gather x3, waiting for transfers between devices, gather_weight(): return lax.all_gather(half, ROWS_BY, axis=0, tiled=True)  30.7 us
    reduce_scatter x4, waiting for transfers between devices, sum_planes(): summed = lax.psum_scatter(grad, 'dp', scatter_dimension=0, tiled=True)  19 us
    sub x6, other arithmetic, adam_update(): weight_out = weight_in - LEARN_RATE * (ratio + WEIGHT_DECAY * weight_in)  16.5 us
    ppermute x2, waiting for transfers between devices, send_shares(): return (keep, lax.ppermute(give, 'section', [(0, 1), (1, 0)]))  15.2 us
    unnamed x224, local copies, waits for them, and re-layouts  13.9 us
  transfers between devices with their start and end apart: 90, of which 57 were waited for; matrix products, arithmetic and copies ran while one was open for 17% of the time, Pallas kernels for 1%

profile of v6, /device:TPU:0, one launch (start us, length us, event | category | flops | bytes accessed | tf_op | source)
XLA Modules:
  0.0 442.6 jit_solution(10568403702890305517)
XLA Ops:
  17.6 3.7 collective-permute-start.10
  22.1 3.3 collective-permute-done.10
  36.2 3.0 collective-permute-start.1
  44.7 15.2 %collective-permute-done.19 = bf16[144,2304]{1,0:T(8,128)(2,1)S(1)} collective-permute-done((bf16[144,2304]{1,0:T(8,128)(2,1)S(1)}, bf16[144,2304]{1,0:T(8,128)(2,1)S(1)}, u32[]{:S(2)}, u32[]{:S(2)}) %collective-permute-start.19) | collective-permute-done | bytes 663584 | tf_op jit(solution)/shard_map/weights_in/ppermute | solution.py:120
  64.4 3.0 collective-permute-start.4
  73.1 9.5 %all-gather.1 = f32[8,2,1728]{2,1,0:T(2,128)S(1)} all-gather(f32[1,2,1728]{2,1,0:T(2,128)S(1)} %fusion.156), channel_id=2, replica_groups=mesh['section'=2,'row'=2,'core'=2,'dp'=4] {'section','row','core'}, dimensions={0}, use_global_device_ids=true | all-gather | bytes 124416 | tf_op jit(solution)/shard_map/modulation/all_gather | solution.py:485
  87.1 3.5 broadcast_select_fusion
  97.3 4.1 collective-permute-done.12
  112.1 3.7 collective-permute-done.16
  116.4 23.0 %all-gather.8.cloned.1.call-done = bf16[1152,2304]{1,0:T(8,128)(2,1)} async-done(((bf16[144,2304]{1,0:T(8,128)(2,1)}), bf16[1152,2304]{1,0:T(8,128)(2,1)}) %all-gather.8.cloned.1.call-update) | async-done | bytes 5308432 | tf_op jit(solution)/shard_map/weights_in/all_gather | solution.py:172
  139.4 4.0 multiply_convert_fusion.2
  148.2 4.0 collective-permute-done.20
  158.5 3.0 collective-permute-done.23
  161.4 3.6 collective-permute-done.24
  174.6 3.7 collective-permute-done.26
  189.4 7.6 %all-gather.10.cloned.1.call-done.up_ref.down_ref = bf16[1152,2304]{1,0:T(8,128)(2,1)} async-done(((bf16[144,2304]{1,0:T(8,128)(2,1)}), bf16[1152,2304]{1,0:T(8,128)(2,1)}) %all-gather.10.cloned.1.call-update) | async-done | bytes 5308432 | tf_op jit(solution)/shard_map/encoder/all_gather | solution.py:172
  199.5 5.2 %decoder.1 = (bf16[256,1152]{1,0:T(8,128)(2,1)S(1)}, bf16[256,1152]{1,0:T(8,128)(2,1)S(1)}, bf16[256,1152]{1,0:T(8,128)(2,1)S(1)}) custom-call(bf16[256,1152]{1,0:T(8,128)(2,1)S(1)} %pad_maximum_fusion.9.normed, bf16[1152,2304]{1,0:T(8,128)(2,1)S(1)} %copy-done.2, bf16[1152,2304]{1,0:T(8,128)(2,1)S(1)} %copy-done.2, ...), custom_call_target="tpu_custom_call" | custom-call | flops 2038431744 | bytes 8257536 | tf_op jit(solution)/shard_map/decoder/pallas_call | solution.py:268
  217.6 4.1 collective-permute-done.34.first
  228.2 3.0 collective-permute-done.37
  231.2 3.6 collective-permute-done.38
  251.2 13.2 %reduce-scatter.5.cloned.1.call-done = bf16[1,144,2304]{2,1,0:T(8,128)(2,1)} async-done(((bf16[4,144,2304]{2,1,0:T(8,128)(2,1)}), bf16[1,144,2304]{2,1,0:T(8,128)(2,1)}) %reduce-scatter.5.cloned.1.call-update) | async-done | bytes 663568 | tf_op jit(solution)/shard_map/decoder_back/reduce_scatter | solution.py:187
  271.9 3.6 collective-permute-done.45
  277.0 3.5 fusion.46
  304.4 4.4 collective-permute-done.53
  320.4 4.1 collective-permute-done.59
  331.0 3.2 collective-permute-done.62
  349.3 2.9 reduce-scatter.9.cloned.1.call-done
  358.6 3.9 all-to-all-start
  362.6 4.8 %all-to-all-done = f32[8,1,1728]{2,1,0:T(1,128)S(1)} async-done(((f32[8,1,1728]{2,1,0:T(1,128)}), f32[8,1,1728]{2,1,0:T(1,128)S(1)}, u32[]{:S(2)}, u32[]{:S(2)}) %all-to-all-start) | async-done | bytes 55328 | tf_op jit(solution)/shard_map/modulation_back/all_to_all | solution.py:635
  380.1 3.0 multiply_reduce_fusion
  396.1 3.1 collective-permute-done.75
  416.6 6.6 %multiply_subtract_fusion = (f32[1,288,1728]{2,1,0:T(8,128)}, f32[1,288,1728]{2,1,0:T(8,128)}, f32[1,288,1728]{2,1,0:T(8,128)}) fusion(f32[1,288,1728]{2,1,0:T(8,128)S(1)} %copy-done.16, f32[288,1728]{1,0:T(8,128)} %get-tuple-element.198, f32[]{:T(128)S(6)} %min.3, f32[1,288,1728]{2,1,0:T(8,128)} %param.45, f32[1,288,1728]{2,1,0:T(8,128)} %param.46), kind=kLoop, calls=%fused_computation.50 | loop fusion | flops 7962624 | bytes 13934596 | tf_op jit(solution)/shard_map/update/sub | solution.py:406
  (581 shorter events, 249.4 us)
Async XLA Ops:
  7.2 78.4 %all-gather.6.cloned.1.call-start = ((), (), s32[]{:S(2)}) async-start(), calls=%async_computation.5 | async-start | bytes 4976640 | tf_op jit(solution)/shard_map/weights_in/all_gather | solution.py:172
  14.7 16.6 %collective-permute-start.7 = (bf16[144,1152]{1,0:T(8,128)(2,1)S(1)}, bf16[144,1152]{1,0:T(8,128)(2,1)S(1)}, u32[]{:S(2)}, u32[]{:S(2)}) collective-permute-start(bf16[144,1152]{1,0:T(8,128)(2,1)S(1)} %get-tuple-element.270), channel_id=1, source_target_pairs={{0,16},{16,0},{1,17},{17,1},{2,18},{18,2},{3,19},{19,3},{4,20},{20... | collective-permute-start | bytes 995336 | tf_op jit(solution)/shard_map/weights_in/ppermute | solution.py:120
  21.3 9.3 %collective-permute-start.9 = (bf16[144,384]{1,0:T(8,128)(2,1)S(1)}, bf16[144,384]{1,0:T(8,128)(2,1)S(1)}, u32[]{:S(2)}, u32[]{:S(2)}) collective-permute-start(bf16[144,384]{1,0:T(8,128)(2,1)S(1)} %slice.400), channel_id=1, source_target_pairs={{0,2},{1,3},{2,0},{3,1},{4,6},{5,7},{6,4},{7,5},{8,10},{9,11},{10,... | collective-permute-start | bytes 331784 | tf_op jit(solution)/shard_map/weights_in/ppermute | solution.py:459
  32.2 107.2 %all-gather.8.cloned.1.call-start = ((), (), s32[]{:S(2)}) async-start(), calls=%async_computation.6 | async-start | bytes 5971968 | tf_op jit(solution)/shard_map/weights_in/all_gather | solution.py:172
  36.1 26.2 %collective-permute-start = (s32[2,2]{0,1:T(2,128)S(1)}, s32[2,2]{0,1:T(2,128)S(1)}, u32[]{:S(2)}, u32[]{:S(2)}) collective-permute-start(s32[2,2]{0,1:T(2,128)S(1)} %pad_add_fusion.1), channel_id=1, source_target_pairs={{0,1},{1,0},{2,3},{3,2},{4,5},{5,4},{6,7},{7,6},{8,9},{9,8},{10,11... | collective-permute-start | bytes 56 | tf_op jit(solution)/shard_map/modulation/ppermute | solution.py:90
  36.2 26.1 %collective-permute-start.1 = (s32[2,2]{0,1:T(2,128)S(1)}, s32[2,2]{0,1:T(2,128)S(1)}, u32[]{:S(2)}, u32[]{:S(2)}) collective-permute-start(s32[2,2]{0,1:T(2,128)S(1)} %pad_add_fusion.1), channel_id=1, source_target_pairs={{0,2},{1,3},{2,0},{3,1},{4,6},{5,7},{6,4},{7,5},{8,10},{9,11},{10,... | collective-permute-start | bytes 56 | tf_op jit(solution)/shard_map/modulation/ppermute | solution.py:90
  39.2 23.1 %collective-permute-start.2 = (s32[2,2]{0,1:T(2,128)S(1)}, s32[2,2]{0,1:T(2,128)S(1)}, u32[]{:S(2)}, u32[]{:S(2)}) collective-permute-start(s32[2,2]{0,1:T(2,128)S(1)} %pad_add_fusion.1), channel_id=1, source_target_pairs={{0,3},{1,2},{2,1},{3,0},{4,7},{5,6},{6,5},{7,4},{8,11},{9,10},{10,... | collective-permute-start | bytes 56 | tf_op jit(solution)/shard_map/modulation/ppermute | solution.py:90
  43.4 16.5 %collective-permute-start.19 = (bf16[144,2304]{1,0:T(8,128)(2,1)S(1)}, bf16[144,2304]{1,0:T(8,128)(2,1)S(1)}, u32[]{:S(2)}, u32[]{:S(2)}) collective-permute-start(bf16[144,2304]{1,0:T(8,128)(2,1)S(1)} %broadcast_select_fusion.7), channel_id=1, source_target_pairs={{0,16},{16,0},{1,17},{17,1},{2,18},{18,2},{3,19},{19,3},{4,20},{20... | collective-permute-start | bytes 1990664 | tf_op jit(solution)/shard_map/weights_in/ppermute | solution.py:120
  61.3 135.7 %all-gather.10.cloned.1.call-start = ((), (), s32[]{:S(2)}) async-start(), calls=%async_computation.7 | async-start | bytes 5971968 | tf_op jit(solution)/shard_map/encoder/all_gather | solution.py:172
  95.3 8.7 %collective-permute-start.13 = (bf16[64,1152]{1,0:T(8,128)(2,1)S(1)}, bf16[64,1152]{1,0:T(8,128)(2,1)S(1)}, u32[]{:S(2)}, u32[]{:S(2)}) collective-permute-start(bf16[64,1152]{1,0:T(8,128)(2,1)S(1)} %get-tuple-element.299), channel_id=1, source_target_pairs={{0,8},{8,0},{16,24},{24,16},{1,9},{9,1},{17,25},{25,17},{2,10},{10... | collective-permute-start | bytes 442376 | tf_op jit(solution)/shard_map/encoder/ppermute | solution.py:60
  107.1 8.8 %collective-permute-start.16 = (bf16[64,1152]{1,0:T(8,128)(2,1)S(1)}, bf16[64,1152]{1,0:T(8,128)(2,1)S(1)}, u32[]{:S(2)}, u32[]{:S(2)}) collective-permute-start(bf16[64,1152]{1,0:T(8,128)(2,1)S(1)} %add_convert_fusion.4), channel_id=1, source_target_pairs={{0,8},{8,0},{16,24},{24,16},{1,9},{9,1},{17,25},{25,17},{2,10},{10... | collective-permute-start | bytes 442376 | tf_op jit(solution)/shard_map/encoder/ppermute | solution.py:60
  116.0 148.5 %reduce-scatter.5.cloned.1.call-start = ((), (), s32[]{:S(2)}) async-start(), calls=%async_computation.8 | async-start | bytes 3317760 | tf_op jit(solution)/shard_map/decoder_back/reduce_scatter | solution.py:187
  156.4 8.7 %collective-permute-start.24 = (bf16[64,1152]{1,0:T(8,128)(2,1)S(1)}, bf16[64,1152]{1,0:T(8,128)(2,1)S(1)}, u32[]{:S(2)}, u32[]{:S(2)}) collective-permute-start(bf16[64,1152]{1,0:T(8,128)(2,1)S(1)} %multiply_convert_fusion.5), channel_id=1, source_target_pairs={{0,8},{8,0},{16,24},{24,16},{1,9},{9,1},{17,25},{25,17},{2,10},{10... | collective-permute-start | bytes 442376 | tf_op jit(solution)/shard_map/encoder/ppermute | solution.py:60
  212.9 85.7 %reduce-scatter.7.cloned.1.call-start = ((), (), s32[]{:S(2)}) async-start(), calls=%async_computation.9 | async-start | bytes 1658880 | tf_op jit(solution)/shard_map/decoder_back/reduce_scatter | solution.py:187
  226.1 8.7 %collective-permute-start.38 = (bf16[64,1152]{1,0:T(8,128)(2,1)S(1)}, bf16[64,1152]{1,0:T(8,128)(2,1)S(1)}, u32[]{:S(2)}, u32[]{:S(2)}) collective-permute-start(bf16[64,1152]{1,0:T(8,128)(2,1)S(1)} %get-tuple-element.128), channel_id=1, source_target_pairs={{0,8},{8,0},{16,24},{24,16},{1,9},{9,1},{17,25},{25,17},{2,10},{10... | collective-permute-start | bytes 442376 | tf_op jit(solution)/shard_map/decoder_back/ppermute | solution.py:60
  242.2 8.8 %collective-permute-start.41 = (bf16[64,1152]{1,0:T(8,128)(2,1)S(1)}, bf16[64,1152]{1,0:T(8,128)(2,1)S(1)}, u32[]{:S(2)}, u32[]{:S(2)}) collective-permute-start(bf16[64,1152]{1,0:T(8,128)(2,1)S(1)} %get-tuple-element.284), channel_id=1, source_target_pairs={{0,8},{8,0},{16,24},{24,16},{1,9},{9,1},{17,25},{25,17},{2,10},{10... | collective-permute-start | bytes 442376 | tf_op jit(solution)/shard_map/decoder_back/ppermute | solution.py:60
  251.0 101.2 %reduce-scatter.9.cloned.1.call-start = ((), (), s32[]{:S(2)}) async-start(), calls=%async_computation.10 | async-start | bytes 3317760 | tf_op jit(solution)/shard_map/encoder_back/reduce_scatter | solution.py:187
  286.7 8.6 %collective-permute-start.48 = (bf16[64,1152]{1,0:T(8,128)(2,1)}, bf16[64,1152]{1,0:T(8,128)(2,1)S(1)}, u32[]{:S(2)}, u32[]{:S(2)}) collective-permute-start(bf16[64,1152]{1,0:T(8,128)(2,1)} %get-tuple-element.280), channel_id=1, source_target_pairs={{0,8},{8,0},{16,24},{24,16},{1,9},{9,1},{17,25},{25,17},{2,10},{10... | collective-permute-start | bytes 442376 | tf_op jit(solution)/shard_map/encoder_back/ppermute | solution.py:60
  300.1 88.5 %reduce-scatter.11.cloned.1.call-start = ((), (), s32[]{:S(2)}) async-start(), calls=%async_computation.11 | async-start | bytes 1658880 | tf_op jit(solution)/shard_map/encoder_back/reduce_scatter | solution.py:187
  316.7 24.4 %collective-permute-start.58 = (bf16[4,144,1152]{2,1,0:T(8,128)(2,1)S(1)}, bf16[4,144,1152]{2,1,0:T(8,128)(2,1)S(1)}, u32[]{:S(2)}, u32[]{:S(2)}) collective-permute-start(bf16[4,144,1152]{2,1,0:T(8,128)(2,1)S(1)} %dynamic-slice_bitcast_fusion), channel_id=1, source_target_pairs={{0,4},{4,0},{1,5},{5,1},{2,6},{6,2},{3,7},{7,3},{8,12},{12,8},{9,1... | collective-permute-start | bytes 3981320 | tf_op jit(solution)/shard_map/encoder_back/ppermute | solution.py:64
  318.3 8.9 %collective-permute-start.60 = (bf16[64,1152]{1,0:T(8,128)(2,1)S(1)}, bf16[64,1152]{1,0:T(8,128)(2,1)S(1)}, u32[]{:S(2)}, u32[]{:S(2)}) collective-permute-start(bf16[64,1152]{1,0:T(8,128)(2,1)S(1)} %get-tuple-element.274), channel_id=1, source_target_pairs={{0,8},{8,0},{16,24},{24,16},{1,9},{9,1},{17,25},{25,17},{2,10},{10... | collective-permute-start | bytes 442376 | tf_op jit(solution)/shard_map/encoder_back/ppermute | solution.py:60
  328.2 8.8 %collective-permute-start.63 = (bf16[64,1152]{1,0:T(8,128)(2,1)S(1)}, bf16[64,1152]{1,0:T(8,128)(2,1)S(1)}, u32[]{:S(2)}, u32[]{:S(2)}) collective-permute-start(bf16[64,1152]{1,0:T(8,128)(2,1)S(1)} %get-tuple-element.262), channel_id=1, source_target_pairs={{0,8},{8,0},{16,24},{24,16},{1,9},{9,1},{17,25},{25,17},{2,10},{10... | collective-permute-start | bytes 442376 | tf_op jit(solution)/shard_map/encoder_back/ppermute | solution.py:60
  337.5 10.6 %collective-permute-start.65 = (bf16[256,1152]{1,0:T(8,128)(2,1)S(1)}, bf16[256,1152]{1,0:T(8,128)(2,1)S(1)}, u32[]{:S(2)}, u32[]{:S(2)}) collective-permute-start(bf16[256,1152]{1,0:T(8,128)(2,1)S(1)} %convolution_convert_fusion.12), channel_id=1, source_target_pairs={{0,4},{4,0},{1,5},{5,1},{2,6},{6,2},{3,7},{7,3},{8,12},{12,8},{9,1... | collective-permute-start | bytes 1769480 | tf_op jit(solution)/shard_map/encoder_back/ppermute | solution.py:64
  338.9 9.0 %collective-permute-start.56 = (bf16[64,1152]{1,0:T(8,128)(2,1)S(1)}, bf16[64,1152]{1,0:T(8,128)(2,1)S(1)}, u32[]{:S(2)}, u32[]{:S(2)}) collective-permute-start(bf16[64,1152]{1,0:T(8,128)(2,1)S(1)} %get-tuple-element.276), channel_id=1, source_target_pairs={{0,8},{8,0},{16,24},{24,16},{1,9},{9,1},{17,25},{25,17},{2,10},{10... | collective-permute-start | bytes 442376 | tf_op jit(solution)/shard_map/encoder_back/ppermute | solution.py:60
  353.3 14.1 %collective-permute-start.66 = (bf16[64,1152]{1,0:T(8,128)(2,1)S(1)}, bf16[64,1152]{1,0:T(8,128)(2,1)S(1)}, u32[]{:S(2)}, u32[]{:S(2)}) collective-permute-start(bf16[64,1152]{1,0:T(8,128)(2,1)S(1)} %get-tuple-element.177), channel_id=1, source_target_pairs={{0,16},{8,24},{16,0},{24,8},{1,17},{9,25},{17,1},{25,9},{2,18},{10... | collective-permute-start | bytes 442376 | tf_op jit(solution)/shard_map/encoder_back/ppermute | solution.py:60
  354.8 12.6 %collective-permute-start.67 = (bf16[64,1152]{1,0:T(8,128)(2,1)S(1)}, bf16[64,1152]{1,0:T(8,128)(2,1)S(1)}, u32[]{:S(2)}, u32[]{:S(2)}) collective-permute-start(bf16[64,1152]{1,0:T(8,128)(2,1)S(1)} %get-tuple-element.177), channel_id=1, source_target_pairs={{0,8},{8,0},{16,24},{24,16},{1,9},{9,1},{17,25},{25,17},{2,10},{10... | collective-permute-start | bytes 442376 | tf_op jit(solution)/shard_map/encoder_back/ppermute | solution.py:60
  356.2 11.1 %collective-permute-start.68 = (bf16[64,1152]{1,0:T(8,128)(2,1)S(1)}, bf16[64,1152]{1,0:T(8,128)(2,1)S(1)}, u32[]{:S(2)}, u32[]{:S(2)}) collective-permute-start(bf16[64,1152]{1,0:T(8,128)(2,1)S(1)} %get-tuple-element.177), channel_id=1, source_target_pairs={{0,24},{8,16},{16,8},{24,0},{1,25},{9,17},{17,9},{25,1},{2,26},{10... | collective-permute-start | bytes 442376 | tf_op jit(solution)/shard_map/encoder_back/ppermute | solution.py:60
  358.6 8.7 %all-to-all-start = ((f32[8,1,1728]{2,1,0:T(1,128)}), f32[8,1,1728]{2,1,0:T(1,128)S(1)}, u32[]{:S(2)}, u32[]{:S(2)}) async-start(f32[8,1,1728]{2,1,0:T(1,128)} %all_to_all.11), calls=%async_computation.3 | async-start | bytes 114688 | tf_op jit(solution)/shard_map/modulation_back/all_to_all | solution.py:635
  368.8 16.9 %collective-permute-start.73 = (bf16[256,1152]{1,0:T(8,128)(2,1)}, bf16[256,1152]{1,0:T(8,128)(2,1)}, u32[]{:S(2)}, u32[]{:S(2)}) collective-permute-start(bf16[256,1152]{1,0:T(8,128)(2,1)} %convolution_convert_fusion.11), channel_id=1, source_target_pairs={{0,4},{4,0},{1,5},{5,1},{2,6},{6,2},{3,7},{7,3},{8,12},{12,8},{9,1... | collective-permute-start | bytes 1769480 | tf_op jit(solution)/shard_map/outputs/ppermute | solution.py:64
  369.9 18.7 %collective-permute-start.72 = (bf16[144,2304]{1,0:T(8,128)(2,1)}, bf16[144,2304]{1,0:T(8,128)(2,1)S(1)}, u32[]{:S(2)}, u32[]{:S(2)}) collective-permute-start(bf16[144,2304]{1,0:T(8,128)(2,1)} %get-tuple-element.249), channel_id=1, source_target_pairs={{0,16},{16,0},{1,17},{17,1},{2,18},{18,2},{3,19},{19,3},{4,20},{20... | collective-permute-start | bytes 1990664 | tf_op jit(solution)/shard_map/returns/ppermute | solution.py:156
  389.5 20.5 %collective-permute-start.81 = (bf16[144,2304]{1,0:T(8,128)(2,1)}, bf16[144,2304]{1,0:T(8,128)(2,1)S(1)}, u32[]{:S(2)}, u32[]{:S(2)}) collective-permute-start(bf16[144,2304]{1,0:T(8,128)(2,1)} %broadcast_select_fusion.4), channel_id=1, source_target_pairs={{0,4},{4,0},{1,5},{5,1},{2,6},{6,2},{3,7},{7,3},{8,12},{12,8},{9,1... | collective-permute-start | bytes 1990664 | tf_op jit(solution)/shard_map/norm/ppermute | solution.py:64
  391.1 10.2 %collective-permute-start.76 = (bf16[144,1152]{1,0:T(8,128)(2,1)S(1)}, bf16[144,1152]{1,0:T(8,128)(2,1)S(1)}, u32[]{:S(2)}, u32[]{:S(2)}) collective-permute-start(bf16[144,1152]{1,0:T(8,128)(2,1)S(1)} %get-tuple-element.268), channel_id=1, source_target_pairs={{0,16},{16,0},{1,17},{17,1},{2,18},{18,2},{3,19},{19,3},{4,20},{20... | collective-permute-start | bytes 995336 | tf_op jit(solution)/shard_map/norm/ppermute | solution.py:156
  (166 other events, 1248.9 us)
Sparse Core Ops, SparseCore 0:
  32.3 49.6 all-gather.5
  84.2 55.1 all-gather.7
  141.6 55.3 all-gather.9
  213.0 51.3 reduce-scatter.4
  267.2 31.3 reduce-scatter.6
  300.7 51.4 reduce-scatter.8
  355.1 32.2 reduce-scatter.10
